TPU v7x, 32 devices: a whole 2x2x4 slice. The times are simulated.
32 devices in a mesh: groups: 2 (over y), rows: 16 (over z, x, core), heads: 1.
Axes of the slice: x: 2, y: 2, z: 4, core: 2. Of those that a mesh axis runs over, the one named last changes fastest.
Arguments:
- query_in: bfloat16 [640, 1024], P(('groups', 'rows'), 'heads'), parts along dimension 0, may hold values from -6 to 6
- key_in: bfloat16 [640, 1024], P(('groups', 'rows'), 'heads'), parts along dimension 0, may hold values from -6 to 6
- value_in: bfloat16 [640, 2048], P(('groups', 'rows'), 'heads'), parts along dimension 0, may hold values from -6 to 6
- gate_in: bfloat16 [640, 2048], P(('groups', 'rows'), 'heads'), parts along dimension 0, may hold values from -6 to 6
- decay_in: float32 [640, 16], P(('groups', 'rows'), 'heads'), parts along dimension 0, may hold values from -6 to 6
- beta_in: float32 [640, 16], P(('groups', 'rows'), 'heads'), parts along dimension 0, may hold values from -6 to 6
- decay_rate: float32 [16], P('heads'), may hold values from 0.02 to 4
- decay_bias: float32 [16], P('heads'), may hold values from -1 to 1
- norm_gain: float32 [128], replicated, may hold values from 0.5 to 1.5
- prior_state: bfloat16 [160, 16, 128, 128], P(('groups', 'rows'), 'heads'), parts along dimension 0, may hold values from -4 to 4
- accepted: int32 [160], P(('groups', 'rows')), parts along dimension 0, may hold values from 1 to 4
- out_weight: bfloat16 [2048, 2048], P('heads', 'rows'), may hold values from -0.125 to 0.125
- residual: bfloat16 [640, 2048], P(('groups', 'rows'), 'heads'), parts along dimension 0, may hold values from -12 to 12
- post_gain: float32 [2048], P('heads'), may hold values from 0.5 to 1.5
- expert_ids: int32 [640, 10], P(('groups', 'rows')), parts along dimension 0, may hold values from 0 to 31, all different within a row; in each aligned block of 20 rows (0 to 19, 20 to 39, ...) at most 8 rows name the same one
- expert_scores: float32 [640, 10], P(('groups', 'rows')), parts along dimension 0, may hold values from 0.1 to 1
- expert_up: bfloat16 [32, 2048, 512], P('rows', 'heads'), may hold values from -0.125 to 0.125
- expert_down: bfloat16 [32, 256, 2048], P('rows', None, 'heads'), may hold values from -0.375 to 0.375
Outputs:
- layer_out: bfloat16 [640, 2048], P(('groups', 'rows'), 'heads'), parts along dimension 0
- kept_state: bfloat16 [160, 16, 128, 128], P(('groups', 'rows'), 'heads'), parts along dimension 0
There are 2 independent parts, one for each index of `groups`. A program takes and returns all parts, laid end to end along the dimension named above; an argument that names none is the same for every part. Nothing has to cross between parts.
Inputs may be any that keep to these rules, and one draw needn't show every extreme that they name: `expert_ids`: every row names 10 different experts. In each aligned block of 20 rows no expert is named more than 8 times, a bound that some block reaches.
All inputs are finite; a program needn't handle non-finite values.
Results may differ from a plain program's by a relative error of at most 0.0034.
Values may be sent and summed in bfloat16 or wider, within the bound.
No kernel may reach another device: no remote copies, remote signals or barrier semaphores. Data moves between devices by JAX's collectives and lax.ppermute only.
A program may use at most 64 MiB of HBM per device.

v0:
```python
import jax
import jax.numpy as jnp
from jax import lax
from jax.sharding import PartitionSpec as P

EPS = 1e-06
HIGH = lax.Precision.HIGHEST


def unit_rows(values_in, width):
    shaped = values_in.reshape(values_in.shape[0], -1, width)
    return shaped * lax.rsqrt(jnp.sum(shaped * shaped, axis=-1, keepdims=True) + EPS)


def delta_rule(
    query_in,
    key_in,
    value_in,
    gate_in,
    decay_in,
    beta_in,
    decay_rate,
    decay_bias,
    norm_gain,
    prior_state,
    accepted,
):
    tok_rows = query_in.shape[0]
    req_rows, heads_here, key_width, value_width = prior_state.shape
    drafts = tok_rows // req_rows
    repeat_by = heads_here // (query_in.shape[1] // key_width)
    queries = jnp.repeat(
        unit_rows(query_in.astype(jnp.float32), key_width), repeat_by, axis=1
    ) * key_width ** (-0.5)
    keys_all = jnp.repeat(unit_rows(key_in.astype(jnp.float32), key_width), repeat_by, axis=1)
    values_all = value_in.astype(jnp.float32).reshape(tok_rows, heads_here, value_width)
    queries = queries.reshape(req_rows, drafts, heads_here, key_width)
    keys_all = keys_all.reshape(req_rows, drafts, heads_here, key_width)
    values_all = values_all.reshape(req_rows, drafts, heads_here, value_width)
    log_decay = -decay_rate * jax.nn.softplus(decay_in + decay_bias)
    log_decay = log_decay.reshape(req_rows, drafts, heads_here)
    beta_rate = jax.nn.sigmoid(beta_in).reshape(req_rows, drafts, heads_here)
    carried = prior_state.astype(jnp.float32)
    held = carried
    readouts = []
    for draft_step in range(drafts):
        carried = carried * jnp.exp(log_decay[:, draft_step])[:, :, None, None]
        memory = jnp.einsum("rhk,rhkv->rhv", keys_all[:, draft_step], carried, precision=HIGH)
        delta_term = (values_all[:, draft_step] - memory) * beta_rate[:, draft_step][:, :, None]
        carried = carried + keys_all[:, draft_step][..., None] * delta_term[:, :, None, :]
        readouts.append(
            jnp.einsum("rhk,rhkv->rhv", queries[:, draft_step], carried, precision=HIGH)
        )
        held = jnp.where((accepted == draft_step + 1)[:, None, None, None], carried, held)
    readout = jnp.stack(readouts, axis=1).reshape(tok_rows, heads_here, value_width)
    inv_norm = lax.rsqrt(jnp.mean(readout * readout, axis=-1, keepdims=True) + EPS)
    gating = jax.nn.silu(gate_in.astype(jnp.float32).reshape(tok_rows, heads_here, value_width))
    mixed_heads = (readout * inv_norm * norm_gain * gating).astype(jnp.bfloat16)
    return (mixed_heads.reshape(tok_rows, heads_here * value_width), held.astype(jnp.bfloat16))


def per_device(
    query_in,
    key_in,
    value_in,
    gate_in,
    decay_in,
    beta_in,
    decay_rate,
    decay_bias,
    norm_gain,
    prior_state,
    accepted,
    out_weight,
    residual,
    post_gain,
    expert_ids,
    expert_scores,
    expert_up,
    expert_down,
):
    mixed_heads, kept_state = delta_rule(
        query_in,
        key_in,
        value_in,
        gate_in,
        decay_in,
        beta_in,
        decay_rate,
        decay_bias,
        norm_gain,
        prior_state,
        accepted,
    )
    partial_value = jnp.dot(
        mixed_heads,
        lax.all_gather(out_weight, "rows", axis=1, tiled=True),
        preferred_element_type=jnp.float32,
    )
    attention = lax.psum_scatter(partial_value, "heads", scatter_dimension=1, tiled=True)
    hidden_sum = residual.astype(jnp.float32) + attention
    full_width = residual.shape[1] * lax.axis_size("heads")
    square = lax.psum(jnp.sum(hidden_sum * hidden_sum, axis=1), "heads")
    inv_rms = lax.rsqrt(square / full_width + EPS)
    normed = (hidden_sum * inv_rms[:, None] * post_gain).astype(jnp.bfloat16)
    tok_rows, top_count = expert_ids.shape
    row_count = lax.axis_size("rows")
    exp_dev = expert_up.shape[0]
    experts_all = exp_dev * row_count
    capacity = max(2, (tok_rows * top_count + experts_all - 1) // experts_all + 1)
    half_width = normed.shape[1]
    flat_ids = expert_ids.reshape(-1)
    onehot = (flat_ids[:, None] == jnp.arange(experts_all, dtype=jnp.int32)[None, :]).astype(
        jnp.int32
    )
    earlier = jnp.cumsum(onehot, axis=0) - onehot
    slot_index = jnp.sum(earlier * onehot, axis=1)
    position = (flat_ids % exp_dev * row_count + flat_ids // exp_dev) * capacity + slot_index
    select = (
        jnp.arange(experts_all * capacity, dtype=jnp.int32)[:, None] == position[None, :]
    ).astype(jnp.bfloat16)
    spread = jnp.repeat(normed, top_count, axis=0)
    outgoing = jnp.dot(select, spread, preferred_element_type=jnp.float32).astype(jnp.bfloat16)
    outgoing = outgoing.reshape(exp_dev, row_count, capacity, half_width)
    arrived = lax.all_to_all(outgoing, "rows", split_axis=1, concat_axis=1, tiled=True)
    rows_in = arrived.reshape(exp_dev, row_count * capacity, half_width)
    partial_up = jnp.einsum("lnd,ldf->lnf", rows_in, expert_up, preferred_element_type=jnp.float32)
    full_up = lax.psum(partial_up, "heads")
    inner_width = expert_down.shape[1]
    activation = (jax.nn.silu(full_up[..., :inner_width]) * full_up[..., inner_width:]).astype(
        jnp.bfloat16
    )
    result = jnp.einsum(
        "lnf,lfd->lnd", activation, expert_down, preferred_element_type=jnp.float32
    ).astype(jnp.bfloat16)
    returned = lax.all_to_all(
        result.reshape(exp_dev, row_count, capacity, half_width),
        "rows",
        split_axis=1,
        concat_axis=1,
        tiled=True,
    )
    values_back = jnp.dot(
        select.T, returned.reshape(-1, half_width), preferred_element_type=jnp.float32
    )
    values_back = values_back.reshape(tok_rows, top_count, half_width)
    weights = expert_scores / jnp.sum(expert_scores, axis=1, keepdims=True)
    layer_out = (hidden_sum + jnp.sum(weights[:, :, None] * values_back, axis=1)).astype(
        jnp.bfloat16
    )
    return (layer_out, kept_state)


def solution(mesh):
    return jax.shard_map(
        per_device,
        mesh=mesh,
        in_specs=(
            P(("groups", "rows"), "heads"),
            P(("groups", "rows"), "heads"),
            P(("groups", "rows"), "heads"),
            P(("groups", "rows"), "heads"),
            P(("groups", "rows"), "heads"),
            P(("groups", "rows"), "heads"),
            P("heads"),
            P("heads"),
            P(),
            P(("groups", "rows"), "heads", None, None),
            P(("groups", "rows")),
            P("heads", "rows"),
            P(("groups", "rows"), "heads"),
            P("heads"),
            P(("groups", "rows"), None),
            P(("groups", "rows"), None),
            P("rows", "heads", None),
            P("rows", None, "heads"),
        ),
        out_specs=(P(("groups", "rows"), "heads"), P(("groups", "rows"), "heads", None, None)),
        check_vma=False,
    )
```

profile of v0, /device:TPU:0, one launch (start us, length us, event | category | flops | bytes accessed | tf_op | source)
XLA Modules:
  0.0 166.7 jit_solution(11844828361934438481)
XLA Ops:
  7.2 0.0 copy-start
  7.2 0.0 all-gather.2.cloned.1.call-start
  7.2 0.7 all-gather.2.cloned.1.call-update
  7.9 0.8 reshape.240
  8.7 0.8 reshape.242
  9.6 0.7 neg.19
  10.2 0.8 fusion.72
  11.0 0.1 copy.34
  11.1 0.9 reshape_reshape.12
  12.1 0.7 add_divide_fusion
  12.8 0.1 copy.36
  12.9 0.1 multiply_reduce_fusion.3
  13.0 0.1 multiply_reduce_fusion.2
  13.2 0.1 slice_multiply_fusion.1
  13.3 0.1 broadcast_in_dim.30
  13.5 0.0 copy-start.2
  13.5 6.3 %fusion.1 = f32[5,16,1,128]{3,2,1,0:T(1,128)S(1)} fusion(f32[5,16,128,1]{2,3,1,0:T(1,128)S(1)} %bitcast.193, bf16[5,16,128,128]{3,2,1,0:T(8,128)(2,1)} %param.27, f32[5,16]{1,0:T(8,128)S(1)} %get-tuple-element.33), kind=kOutput, calls=%fused_computation.3 | convolution fusion | flops 18350080 | bytes 2703680 | tf_op jit(solution)/shard_map/rhk,rhkv->rhv/dot_general | solution.py:48
  19.8 0.1 fusion.69
  19.8 7.0 %fusion.9 = f32[5,16,1,128]{3,2,1,0:T(1,128)S(1)} fusion(f32[5,16,128,1]{2,3,1,0:T(1,128)S(1)} %bitcast.190, bf16[5,16,128,128]{3,2,1,0:T(8,128)(2,1)} %param.27, f32[5,16]{1,0:T(8,128)S(1)} %get-tuple-element.32, f32[5,16,128]{2,1,0:T(8,128)S(1)} %fusion.69, f32[5,16,128]{2,1,0:T(8,128)S(1)} %get-tuple-element.9, f32[5,16]{1,0:T(8,128)S(1)} %get-tuple-element.33), kind=kOutput, calls=%fused_computation.13 | convolution fusion | flops 22282240 | bytes 2785920 | tf_op jit(solution)/shard_map/rhk,rhkv->rhv/dot_general | solution.py:48
  26.9 0.1 fusion.67
  27.0 8.1 %fusion.16 = f32[5,16,1,128]{3,2,1,0:T(1,128)S(1)} fusion(f32[5,16,128,1]{2,3,1,0:T(1,128)S(1)} %bitcast.189, bf16[5,16,128,128]{3,2,1,0:T(8,128)(2,1)S(1)} %copy-done.2, f32[5,16]{1,0:T(8,128)S(1)} %get-tuple-element.31, f32[5,16,128]{2,1,0:T(8,128)S(1)} %fusion.67, f32[5,16,128]{2,1,0:T(8,128)S(1)} %get-tuple-element.10, ...), kind=kOutput, calls=%fused_computation.19 | convolution fusion | flops 26214400 | bytes 2868160 | tf_op jit(solution)/shard_map/rhk,rhkv->rhv/dot_general | solution.py:48
  35.0 0.1 fusion.65
  35.1 9.6 %fusion.13 = f32[5,16,1,128]{3,2,1,0:T(1,128)S(1)} fusion(f32[5,16,128,1]{2,3,1,0:T(1,128)S(1)} %bitcast.188, f32[5,16]{1,0:T(8,128)S(1)} %get-tuple-element.30, bf16[5,16,128,128]{3,2,1,0:T(8,128)(2,1)S(1)} %copy-done.2, f32[5,16,128]{2,1,0:T(8,128)S(1)} %fusion.65, f32[5,16,128]{2,1,0:T(8,128)S(1)} %get-tuple-element.11, ...), kind=kOutput, calls=%fused_computation.16 | convolution fusion | flops 30146560 | bytes 2950400 | tf_op jit(solution)/shard_map/rhk,rhkv->rhv/dot_general | solution.py:48
  44.7 0.1 fusion.63
  44.8 0.1 multiply_multiply_fusion
  44.9 0.1 broadcast_in_dim.29
  45.0 5.0 %fusion.7 = f32[5,16,1,128]{3,2,1,0:T(1,128)S(1)} fusion(f32[5,16,128,1]{2,3,1,0:T(1,128)S(1)} %bitcast.183, bf16[5,16,128,128]{3,2,1,0:T(8,128)(2,1)S(1)} %copy-done.2, f32[5,16,128]{2,1,0:T(8,128)S(1)} %fusion.69, f32[5,16,128]{2,1,0:T(8,128)S(1)} %get-tuple-element.9, f32[5,16]{1,0:T(8,128)S(1)} %get-tuple-element.33), kind=kOutput, calls=%fused_computation.12 | convolution fusion | flops 20971520 | bytes 2785600 | tf_op jit(solution)/shard_map/rhk,rhkv->rhv/dot_general | solution.py:52
  50.0 7.8 %fusion.12 = f32[5,16,1,128]{3,2,1,0:T(1,128)S(1)} fusion(f32[5,16,128,1]{2,3,1,0:T(1,128)S(1)} %bitcast.182, bf16[5,16,128,128]{3,2,1,0:T(8,128)(2,1)S(1)} %copy-done.2, f32[5,16,128]{2,1,0:T(8,128)S(1)} %fusion.67, f32[5,16,128]{2,1,0:T(8,128)S(1)} %get-tuple-element.10, f32[5,16]{1,0:T(8,128)S(1)} %get-tuple-element.32, f32[5,16,128]{2,1,0:T(8,128)S(1)} %fusion.69, ...), kind=kOutput, calls=%fused_computation.15 | convolution fusion | flops 24903680 | bytes 2867840 | tf_op jit(solution)/shard_map/rhk,rhkv->rhv/dot_general | solution.py:52
  57.8 9.6 %fusion.44 = f32[5,16,1,128]{3,2,1,0:T(1,128)S(1)} fusion(f32[5,16,128,1]{2,3,1,0:T(1,128)S(1)} %bitcast.181, bf16[5,16,128,128]{3,2,1,0:T(8,128)(2,1)S(1)} %copy-done.2, f32[5,16,128]{2,1,0:T(8,128)S(1)} %fusion.65, f32[5,16,128]{2,1,0:T(8,128)S(1)} %get-tuple-element.11, f32[5,16]{1,0:T(8,128)S(1)} %get-tuple-element.31, f32[5,16,128]{2,1,0:T(8,128)S(1)} %fusion.67, ...), kind=kOutput, calls=%fused_computation.50 | convolution fusion | flops 28835840 | bytes 2950080 | tf_op jit(solution)/shard_map/rhk,rhkv->rhv/dot_general | solution.py:52
  67.4 0.0 copy-start.14
  67.4 0.0 copy-start.15
  67.4 0.0 copy-start.5
  67.4 13.2 %fusion.15 = f32[5,16,1,128]{3,2,1,0:T(1,128)S(1)} fusion(f32[5,16,128,1]{2,3,1,0:T(1,128)S(1)} %bitcast.180, f32[5,16,128]{2,1,0:T(8,128)S(1)} %fusion.63, f32[5,16,128]{2,1,0:T(8,128)S(1)} %get-tuple-element.8, f32[5,16]{1,0:T(8,128)S(1)} %get-tuple-element.30, bf16[5,16,128,128]{3,2,1,0:T(8,128)(2,1)S(1)} %copy-done.2, f32[5,16,128]{2,1,0:T(8,128)S(1)} %fusion.65, ...), kind=kOutput, calls=%fused_computation.18 | convolution fusion | flops 32768000 | bytes 3032320 | tf_op jit(solution)/shard_map/rhk,rhkv->rhv/dot_general | solution.py:52
  80.6 0.1 multiply_reduce_fusion.1
  80.8 0.1 copy.81
  80.9 0.1 mul.315
  81.0 0.1 copy.82
  81.1 0.1 copy.40
  81.2 0.1 reshape.232
  81.3 0.6 reduce-window.6
  81.9 0.2 slice_reduce_fusion
  82.1 0.1 bitcast_bitcast_fusion
  82.3 8.7 %all-gather.2.cloned.1.call-done = bf16[2048,2048]{1,0:T(8,128)(2,1)} async-done(((bf16[2048,128]{1,0:T(8,128)(2,1)}), bf16[2048,2048]{1,0:T(8,128)(2,1)}) %all-gather.2.cloned.1.call-update) | async-done | bytes 8388624 | tf_op jit(solution)/shard_map/all_gather | solution.py:97
  91.0 4.7 %multiply_reduce_fusion = (f32[20]{0:T(128)S(1)}, f32[20,2048]{1,0:T(8,128)S(1)}) fusion(bf16[2048,2048]{1,0:T(8,128)(2,1)} %all-gather.2.cloned.1.call-done, bf16[20,2048]{1,0:T(8,128)(2,1)S(1)} %copy-done.5, f32[20,2048]{1,0:T(8,128)S(1)} %bitcast.160, f32[20,2048]{1,0:T(8,128)S(1)} %bitcast.161, f32[2048]{0:T(1024)S(1)} %broadcast_bitcast_fusion, ...), kind=kOutput, calls=%fused_computation.68 | convolution fusion | flops 168304624 | bytes 9052240 | tf_op jit(solution)/shard_map/dot_general | solution.py:95
  95.8 0.7 copy-done.3
  96.4 0.1 multiply_convert_fusion
  96.5 0.1 broadcast_in_dim.31
  96.7 1.2 reshape.235
  97.8 1.7 %convolution_convert_fusion.1 = bf16[256,2048]{1,0:T(8,128)(2,1)S(1)} fusion(bf16[200,2048]{1,0:T(8,128)(2,1)} %reshape.235, s32[200]{0:T(256)S(1)} %multiply_add_fusion.8), kind=kOutput, calls=%fused_computation.47 | convolution fusion | flops 210290688 | bytes 1868576 | tf_op jit(solution)/shard_map/dot_general | solution.py:123
  99.6 0.1 copy.43
  99.7 27.8 %all_to_all.10 = bf16[2,16,8,2048]{3,2,0,1:T(8,128)(2,1)S(1)} all-to-all(bf16[2,16,8,2048]{3,2,0,1:T(8,128)(2,1)S(1)} %copy.43), channel_id=1, replica_groups=mesh['groups'=2,'rows'=16,'heads'=1] {'rows'}, dimensions={1} | all-to-all | bytes 2097152 | tf_op jit(solution)/shard_map/all_to_all | solution.py:125
  127.5 0.7 fusion.46
  128.2 0.0 copy-start.12
  128.2 0.5 fusion.43
  128.7 1.1 copy.45
  129.8 5.0 %all-to-all-start.1 = ((bf16[2,16,8,2048]{3,2,0,1:T(8,128)(2,1)}), bf16[2,16,8,2048]{3,2,0,1:T(8,128)(2,1)S(1)}, u32[]{:S(2)}, u32[]{:S(2)}) async-start(bf16[2,16,8,2048]{3,2,0,1:T(8,128)(2,1)} %copy.45), calls=%async_computation.1 | async-start | bytes 2097152 | tf_op jit(solution)/shard_map/all_to_all | solution.py:136
  134.8 0.1 iota_compare_fusion.2
  134.9 0.7 eq.71
  135.6 0.7 broadcast_compare_fusion.3
  136.3 10.4 %fusion.5 = bf16[5,16,128,128]{3,2,1,0:T(8,128)(2,1)} fusion(bf16[5,16,128,128]{3,2,1,0:T(8,128)(2,1)} %param.27, f32[5,16,128]{2,1,0:T(8,128)} %copy-done.6, f32[5,16,128]{2,1,0:T(8,128)} %copy-done.7, f32[5,16]{1,0:T(8,128)S(1)} %get-tuple-element.30, f32[5,16,128]{2,1,0:T(8,128)S(1)} %fusion.67, f32[5,16,128]{2,1,0:T(8,128)} %copy-done.9, ...), kind=kLoop, calls=%fused_computation.7 | loop fusion | flops 23592960 | bytes 5571860 | tf_op jit(solution)/shard_map/convert_element_type | solution.py:59
  146.7 11.0 %all-to-all-done.1 = bf16[2,16,8,2048]{3,2,0,1:T(8,128)(2,1)S(1)} async-done(((bf16[2,16,8,2048]{3,2,0,1:T(8,128)(2,1)}), bf16[2,16,8,2048]{3,2,0,1:T(8,128)(2,1)S(1)}, u32[]{:S(2)}, u32[]{:S(2)}) %all-to-all-start.1) | async-done | bytes 1048608 | tf_op jit(solution)/shard_map/all_to_all | solution.py:136
  157.7 0.1 copy.46
  157.8 1.3 fusion.45
  159.2 0.7 add_convert_fusion
  (55 shorter events, 0.5 us)
Async XLA Ops:
  7.2 121.0 %copy-start = (bf16[2,256,2048]{2,1,0:T(8,128)(2,1)S(1)}, bf16[2,256,2048]{2,1,0:T(8,128)(2,1)}, u32[]{:S(2)}) copy-start(bf16[2,256,2048]{2,1,0:T(8,128)(2,1)} %param.35) | copy-start | bytes 6291460
  7.2 83.8 %all-gather.2.cloned.1.call-start = ((), (), s32[]{:S(2)}) async-start(), calls=%async_computation.2 | async-start | bytes 8912896 | tf_op jit(solution)/shard_map/all_gather | solution.py:97
  13.4 53.9 %copy-start.7 = (f32[5,16,128]{2,1,0:T(8,128)}, f32[5,16,128]{2,1,0:T(8,128)S(1)}, u32[]{:S(2)}) copy-start(f32[5,16,128]{2,1,0:T(8,128)S(1)} %get-tuple-element.8) | copy-start | bytes 122884
  13.4 53.9 %copy-start.8 = (f32[5,16,128]{2,1,0:T(8,128)}, f32[5,16,128]{2,1,0:T(8,128)S(1)}, u32[]{:S(2)}) copy-start(f32[5,16,128]{2,1,0:T(8,128)S(1)} %get-tuple-element.9) | copy-start | bytes 122884
  13.4 53.9 %copy-start.9 = (f32[5,16,128]{2,1,0:T(8,128)}, f32[5,16,128]{2,1,0:T(8,128)S(1)}, u32[]{:S(2)}) copy-start(f32[5,16,128]{2,1,0:T(8,128)S(1)} %get-tuple-element.10) | copy-start | bytes 122884
  13.5 53.9 %copy-start.10 = (f32[5,16,128]{2,1,0:T(8,128)}, f32[5,16,128]{2,1,0:T(8,128)S(1)}, u32[]{:S(2)}) copy-start(f32[5,16,128]{2,1,0:T(8,128)S(1)} %get-tuple-element.11) | copy-start | bytes 122884
  13.5 13.5 %copy-start.2 = (bf16[5,16,128,128]{3,2,1,0:T(8,128)(2,1)S(1)}, bf16[5,16,128,128]{3,2,1,0:T(8,128)(2,1)}, u32[]{:S(2)}) copy-start(bf16[5,16,128,128]{3,2,1,0:T(8,128)(2,1)} %param.27) | copy-start | bytes 7864324
  44.8 22.6 %copy-start.6 = (f32[5,16,128]{2,1,0:T(8,128)}, f32[5,16,128]{2,1,0:T(8,128)S(1)}, u32[]{:S(2)}) copy-start(f32[5,16,128]{2,1,0:T(8,128)S(1)} %fusion.63) | copy-start | bytes 122884
  67.4 13.7 %copy-start.14 = (s32[20,10]{0,1:T(8,128)S(1)}, s32[20,10]{0,1:T(8,128)}, u32[]{:S(2)}) copy-start(s32[20,10]{0,1:T(8,128)} %param.32) | copy-start | bytes 2404
  67.4 14.9 %copy-start.15 = (f32[128]{0:T(128)S(1)}, f32[128]{0:T(128)}, u32[]{:S(2)}) copy-start(f32[128]{0:T(128)} %param.26) | copy-start | bytes 1540
  67.4 23.6 %copy-start.5 = (bf16[20,2048]{1,0:T(8,128)(2,1)S(1)}, bf16[20,2048]{1,0:T(8,128)(2,1)}, u32[]{:S(2)}) copy-start(bf16[20,2048]{1,0:T(8,128)(2,1)} %param.21) | copy-start | bytes 245764
  67.4 23.6 %copy-start.11 = (bf16[20,2048]{1,0:T(8,128)(2,1)S(1)}, bf16[20,2048]{1,0:T(8,128)(2,1)}, u32[]{:S(2)}) copy-start(bf16[20,2048]{1,0:T(8,128)(2,1)} %param.30) | copy-start | bytes 245764
  91.0 5.4 %copy-start.13 = (f32[2048]{0:T(1024)S(1)}, f32[2048]{0:T(1024)}, u32[]{:S(2)}) copy-start(f32[2048]{0:T(1024)} %param.31) | copy-start | bytes 24580
  95.7 0.7 copy-start.3
  97.8 29.6 %copy-start.1 = (bf16[2,2048,512]{2,1,0:T(8,128)(2,1)S(1)}, bf16[2,2048,512]{2,1,0:T(8,128)(2,1)}, u32[]{:S(2)}) copy-start(bf16[2,2048,512]{2,1,0:T(8,128)(2,1)} %param.34) | copy-start | bytes 12582916
  128.2 6.6 %copy-start.12 = (f32[20,10]{0,1:T(8,128)S(1)}, f32[20,10]{0,1:T(8,128)}, u32[]{:S(2)}) copy-start(f32[20,10]{0,1:T(8,128)} %param.33) | copy-start | bytes 2404
  129.8 27.9 %all-to-all-start.1 = ((bf16[2,16,8,2048]{3,2,0,1:T(8,128)(2,1)}), bf16[2,16,8,2048]{3,2,0,1:T(8,128)(2,1)S(1)}, u32[]{:S(2)}, u32[]{:S(2)}) async-start(bf16[2,16,8,2048]{3,2,0,1:T(8,128)(2,1)} %copy.45), calls=%async_computation.1 | async-start | bytes 2097152 | tf_op jit(solution)/shard_map/all_to_all | solution.py:136
  134.8 24.4 %copy-start.4 = (f32[20,2048]{1,0:T(8,128)S(1)}, f32[20,2048]{1,0:T(8,128)}, u32[]{:S(2)}) copy-start(f32[20,2048]{1,0:T(8,128)} %copy-done.3) | copy-start | bytes 491524
Sparse Core Ops, SparseCore 0:
  10.2 80.7 all-gather.1
where the time goes:
time: 169 us; the launch traced here: 167 us
  matrix products  75.5 us (45%)
  blocking collectives  27.8 us (16%)
  waiting for transfers between devices  20.4 us (12%)
  other arithmetic  18.2 us (11%)
  between operations  14.6 us (9%)
  local copies, waits for them, and re-layouts  5.17 us (3%)
  starting transfers between devices  5.02 us (3%)
    dot_general x4, matrix products, delta_rule(): jnp.einsum('rhk,rhkv->rhv', queries[:, draft_step], carried, precision=HIGH)  35.5 us
    dot_general x4, matrix products, delta_rule(): jnp.einsum('rhk,rhkv->rhv', keys_all[:, draft_step], carried, precision=H...  31 us
    all_to_all x1, blocking collectives, per_device(): lax.all_to_all(outgoing, 'rows', split_axis=1, concat_axis=1, tiled=True)  27.8 us
    all_to_all x1, waiting for transfers between devices, per_device(): lax.all_to_all(result.reshape(exp_dev, row_count, capacity, half_width),...  11 us
    convert_element_type x1, other arithmetic, delta_rule(): held.astype(jnp.bfloat16)  10.4 us
    all_gather x1, waiting for transfers between devices, per_device(): lax.all_gather(out_weight, 'rows', axis=1, tiled=True)  8.74 us
    all_to_all x1, starting transfers between devices, per_device(): lax.all_to_all(result.reshape(exp_dev, row_count, capacity, half_width),...  4.98 us
    dot_general x1, matrix products, per_device(): jnp.dot(mixed_heads, lax.all_gather(out_weight, 'rows', axis=1, tiled=Tru...  4.71 us
  transfers between devices with their start and end apart: 2, of which 2 were waited for; matrix products, arithmetic and copies ran while one was open for 51% of the time, Pallas kernels for 0%

commit v1 on v0

v1 whole, which is shorter than its diff:
```python
import functools

import jax
import jax.numpy as jnp
from jax import lax
from jax.experimental import pallas as pl
from jax.experimental.pallas import tpu as pltpu
from jax.sharding import PartitionSpec as P

EPS = 1e-06
BF16 = jnp.bfloat16
F32 = jnp.float32


def round_up(value, step):
    return -(-value // step) * step


def delta_kernel(
    drafts,
    group,
    accepted_ref,
    query_ref,
    key_ref,
    value_ref,
    gate_ref,
    decay_ref,
    beta_ref,
    rate_ref,
    bias_ref,
    gain_ref,
    state_ref,
    mixed_ref,
    kept_ref,
    coef,
    unit,
    vals,
):
    step = pl.program_id(0)
    tok = query_ref.shape[0]
    pad = coef.shape[1]
    reqs, _, width, vwidth = state_ref.shape
    repeat = state_ref.shape[1] // group

    def shift(values, by):
        return pltpu.roll(values, by % pad, 0) if by % pad else values

    @pl.when(step == 0)
    def _():
        heads = decay_ref.shape[1]
        coef[...] = jnp.zeros_like(coef)
        unit[...] = jnp.zeros_like(unit)
        vals[...] = jnp.zeros_like(vals)
        at = lax.broadcasted_iota(jnp.int32, (pad, heads), 0)
        draft = at % drafts
        left = jnp.zeros_like(at)
        for r in range(reqs):
            left = jnp.where(at // drafts == r, accepted_ref[r], left)
        left = left - 1 - draft
        coef[0, 0:tok, :] = -rate_ref[...] * jax.nn.softplus(decay_ref[...] + bias_ref[...])
        coef[1, 0:tok, :] = jax.nn.sigmoid(beta_ref[...])
        log_decay = coef[0]
        sums = [jnp.zeros_like(log_decay)]
        for o in range(drafts):
            sums.append(sums[-1] + shift(log_decay, o))
        total = sums[1]
        for s in range(1, drafts):
            total = jnp.where(draft == s, sums[s + 1], total)
        coef[0] = jnp.exp(total)
        for o in range(1, drafts):
            coef[1 + o] = jnp.where(draft >= o, jnp.exp(sums[o]), 0.0)
        ahead = jnp.zeros_like(log_decay)
        later = jnp.zeros_like(log_decay)
        for o in range(1, drafts):
            ahead = ahead + shift(log_decay, -o)
            later = jnp.where(left == o, ahead, later)
        coef[1 + drafts] = jnp.where(left >= 0, jnp.exp(later), 0.0)
        coef[2 + drafts] = jnp.exp(total + later)

    lane = lax.broadcasted_iota(jnp.int32, coef.shape[1:], 1)
    row = lax.broadcasted_iota(jnp.int32, (2 * pad, width), 0)
    request = row % pad // drafts
    row3 = lax.broadcasted_iota(jnp.int32, (3 * pad, width), 0)
    request3 = row3 % pad // drafts
    for i in range(group):
        cols = slice(i * width, (i + 1) * width)
        for slot, ref, factor in ((0, query_ref, width ** (-0.5)), (1, key_ref, 1.0)):
            raw = ref[:, cols].astype(F32)
            scale = lax.rsqrt(jnp.sum(raw * raw, axis=1, keepdims=True) + EPS) * factor
            unit[i, slot * pad : slot * pad + tok, :] = raw * scale
        both = unit[i]
        high = both.astype(BF16).astype(F32)
        low = both - high
        spread = []
        for r in range(reqs):
            part = request == r
            spread.append(
                jnp.concatenate(
                    [jnp.where(part, high, 0.0), jnp.where(part, low, 0.0)], axis=0
                ).astype(BF16)
            )
        spread = jnp.concatenate(spread, axis=1)
        prior = jnp.concatenate(
            [
                jnp.concatenate([state_ref[r, repeat * i + j] for j in range(repeat)], axis=1)
                for r in range(reqs)
            ],
            axis=0,
        )
        read = jnp.dot(spread, prior, preferred_element_type=F32)
        query_prior = read[0:pad] + read[2 * pad : 3 * pad]
        key_prior = read[pad : 2 * pad] + read[3 * pad : 4 * pad]
        query, key = both[0:pad], both[pad : 2 * pad]
        shifted = [shift(key, o) for o in range(drafts)]
        query_key = [jnp.sum(query * s, axis=1, keepdims=True) for s in shifted]
        key_key = [jnp.sum(key * s, axis=1, keepdims=True) for s in shifted]
        written = []
        keeps = []
        for j in range(repeat):
            head = (step * group + i) * repeat + j
            vcols = slice((repeat * i + j) * vwidth, (repeat * i + j + 1) * vwidth)
            at = slice(j * vwidth, (j + 1) * vwidth)

            def column(index):
                return jnp.sum(jnp.where(lane == head, coef[index], 0.0), axis=1, keepdims=True)

            through, rate = column(0), column(1)
            decays = [column(1 + o) for o in range(1, drafts)]
            vals[j, 0:tok, :] = value_ref[:, vcols].astype(F32)
            base = rate * (vals[j] - through * key_prior[:, at])
            mixes = [rate * decays[o - 1] * key_key[o] for o in range(1, drafts)]
            delta = base
            for _ in range(1, drafts):
                delta = base - sum(mixes[o - 1] * shift(delta, o) for o in range(1, drafts))
            out = through * query_prior[:, at] + query_key[0] * delta
            for o in range(1, drafts):
                out = out + (decays[o - 1] * query_key[o]) * shift(delta, o)
            norm = lax.rsqrt(jnp.mean(out * out, axis=1, keepdims=True) + EPS)
            gate = gate_ref[:, vcols].astype(F32)
            mixed = (out * norm)[0:tok] * gain_ref[...] * jax.nn.silu(gate)
            mixed_ref[:, vcols] = mixed.astype(BF16)
            written.append(column(1 + drafts) * delta)
            keeps.append(jnp.broadcast_to(column(2 + drafts), (pad, vwidth)))
        written = jnp.concatenate(written, axis=1)
        whigh = written.astype(BF16).astype(F32)
        wlow = written - whigh
        wrote = jnp.concatenate([whigh, wlow, whigh], axis=0).astype(BF16)
        kcat = jnp.concatenate([high[pad:], high[pad:], low[pad:]], axis=0)
        kspread = jnp.concatenate(
            [jnp.where(request3 == r, kcat, 0.0).astype(BF16) for r in range(reqs)], axis=1
        )
        update = lax.dot_general(
            kspread, wrote, (((0,), (0,)), ((), ())), preferred_element_type=F32
        )
        for r in range(reqs):
            for j in range(repeat):
                keep = keeps[j][r * drafts : r * drafts + 1, :]
                kept_ref[r, repeat * i + j] = (
                    keep * state_ref[r, repeat * i + j].astype(F32)
                    + update[r * width : (r + 1) * width, j * vwidth : (j + 1) * vwidth]
                ).astype(BF16)


def delta_rule(
    query_in,
    key_in,
    value_in,
    gate_in,
    decay_in,
    beta_in,
    decay_rate,
    decay_bias,
    norm_gain,
    prior_state,
    accepted,
):
    tok = query_in.shape[0]
    reqs, heads, width, vwidth = prior_state.shape
    drafts = tok // reqs
    query_heads = query_in.shape[1] // width
    repeat = heads // query_heads
    group = 2 if query_heads % 2 == 0 else 1
    pad = round_up(tok, 8)
    whole = lambda *shape: pl.BlockSpec(shape, lambda g: (0,) * len(shape))
    qblock = pl.BlockSpec((tok, group * width), lambda g: (0, g))
    vblock = pl.BlockSpec((tok, group * repeat * vwidth), lambda g: (0, g))
    sblock = pl.BlockSpec((reqs, group * repeat, width, vwidth), lambda g: (0, g, 0, 0))
    return pl.pallas_call(
        functools.partial(delta_kernel, drafts, group),
        grid=(query_heads // group,),
        in_specs=[
            pl.BlockSpec(memory_space=pltpu.SMEM),
            qblock,
            qblock,
            vblock,
            vblock,
            whole(tok, heads),
            whole(tok, heads),
            whole(1, heads),
            whole(1, heads),
            whole(1, vwidth),
            sblock,
        ],
        out_specs=[vblock, sblock],
        out_shape=[
            jax.ShapeDtypeStruct((tok, heads * vwidth), BF16),
            jax.ShapeDtypeStruct(prior_state.shape, BF16),
        ],
        scratch_shapes=[
            pltpu.VMEM((3 + drafts, pad, heads), F32),
            pltpu.VMEM((group, 2 * pad, width), F32),
            pltpu.VMEM((repeat, pad, vwidth), F32),
        ],
        compiler_params=pltpu.CompilerParams(vmem_limit_bytes=32 * 1024 * 1024),
        cost_estimate=pl.CostEstimate(
            flops=4 * heads * reqs * width * vwidth * 96,
            bytes_accessed=4 * heads * reqs * width * vwidth,
            transcendentals=0,
        ),
    )(
        accepted,
        query_in,
        key_in,
        value_in,
        gate_in,
        decay_in,
        beta_in,
        decay_rate.reshape(1, heads),
        decay_bias.reshape(1, heads),
        norm_gain.reshape(1, vwidth),
        prior_state,
    )


def swap(values, mask):
    count = lax.axis_size("rows")
    return lax.ppermute(values, "rows", [(i, i ^ mask) for i in range(count)])


def routing(expert_ids, expert_scores, experts):
    weights = expert_scores / jnp.sum(expert_scores, axis=1, keepdims=True)
    named = expert_ids[:, :, None] == jnp.arange(experts, dtype=jnp.int32)
    dense = jnp.sum(jnp.where(named, weights[:, :, None], 0.0), axis=1)
    high = dense.astype(BF16)
    low = (dense - high.astype(F32)).astype(BF16)
    return jnp.concatenate([high, low], axis=1)


def run_experts(tokens, routes, ups, downs, numbers, experts):
    total = None
    for up, down, number in zip(ups, downs, numbers):
        inner = down.shape[0]
        full = jnp.dot(tokens, up, preferred_element_type=F32)
        here = lax.dynamic_slice(routes, (0, number), (routes.shape[0], 1)).astype(F32)
        rest = lax.dynamic_slice(routes, (0, experts + number), (routes.shape[0], 1)).astype(F32)
        act = jax.nn.silu(full[:, :inner]) * full[:, inner:] * (here + rest)
        term = jnp.dot(act.astype(BF16), down, preferred_element_type=F32)
        total = term if total is None else total + term
    return total


def plane_layer(
    mixed,
    out_weight,
    residual,
    post_gain,
    expert_ids,
    expert_scores,
    expert_up,
    expert_down,
):
    count = lax.axis_size("rows")
    line = count // 4
    me = lax.axis_index("rows")
    here = me // 4
    others = range(1, line)
    tok, full = residual.shape
    exp_dev = expert_up.shape[0]
    experts = exp_dev * count
    part = full // line

    weight_x = swap(out_weight, 2)
    up_mate = swap(expert_up, 1)
    down_mate = swap(expert_down, 1)
    weights = [out_weight, swap(out_weight, 1), weight_x, swap(weight_x, 1)]
    projection = jnp.zeros((out_weight.shape[0], part), BF16)
    for mask, piece in enumerate(weights):
        projection = lax.dynamic_update_slice(
            projection, piece, (0, ((me % 4) ^ mask) * piece.shape[1])
        )

    routes = routing(expert_ids, expert_scores, experts)
    own_res = [
        lax.dynamic_slice(residual, (0, (here ^ m) * part), (tok, part)) for m in range(line)
    ]
    packed = [jnp.concatenate([mixed, own_res[m], routes], axis=1) for m in range(line)]
    got = [packed[0]] + [swap(packed[m], 4 * m) for m in others]
    got = jnp.concatenate(got, axis=0)
    width = mixed.shape[1]
    hidden = got[:, width : width + part].astype(F32) + jnp.dot(
        got[:, :width], projection, preferred_element_type=F32
    )
    hidden = hidden.astype(BF16)
    routes = got[:, width + part :]

    hid = jnp.zeros((line * tok, full), BF16)
    for m in range(line):
        piece = hidden if m == 0 else swap(hidden, 4 * m)
        piece = jnp.concatenate([piece[tok * (j ^ m) : tok * (j ^ m) + tok] for j in range(line)], axis=0)
        hid = lax.dynamic_update_slice(hid, piece, (0, (here ^ m) * part))
    hid = hid.astype(F32)
    scale = lax.rsqrt(jnp.mean(hid * hid, axis=1, keepdims=True) + EPS)
    normed = (hid * scale * post_gain).astype(BF16)

    sent = jnp.concatenate([normed, routes], axis=1)
    came = swap(sent, 2)
    ups = [expert_up[i] for i in range(exp_dev)] + [up_mate[i] for i in range(exp_dev)]
    downs = [expert_down[i] for i in range(exp_dev)] + [down_mate[i] for i in range(exp_dev)]
    numbers = [me * exp_dev + i for i in range(exp_dev)] + [(me ^ 1) * exp_dev + i for i in range(exp_dev)]
    own_sum = run_experts(normed, routes, ups, downs, numbers, experts)
    far_sum = run_experts(came[:, :full], came[:, full:], ups, downs, numbers, experts)
    back = swap(far_sum.astype(BF16), 2)
    total = own_sum + back.astype(F32)
    out = hid[:tok] + total[:tok]
    for m in others:
        out = out + swap(total[m * tok : (m + 1) * tok].astype(BF16), 4 * m).astype(F32)
    return out.astype(BF16)


def general_layer(
    mixed,
    out_weight,
    residual,
    post_gain,
    expert_ids,
    expert_scores,
    expert_up,
    expert_down,
):
    partial_value = jnp.dot(
        mixed,
        lax.all_gather(out_weight, "rows", axis=1, tiled=True),
        preferred_element_type=F32,
    )
    attention = lax.psum_scatter(partial_value, "heads", scatter_dimension=1, tiled=True)
    hidden_sum = residual.astype(F32) + attention
    full_width = residual.shape[1] * lax.axis_size("heads")
    square = lax.psum(jnp.sum(hidden_sum * hidden_sum, axis=1), "heads")
    inv_rms = lax.rsqrt(square / full_width + EPS)
    normed = (hidden_sum * inv_rms[:, None] * post_gain).astype(BF16)
    tok_rows, top_count = expert_ids.shape
    row_count = lax.axis_size("rows")
    exp_dev = expert_up.shape[0]
    experts_all = exp_dev * row_count
    capacity = max(2, (tok_rows * top_count + experts_all - 1) // experts_all + 1)
    half_width = normed.shape[1]
    flat_ids = expert_ids.reshape(-1)
    onehot = (flat_ids[:, None] == jnp.arange(experts_all, dtype=jnp.int32)[None, :]).astype(
        jnp.int32
    )
    earlier = jnp.cumsum(onehot, axis=0) - onehot
    slot_index = jnp.sum(earlier * onehot, axis=1)
    position = (flat_ids % exp_dev * row_count + flat_ids // exp_dev) * capacity + slot_index
    select = (
        jnp.arange(experts_all * capacity, dtype=jnp.int32)[:, None] == position[None, :]
    ).astype(BF16)
    spread = jnp.repeat(normed, top_count, axis=0)
    outgoing = jnp.dot(select, spread, preferred_element_type=F32).astype(BF16)
    outgoing = outgoing.reshape(exp_dev, row_count, capacity, half_width)
    arrived = lax.all_to_all(outgoing, "rows", split_axis=1, concat_axis=1, tiled=True)
    rows_in = arrived.reshape(exp_dev, row_count * capacity, half_width)
    partial_up = jnp.einsum("lnd,ldf->lnf", rows_in, expert_up, preferred_element_type=F32)
    full_up = lax.psum(partial_up, "heads")
    inner_width = expert_down.shape[1]
    activation = (jax.nn.silu(full_up[..., :inner_width]) * full_up[..., inner_width:]).astype(BF16)
    result = jnp.einsum("lnf,lfd->lnd", activation, expert_down, preferred_element_type=F32)
    returned = lax.all_to_all(
        result.astype(BF16).reshape(exp_dev, row_count, capacity, half_width),
        "rows",
        split_axis=1,
        concat_axis=1,
        tiled=True,
    )
    values_back = jnp.dot(select.T, returned.reshape(-1, half_width), preferred_element_type=F32)
    values_back = values_back.reshape(tok_rows, top_count, half_width)
    weights = expert_scores / jnp.sum(expert_scores, axis=1, keepdims=True)
    return (hidden_sum + jnp.sum(weights[:, :, None] * values_back, axis=1)).astype(BF16)


def per_device(mesh_shape, *args):
    delta_args, layer_args = args[:11], args[11:]
    mixed, kept_state = delta_rule(*delta_args)
    short = mesh_shape["heads"] == 1 and mesh_shape["rows"] in (8, 16)
    layer = plane_layer if short else general_layer
    return (layer(mixed, *layer_args), kept_state)


def solution(mesh):
    return jax.shard_map(
        functools.partial(per_device, dict(mesh.shape)),
        mesh=mesh,
        in_specs=(
            P(("groups", "rows"), "heads"),
            P(("groups", "rows"), "heads"),
            P(("groups", "rows"), "heads"),
            P(("groups", "rows"), "heads"),
            P(("groups", "rows"), "heads"),
            P(("groups", "rows"), "heads"),
            P("heads"),
            P("heads"),
            P(),
            P(("groups", "rows"), "heads", None, None),
            P(("groups", "rows")),
            P("heads", "rows"),
            P(("groups", "rows"), "heads"),
            P("heads"),
            P(("groups", "rows"), None),
            P(("groups", "rows"), None),
            P("rows", "heads", None),
            P("rows", None, "heads"),
        ),
        out_specs=(P(("groups", "rows"), "heads"), P(("groups", "rows"), "heads", None, None)),
        check_vma=False,
    )
```

time: 169 us -> 90.3 us (0.53)
  matrix products: 75.5 us -> 7.1 us
  blocking collectives: 27.8 us -> 0 us
  waiting for transfers between devices: 20.4 us -> 36.8 us
  starting transfers between devices: 5.02 us -> 19.9 us
  other arithmetic: 18.2 us -> 4.04 us
  between operations: 14.6 us -> 0.91 us
  local copies, waits for them, and re-layouts: 5.17 us -> 15.1 us
  Pallas kernels: 0 us -> 5.64 us
    dot_general x13 -> x17, matrix products: 75.5 us -> 7.1 us  [the longest x8 3.81 us: run_experts(): full = jnp.dot(tokens, up, preferred_element_type=F32)]
    ppermute x0 -> x16, waiting for transfers between devices: none -> 36.8 us  [swap(): return lax.ppermute(values, 'rows', [(i, i ^ mask) for i in range(count)])]
    all_to_all x1 -> x0, blocking collectives: 27.8 us -> none  [per_device(): lax.all_to_all(outgoing, 'rows', split_axis=1, concat_axis=1, tiled=True)]
    ppermute x0 -> x16, starting transfers between devices: none -> 19.9 us  [swap(): return lax.ppermute(values, 'rows', [(i, i ^ mask) for i in range(count)])]
    all_to_all x1 -> x0, waiting for transfers between devices: 11 us -> none  [per_device(): lax.all_to_all(result.reshape(exp_dev, row_count, capacity, half_width),...]
    convert_element_type x3 -> x4, other arithmetic: 11.2 us -> 0.9 us  [the longest x1 0.7 us: plane_layer(): return out.astype(BF16)]
    unnamed x45 -> x28, local copies, waits for them, and re-layouts: 1.12 us -> 10.4 us
    all_gather x1 -> x0, waiting for transfers between devices: 8.74 us -> none  [per_device(): lax.all_gather(out_weight, 'rows', axis=1, tiled=True)]
  transfers between devices with their start and end apart: 2 -> 16, of which waited for: 2 -> 10; matrix products, arithmetic and copies ran while one was open for 51% -> 17% of each run, Pallas kernels for 0% -> 6%
where the time goes in v1:
time: 90.3 us; the launch traced here: 89.5 us
  waiting for transfers between devices  36.8 us (41%)
  starting transfers between devices  19.9 us (22%)
  local copies, waits for them, and re-layouts  15.1 us (17%)
  matrix products  7.1 us (8%)
  Pallas kernels  5.64 us (6%)
  other arithmetic  4.04 us (4%)
  between operations  0.91 us (1%)
    ppermute x16, waiting for transfers between devices, swap(): return lax.ppermute(values, 'rows', [(i, i ^ mask) for i in range(count)])  36.8 us
    ppermute x16, starting transfers between devices, swap(): return lax.ppermute(values, 'rows', [(i, i ^ mask) for i in range(count)])  19.9 us
    unnamed x28, local copies, waits for them, and re-layouts  10.4 us
    pallas_call x1, Pallas kernels, delta_rule(): pl.pallas_call(functools.partial(delta_kernel, drafts, group), grid=(quer...  5.64 us
    dot_general x8, matrix products, run_experts(): full = jnp.dot(tokens, up, preferred_element_type=F32)  3.81 us
    dot_general x8, matrix products, run_experts(): term = jnp.dot(act.astype(BF16), down, preferred_element_type=F32)  2.8 us
    dynamic_update_slice x4, local copies, waits for them, and re-layouts, plane_layer(): lax.dynamic_update_slice(projection, piece, (0, (me % 4 ^ mask) * piece.s...  2.6 us
  transfers between devices with their start and end apart: 16, of which 10 were waited for; matrix products, arithmetic and copies ran while one was open for 17% of the time, Pallas kernels for 6%

profile of v1, /device:TPU:0, one launch (start us, length us, event | category | flops | bytes accessed | tf_op | source)
XLA Modules:
  0.0 89.5 jit_solution(9111690962547836198)
XLA Ops:
  0.6 3.0 %collective-permute-start.4 = (bf16[2048,128]{1,0:T(8,128)(2,1)}, bf16[2048,128]{1,0:T(8,128)(2,1)}, u32[]{:S(2)}, u32[]{:S(2)}) collective-permute-start(bf16[2048,128]{1,0:T(8,128)(2,1)} %param.29), channel_id=1, source_target_pairs={{0,2},{1,3},{2,0},{3,1},{4,6},{5,7},{6,4},{7,5},{8,10},{9,11},{10,... | collective-permute-start | bytes 1572872 | tf_op jit(solution)/shard_map/ppermute | solution.py:237
  3.6 0.7 reduce_sum.27
  4.4 0.7 broadcast_divide_fusion
  5.1 0.8 select_reduce_fusion
  5.9 0.8 constant_dynamic-slice_fusion.3
  6.7 0.8 copy.28.decay_ref
  7.5 0.8 copy.29.beta_ref
  8.3 1.7 %copy-done = bf16[5,16,128,128]{3,2,1,0:T(8,128)(2,1)S(1)} copy-done((bf16[5,16,128,128]{3,2,1,0:T(8,128)(2,1)S(1)}, bf16[5,16,128,128]{3,2,1,0:T(8,128)(2,1)}, u32[]{:S(2)}) %copy-start) | copy-done | bytes 2621464
  10.0 0.9 copy-done.1
  10.9 0.9 copy-done.2
  11.8 0.8 copy-done.3
  12.6 0.8 copy-done.4
  13.4 0.7 copy-done.5
  14.0 0.7 copy-done.6
  14.7 0.7 copy-done.7
  15.4 0.7 copy-done.8
  16.0 5.6 %shard_map.185 = (bf16[20,2048]{1,0:T(8,128)(2,1)S(1)}, bf16[5,16,128,128]{3,2,1,0:T(8,128)(2,1)}) custom-call(s32[5]{0:T(128)S(1)} %copy-done.5, bf16[20,1024]{1,0:T(8,128)(2,1)S(1)} %copy-done.3, bf16[20,1024]{1,0:T(8,128)(2,1)S(1)} %copy-done.4, bf16[20,2048]{1,0:T(8,128)(2,1)S(1)} %copy-done.1, bf16[20,2048]{1,0:T(8,128)(2,1)S(1)} %copy-done.2, ...), custom_call_target="tpu_custom_call" | custom-call | flops 503316480 | bytes 5242880 | tf_op jit(solution)/shard_map/pallas_call | solution.py:188
  21.7 0.7 concatenate.36
  22.4 1.6 %collective-permute-start = (bf16[20,2624]{1,0:T(8,128)(2,1)}, bf16[20,2624]{1,0:T(8,128)(2,1)S(1)}, u32[]{:S(2)}, u32[]{:S(2)}) collective-permute-start(bf16[20,2624]{1,0:T(8,128)(2,1)} %concatenate.36), channel_id=1, source_target_pairs={{0,4},{1,5},{2,6},{3,7},{4,0},{5,1},{6,2},{7,3},{8,12},{9,13},{10,... | collective-permute-start | bytes 314888 | tf_op jit(solution)/shard_map/ppermute | solution.py:237
  24.1 2.6 %collective-permute-start.1 = (bf16[20,2624]{1,0:T(8,128)(2,1)S(1)}, bf16[20,2624]{1,0:T(8,128)(2,1)S(1)}, u32[]{:S(2)}, u32[]{:S(2)}) collective-permute-start(bf16[20,2624]{1,0:T(8,128)(2,1)S(1)} %concatenate.37), channel_id=1, source_target_pairs={{0,8},{1,9},{2,10},{3,11},{4,12},{5,13},{6,14},{7,15},{8,0},{9,1},... | collective-permute-start | bytes 314888 | tf_op jit(solution)/shard_map/ppermute | solution.py:237
  26.8 0.2 collective-permute-start.2
  27.0 0.1 broadcast_in_dim.27
  27.4 3.4 %collective-permute-done = bf16[20,2624]{1,0:T(8,128)(2,1)S(1)} collective-permute-done((bf16[20,2624]{1,0:T(8,128)(2,1)}, bf16[20,2624]{1,0:T(8,128)(2,1)S(1)}, u32[]{:S(2)}, u32[]{:S(2)}) %collective-permute-start) | collective-permute-done | bytes 104992 | tf_op jit(solution)/shard_map/ppermute | solution.py:237
  30.8 6.0 %collective-permute-done.1 = bf16[20,2624]{1,0:T(8,128)(2,1)S(1)} collective-permute-done((bf16[20,2624]{1,0:T(8,128)(2,1)S(1)}, bf16[20,2624]{1,0:T(8,128)(2,1)S(1)}, u32[]{:S(2)}, u32[]{:S(2)}) %collective-permute-start.1) | collective-permute-done | bytes 104992 | tf_op jit(solution)/shard_map/ppermute | solution.py:237
  36.8 0.5 collective-permute-start.5
  37.5 1.2 %constant_dynamic-update-slice_fusion.3 = bf16[2048,512]{1,0:T(8,128)(2,1)S(1)} fusion(bf16[2048,512]{1,0:T(8,128)(2,1)S(1)} %constant_dynamic-update-slice_fusion.4, bf16[2048,128]{1,0:T(8,128)(2,1)} %collective-permute-done.3, s32[]{:T(128)S(6)} %select_n.89), kind=kLoop, calls=%fused_computation.114 | loop fusion | bytes 1048580 | tf_op jit(solution)/shard_map/dynamic_update_slice | solution.py:288
  38.7 1.2 %constant_dynamic-update-slice_fusion.2 = bf16[2048,512]{1,0:T(8,128)(2,1)S(1)} fusion(bf16[2048,512]{1,0:T(8,128)(2,1)S(1)} %constant_dynamic-update-slice_fusion.3, bf16[2048,128]{1,0:T(8,128)(2,1)} %collective-permute-done.4, s32[]{:T(128)S(6)} %select_n.90), kind=kLoop, calls=%fused_computation.113 | loop fusion | bytes 1048580 | tf_op jit(solution)/shard_map/dynamic_update_slice | solution.py:288
  39.8 5.1 %collective-permute-done.5 = bf16[2048,128]{1,0:T(8,128)(2,1)S(1)} collective-permute-done((bf16[2048,128]{1,0:T(8,128)(2,1)}, bf16[2048,128]{1,0:T(8,128)(2,1)S(1)}, u32[]{:S(2)}, u32[]{:S(2)}) %collective-permute-start.5) | collective-permute-done | bytes 524320 | tf_op jit(solution)/shard_map/ppermute | solution.py:237
  45.1 0.5 constant_dynamic-update-slice_fusion
  45.7 0.3 add_reduce_fusion.5
  46.0 3.1 %collective-permute-start.7 = (bf16[80,512]{1,0:T(8,128)(2,1)S(1)}, bf16[80,512]{1,0:T(8,128)(2,1)S(1)}, u32[]{:S(2)}, u32[]{:S(2)}) collective-permute-start(bf16[80,512]{1,0:T(8,128)(2,1)S(1)} %get-tuple-element.34), channel_id=1, source_target_pairs={{0,8},{1,9},{2,10},{3,11},{4,12},{5,13},{6,14},{7,15},{8,0},{9,1},... | collective-permute-start | bytes 245768 | tf_op jit(solution)/shard_map/ppermute | solution.py:237
  49.1 1.4 %collective-permute-start.8 = (bf16[80,512]{1,0:T(8,128)(2,1)S(1)}, bf16[80,512]{1,0:T(8,128)(2,1)S(1)}, u32[]{:S(2)}, u32[]{:S(2)}) collective-permute-start(bf16[80,512]{1,0:T(8,128)(2,1)S(1)} %get-tuple-element.34), channel_id=1, source_target_pairs={{0,12},{1,13},{2,14},{3,15},{4,8},{5,9},{6,10},{7,11},{8,4},{9,5},... | collective-permute-start | bytes 245768 | tf_op jit(solution)/shard_map/ppermute | solution.py:237
  50.4 0.9 %collective-permute-done.6 = bf16[80,512]{1,0:T(8,128)(2,1)S(1)} collective-permute-done((bf16[80,512]{1,0:T(8,128)(2,1)S(1)}, bf16[80,512]{1,0:T(8,128)(2,1)S(1)}, u32[]{:S(2)}, u32[]{:S(2)}) %collective-permute-start.6) | collective-permute-done | bytes 81952 | tf_op jit(solution)/shard_map/ppermute | solution.py:237
  51.4 4.4 %collective-permute-done.7 = bf16[80,512]{1,0:T(8,128)(2,1)S(1)} collective-permute-done((bf16[80,512]{1,0:T(8,128)(2,1)S(1)}, bf16[80,512]{1,0:T(8,128)(2,1)S(1)}, u32[]{:S(2)}, u32[]{:S(2)}) %collective-permute-start.7) | collective-permute-done | bytes 81952 | tf_op jit(solution)/shard_map/ppermute | solution.py:237
  55.8 0.2 multiply_reduce_fusion
  56.0 0.1 multiply_convert_fusion
  56.2 0.6 collective-permute-start.11
  56.8 0.5 fusion.6
  57.3 0.5 fusion.10
  57.8 1.1 %copy-done.9 = bf16[2,256,2048]{2,1,0:T(8,128)(2,1)S(1)} copy-done((bf16[2,256,2048]{2,1,0:T(8,128)(2,1)S(1)}, bf16[2,256,2048]{2,1,0:T(8,128)(2,1)}, u32[]{:S(2)}) %copy-start.9) | copy-done | bytes 2097176
  58.9 0.3 fusion.25
  59.2 0.4 convolution_add_fusion.3
  59.6 4.7 %collective-permute-done.11 = bf16[80,2112]{1,0:T(8,128)(2,1)S(1)} collective-permute-done((bf16[80,2112]{1,0:T(8,128)(2,1)S(1)}, bf16[80,2112]{1,0:T(8,128)(2,1)S(1)}, u32[]{:S(2)}, u32[]{:S(2)}) %collective-permute-start.11) | collective-permute-done | bytes 337952 | tf_op jit(solution)/shard_map/ppermute | solution.py:237
  64.3 0.2 add_reduce_fusion.1
  64.5 0.5 fusion.8
  65.0 0.3 fusion.23
  65.4 0.5 fusion.4
  65.8 0.4 convolution_add_fusion.1
  66.2 0.5 fusion.14
  66.7 0.5 fusion.12
  67.2 0.3 fusion.27
  67.5 0.4 fusion.3
  67.9 0.6 collective-permute-start.12
  68.5 0.5 fusion.15
  69.0 0.3 fusion.28
  69.3 0.5 fusion.13
  69.8 5.2 %collective-permute-done.12 = bf16[80,2048]{1,0:T(8,128)(2,1)S(1)} collective-permute-done((bf16[80,2048]{1,0:T(8,128)(2,1)S(1)}, bf16[80,2048]{1,0:T(8,128)(2,1)S(1)}, u32[]{:S(2)}, u32[]{:S(2)}) %collective-permute-start.12) | collective-permute-done | bytes 327712 | tf_op jit(solution)/shard_map/ppermute | solution.py:237
  75.0 0.4 fusion.94
  75.4 4.3 %collective-permute-start.13 = (bf16[20,2048]{1,0:T(8,128)(2,1)S(1)}, bf16[20,2048]{1,0:T(8,128)(2,1)S(1)}, u32[]{:S(2)}, u32[]{:S(2)}) collective-permute-start(bf16[20,2048]{1,0:T(8,128)(2,1)S(1)} %get-tuple-element.16), channel_id=1, source_target_pairs={{0,4},{1,5},{2,6},{3,7},{4,0},{5,1},{6,2},{7,3},{8,12},{9,13},{10,... | collective-permute-start | bytes 245768 | tf_op jit(solution)/shard_map/ppermute | solution.py:237
  79.7 2.1 %collective-permute-start.15 = (bf16[20,2048]{1,0:T(8,128)(2,1)S(1)}, bf16[20,2048]{1,0:T(8,128)(2,1)S(1)}, u32[]{:S(2)}, u32[]{:S(2)}) collective-permute-start(bf16[20,2048]{1,0:T(8,128)(2,1)S(1)} %get-tuple-element.17), channel_id=1, source_target_pairs={{0,12},{1,13},{2,14},{3,15},{4,8},{5,9},{6,10},{7,11},{8,4},{9,5},... | collective-permute-start | bytes 245768 | tf_op jit(solution)/shard_map/ppermute | solution.py:237
  81.8 1.6 %collective-permute-done.13 = bf16[20,2048]{1,0:T(8,128)(2,1)S(1)} collective-permute-done((bf16[20,2048]{1,0:T(8,128)(2,1)S(1)}, bf16[20,2048]{1,0:T(8,128)(2,1)S(1)}, u32[]{:S(2)}, u32[]{:S(2)}) %collective-permute-start.13) | collective-permute-done | bytes 81952 | tf_op jit(solution)/shard_map/ppermute | solution.py:237
  83.4 2.8 %collective-permute-done.15 = bf16[20,2048]{1,0:T(8,128)(2,1)S(1)} collective-permute-done((bf16[20,2048]{1,0:T(8,128)(2,1)S(1)}, bf16[20,2048]{1,0:T(8,128)(2,1)S(1)}, u32[]{:S(2)}, u32[]{:S(2)}) %collective-permute-start.15) | collective-permute-done | bytes 81952 | tf_op jit(solution)/shard_map/ppermute | solution.py:237
  86.2 2.6 %collective-permute-done.14 = bf16[20,2048]{1,0:T(8,128)(2,1)S(1)} collective-permute-done((bf16[20,2048]{1,0:T(8,128)(2,1)S(1)}, bf16[20,2048]{1,0:T(8,128)(2,1)S(1)}, u32[]{:S(2)}, u32[]{:S(2)}) %collective-permute-start.14) | collective-permute-done | bytes 81952 | tf_op jit(solution)/shard_map/ppermute | solution.py:237
  88.8 0.7 fusion.41
  (47 shorter events, 1.1 us)
Async XLA Ops:
  0.6 36.2 %collective-permute-start.4 = (bf16[2048,128]{1,0:T(8,128)(2,1)}, bf16[2048,128]{1,0:T(8,128)(2,1)}, u32[]{:S(2)}, u32[]{:S(2)}) collective-permute-start(bf16[2048,128]{1,0:T(8,128)(2,1)} %param.29), channel_id=1, source_target_pairs={{0,2},{1,3},{2,0},{3,1},{4,6},{5,7},{6,4},{7,5},{8,10},{9,11},{10,... | collective-permute-start | bytes 1572872 | tf_op jit(solution)/shard_map/ppermute | solution.py:237
  3.6 33.8 %collective-permute-start.3 = (bf16[2048,128]{1,0:T(8,128)(2,1)}, bf16[2048,128]{1,0:T(8,128)(2,1)}, u32[]{:S(2)}, u32[]{:S(2)}) collective-permute-start(bf16[2048,128]{1,0:T(8,128)(2,1)} %param.29), channel_id=1, source_target_pairs={{0,1},{1,0},{2,3},{3,2},{4,5},{5,4},{6,7},{7,6},{8,9},{9,8},{10,11... | collective-permute-start | bytes 1572872 | tf_op jit(solution)/shard_map/ppermute | solution.py:237
  8.3 1.7 %copy-start = (bf16[5,16,128,128]{3,2,1,0:T(8,128)(2,1)S(1)}, bf16[5,16,128,128]{3,2,1,0:T(8,128)(2,1)}, u32[]{:S(2)}) copy-start(bf16[5,16,128,128]{3,2,1,0:T(8,128)(2,1)} %state_ref.1) | copy-start | bytes 7864324
  10.0 0.9 copy-start.1
  10.9 0.9 copy-start.2
  11.8 0.8 copy-start.3
  12.6 0.8 copy-start.4
  13.4 0.7 copy-start.5
  14.0 0.7 copy-start.6
  14.7 0.7 copy-start.7
  15.4 0.7 copy-start.8
  21.7 5.5 %copy-start.10 = (bf16[2048,128]{1,0:T(8,128)(2,1)S(1)}, bf16[2048,128]{1,0:T(8,128)(2,1)}, u32[]{:S(2)}) copy-start(bf16[2048,128]{1,0:T(8,128)(2,1)} %param.29) | copy-start | bytes 1572868
  22.4 8.4 %collective-permute-start = (bf16[20,2624]{1,0:T(8,128)(2,1)}, bf16[20,2624]{1,0:T(8,128)(2,1)S(1)}, u32[]{:S(2)}, u32[]{:S(2)}) collective-permute-start(bf16[20,2624]{1,0:T(8,128)(2,1)} %concatenate.36), channel_id=1, source_target_pairs={{0,4},{1,5},{2,6},{3,7},{4,0},{5,1},{6,2},{7,3},{8,12},{9,13},{10,... | collective-permute-start | bytes 314888 | tf_op jit(solution)/shard_map/ppermute | solution.py:237
  24.1 12.8 %collective-permute-start.1 = (bf16[20,2624]{1,0:T(8,128)(2,1)S(1)}, bf16[20,2624]{1,0:T(8,128)(2,1)S(1)}, u32[]{:S(2)}, u32[]{:S(2)}) collective-permute-start(bf16[20,2624]{1,0:T(8,128)(2,1)S(1)} %concatenate.37), channel_id=1, source_target_pairs={{0,8},{1,9},{2,10},{3,11},{4,12},{5,13},{6,14},{7,15},{8,0},{9,1},... | collective-permute-start | bytes 314888 | tf_op jit(solution)/shard_map/ppermute | solution.py:237
  26.8 10.6 %collective-permute-start.2 = (bf16[20,2624]{1,0:T(8,128)(2,1)S(1)}, bf16[20,2624]{1,0:T(8,128)(2,1)S(1)}, u32[]{:S(2)}, u32[]{:S(2)}) collective-permute-start(bf16[20,2624]{1,0:T(8,128)(2,1)S(1)} %concatenate.38), channel_id=1, source_target_pairs={{0,12},{1,13},{2,14},{3,15},{4,8},{5,9},{6,10},{7,11},{8,4},{9,5},... | collective-permute-start | bytes 314888 | tf_op jit(solution)/shard_map/ppermute | solution.py:237
  30.8 36.4 %collective-permute-start.10 = (bf16[2,256,2048]{2,1,0:T(8,128)(2,1)}, bf16[2,256,2048]{2,1,0:T(8,128)(2,1)S(1)}, u32[]{:S(2)}, u32[]{:S(2)}) collective-permute-start(bf16[2,256,2048]{2,1,0:T(8,128)(2,1)} %param.35), channel_id=1, source_target_pairs={{0,1},{1,0},{2,3},{3,2},{4,5},{5,4},{6,7},{7,6},{8,9},{9,8},{10,11... | collective-permute-start | bytes 6291464 | tf_op jit(solution)/shard_map/ppermute | solution.py:237
  36.8 29.4 %collective-permute-start.9 = (bf16[2,2048,512]{2,1,0:T(8,128)(2,1)}, bf16[2,2048,512]{2,1,0:T(8,128)(2,1)S(1)}, u32[]{:S(2)}, u32[]{:S(2)}) collective-permute-start(bf16[2,2048,512]{2,1,0:T(8,128)(2,1)} %param.34), channel_id=1, source_target_pairs={{0,1},{1,0},{2,3},{3,2},{4,5},{5,4},{6,7},{7,6},{8,9},{9,8},{10,11... | collective-permute-start | bytes 12582920 | tf_op jit(solution)/shard_map/ppermute | solution.py:237
  36.8 8.1 %collective-permute-start.5 = (bf16[2048,128]{1,0:T(8,128)(2,1)}, bf16[2048,128]{1,0:T(8,128)(2,1)S(1)}, u32[]{:S(2)}, u32[]{:S(2)}) collective-permute-start(bf16[2048,128]{1,0:T(8,128)(2,1)} %collective-permute-done.4), channel_id=1, source_target_pairs={{0,1},{1,0},{2,3},{3,2},{4,5},{5,4},{6,7},{7,6},{8,9},{9,8},{10,11... | collective-permute-start | bytes 1572872 | tf_op jit(solution)/shard_map/ppermute | solution.py:237
  45.1 10.9 %copy-start.11 = (f32[2048]{0:T(1024)S(1)}, f32[2048]{0:T(1024)}, u32[]{:S(2)}) copy-start(f32[2048]{0:T(1024)} %param.31) | copy-start | bytes 24580
  45.1 11.7 %copy-start.12 = (bf16[2,2048,512]{2,1,0:T(8,128)(2,1)S(1)}, bf16[2,2048,512]{2,1,0:T(8,128)(2,1)}, u32[]{:S(2)}) copy-start(bf16[2,2048,512]{2,1,0:T(8,128)(2,1)} %param.34) | copy-start | bytes 12582916
  45.6 5.7 %collective-permute-start.6 = (bf16[80,512]{1,0:T(8,128)(2,1)S(1)}, bf16[80,512]{1,0:T(8,128)(2,1)S(1)}, u32[]{:S(2)}, u32[]{:S(2)}) collective-permute-start(bf16[80,512]{1,0:T(8,128)(2,1)S(1)} %get-tuple-element.34), channel_id=1, source_target_pairs={{0,4},{1,5},{2,6},{3,7},{4,0},{5,1},{6,2},{7,3},{8,12},{9,13},{10,... | collective-permute-start | bytes 245768 | tf_op jit(solution)/shard_map/ppermute | solution.py:237
  46.0 9.8 %collective-permute-start.7 = (bf16[80,512]{1,0:T(8,128)(2,1)S(1)}, bf16[80,512]{1,0:T(8,128)(2,1)S(1)}, u32[]{:S(2)}, u32[]{:S(2)}) collective-permute-start(bf16[80,512]{1,0:T(8,128)(2,1)S(1)} %get-tuple-element.34), channel_id=1, source_target_pairs={{0,8},{1,9},{2,10},{3,11},{4,12},{5,13},{6,14},{7,15},{8,0},{9,1},... | collective-permute-start | bytes 245768 | tf_op jit(solution)/shard_map/ppermute | solution.py:237
  49.1 6.7 %collective-permute-start.8 = (bf16[80,512]{1,0:T(8,128)(2,1)S(1)}, bf16[80,512]{1,0:T(8,128)(2,1)S(1)}, u32[]{:S(2)}, u32[]{:S(2)}) collective-permute-start(bf16[80,512]{1,0:T(8,128)(2,1)S(1)} %get-tuple-element.34), channel_id=1, source_target_pairs={{0,12},{1,13},{2,14},{3,15},{4,8},{5,9},{6,10},{7,11},{8,4},{9,5},... | collective-permute-start | bytes 245768 | tf_op jit(solution)/shard_map/ppermute | solution.py:237
  56.2 8.1 %collective-permute-start.11 = (bf16[80,2112]{1,0:T(8,128)(2,1)S(1)}, bf16[80,2112]{1,0:T(8,128)(2,1)S(1)}, u32[]{:S(2)}, u32[]{:S(2)}) collective-permute-start(bf16[80,2112]{1,0:T(8,128)(2,1)S(1)} %pad_maximum_fusion.1), channel_id=1, source_target_pairs={{0,2},{1,3},{2,0},{3,1},{4,6},{5,7},{6,4},{7,5},{8,10},{9,11},{10,... | collective-permute-start | bytes 1013768 | tf_op jit(solution)/shard_map/ppermute | solution.py:237
  57.3 1.6 %copy-start.9 = (bf16[2,256,2048]{2,1,0:T(8,128)(2,1)S(1)}, bf16[2,256,2048]{2,1,0:T(8,128)(2,1)}, u32[]{:S(2)}) copy-start(bf16[2,256,2048]{2,1,0:T(8,128)(2,1)} %param.35) | copy-start | bytes 6291460
  67.9 7.1 %collective-permute-start.12 = (bf16[80,2048]{1,0:T(8,128)(2,1)S(1)}, bf16[80,2048]{1,0:T(8,128)(2,1)S(1)}, u32[]{:S(2)}, u32[]{:S(2)}) collective-permute-start(bf16[80,2048]{1,0:T(8,128)(2,1)S(1)} %fusion.3), channel_id=1, source_target_pairs={{0,2},{1,3},{2,0},{3,1},{4,6},{5,7},{6,4},{7,5},{8,10},{9,11},{10,... | collective-permute-start | bytes 983048 | tf_op jit(solution)/shard_map/ppermute | solution.py:237
  75.4 8.0 %collective-permute-start.13 = (bf16[20,2048]{1,0:T(8,128)(2,1)S(1)}, bf16[20,2048]{1,0:T(8,128)(2,1)S(1)}, u32[]{:S(2)}, u32[]{:S(2)}) collective-permute-start(bf16[20,2048]{1,0:T(8,128)(2,1)S(1)} %get-tuple-element.16), channel_id=1, source_target_pairs={{0,4},{1,5},{2,6},{3,7},{4,0},{5,1},{6,2},{7,3},{8,12},{9,13},{10,... | collective-permute-start | bytes 245768 | tf_op jit(solution)/shard_map/ppermute | solution.py:237
  79.7 6.5 %collective-permute-start.15 = (bf16[20,2048]{1,0:T(8,128)(2,1)S(1)}, bf16[20,2048]{1,0:T(8,128)(2,1)S(1)}, u32[]{:S(2)}, u32[]{:S(2)}) collective-permute-start(bf16[20,2048]{1,0:T(8,128)(2,1)S(1)} %get-tuple-element.17), channel_id=1, source_target_pairs={{0,12},{1,13},{2,14},{3,15},{4,8},{5,9},{6,10},{7,11},{8,4},{9,5},... | collective-permute-start | bytes 245768 | tf_op jit(solution)/shard_map/ppermute | solution.py:237
  81.7 7.1 %collective-permute-start.14 = (bf16[20,2048]{1,0:T(8,128)(2,1)S(1)}, bf16[20,2048]{1,0:T(8,128)(2,1)S(1)}, u32[]{:S(2)}, u32[]{:S(2)}) collective-permute-start(bf16[20,2048]{1,0:T(8,128)(2,1)S(1)} %get-tuple-element.18), channel_id=1, source_target_pairs={{0,8},{1,9},{2,10},{3,11},{4,12},{5,13},{6,14},{7,15},{8,0},{9,1},... | collective-permute-start | bytes 245768 | tf_op jit(solution)/shard_map/ppermute | solution.py:237

commit v2 on v1

--- a/solution.py
+++ b/solution.py
@@ -19,6 +19,7 @@
 def delta_kernel(
     drafts,
     group,
+    line,
     accepted_ref,
     query_ref,
     key_ref,
@@ -30,54 +31,85 @@
     bias_ref,
     gain_ref,
     state_ref,
-    mixed_ref,
-    kept_ref,
-    coef,
-    unit,
-    vals,
+    *refs,
 ):
+    if line:
+        residual_ref, ids_ref, scores_ref = refs[:3]
+        packed_refs, refs = refs[3 : 3 + line], refs[3 + line :]
+        kept_ref, coef, unit, vals, mixed_ref, pack = refs
+    else:
+        mixed_ref, kept_ref, coef, unit, vals = refs
     step = pl.program_id(0)
     tok = query_ref.shape[0]
-    pad = coef.shape[1]
+    pad = unit.shape[1] // 2
     reqs, _, width, vwidth = state_ref.shape
     repeat = state_ref.shape[1] // group
+    heads = decay_ref.shape[0]
 
     def shift(values, by):
         return pltpu.roll(values, by % pad, 0) if by % pad else values
 
+    def ahead_of(values, by):
+        return pltpu.roll(values, by % 128, 1) if by % 128 else values
+
     @pl.when(step == 0)
     def _():
-        heads = decay_ref.shape[1]
-        coef[...] = jnp.zeros_like(coef)
         unit[...] = jnp.zeros_like(unit)
         vals[...] = jnp.zeros_like(vals)
-        at = lax.broadcasted_iota(jnp.int32, (pad, heads), 0)
+        coef[...] = jnp.zeros_like(coef)
+        square = (heads, heads)
+        eye = lax.broadcasted_iota(jnp.int32, square, 0) == lax.broadcasted_iota(jnp.int32, square, 1)
+        rate = jnp.sum(jnp.where(eye, rate_ref[...], 0.0), axis=1, keepdims=True)
+        bias = jnp.sum(jnp.where(eye, bias_ref[...], 0.0), axis=1, keepdims=True)
+        coef[0:heads, 0:tok] = -rate * jax.nn.softplus(decay_ref[...] + bias)
+        coef[heads : 2 * heads, 0:tok] = jax.nn.sigmoid(beta_ref[...])
+        log_decay = coef[0:heads]
+        at = lax.broadcasted_iota(jnp.int32, log_decay.shape, 1)
         draft = at % drafts
         left = jnp.zeros_like(at)
         for r in range(reqs):
             left = jnp.where(at // drafts == r, accepted_ref[r], left)
         left = left - 1 - draft
-        coef[0, 0:tok, :] = -rate_ref[...] * jax.nn.softplus(decay_ref[...] + bias_ref[...])
-        coef[1, 0:tok, :] = jax.nn.sigmoid(beta_ref[...])
-        log_decay = coef[0]
         sums = [jnp.zeros_like(log_decay)]
         for o in range(drafts):
-            sums.append(sums[-1] + shift(log_decay, o))
+            sums.append(sums[-1] + ahead_of(log_decay, o))
         total = sums[1]
         for s in range(1, drafts):
             total = jnp.where(draft == s, sums[s + 1], total)
-        coef[0] = jnp.exp(total)
+        coef[0:heads] = jnp.exp(total)
         for o in range(1, drafts):
-            coef[1 + o] = jnp.where(draft >= o, jnp.exp(sums[o]), 0.0)
+            coef[(1 + o) * heads : (2 + o) * heads] = jnp.where(draft >= o, jnp.exp(sums[o]), 0.0)
         ahead = jnp.zeros_like(log_decay)
         later = jnp.zeros_like(log_decay)
         for o in range(1, drafts):
-            ahead = ahead + shift(log_decay, -o)
+            ahead = ahead + ahead_of(log_decay, -o)
             later = jnp.where(left == o, ahead, later)
-        coef[1 + drafts] = jnp.where(left >= 0, jnp.exp(later), 0.0)
-        coef[2 + drafts] = jnp.exp(total + later)
-
-    lane = lax.broadcasted_iota(jnp.int32, coef.shape[1:], 1)
+        coef[(1 + drafts) * heads : (2 + drafts) * heads] = jnp.where(
+            left >= 0, jnp.exp(later), 0.0
+        )
+        coef[(2 + drafts) * heads : (3 + drafts) * heads] = jnp.exp(total + later)
+        coef[...] = coef[...].T
+        if line:
+            rows = pack.shape[0] // 2
+            half = mixed_ref.shape[1] // 2
+            scores = scores_ref[...]
+            scores = scores / jnp.sum(scores, axis=0, keepdims=True)
+            experts = 64
+            number = lax.broadcasted_iota(jnp.int32, (experts, tok), 0)
+            dense = jnp.zeros((experts, tok), F32)
+            for k in range(ids_ref.shape[0]):
+                dense = dense + jnp.where(number == ids_ref[k : k + 1, :], scores[k : k + 1], 0.0)
+            high = dense.astype(BF16).astype(F32)
+            routes = jnp.concatenate([high, dense - high], axis=0)
+            routes = jnp.concatenate(
+                [routes, jnp.zeros((2 * experts, 128 - tok), F32)], axis=1
+            ).T
+            pack[...] = jnp.zeros_like(pack)
+            part = mixed_ref.shape[1] // line
+            at = half + part - (pack.shape[1] - half)
+            pack[rows : 2 * rows, at : at + 128] = routes[0:tok]
+
+    lane = lax.broadcasted_iota(jnp.int32, (pad, coef.shape[1]), 1)
     row = lax.broadcasted_iota(jnp.int32, (2 * pad, width), 0)
     request = row % pad // drafts
     row3 = lax.broadcasted_iota(jnp.int32, (3 * pad, width), 0)
@@ -122,7 +154,8 @@
             at = slice(j * vwidth, (j + 1) * vwidth)
 
             def column(index):
-                return jnp.sum(jnp.where(lane == head, coef[index], 0.0), axis=1, keepdims=True)
+                mine = jnp.where(lane == index * heads + head, coef[0:pad], 0.0)
+                return jnp.sum(mine, axis=1, keepdims=True)
 
             through, rate = column(0), column(1)
             decays = [column(1 + o) for o in range(1, drafts)]
@@ -138,7 +171,12 @@
             norm = lax.rsqrt(jnp.mean(out * out, axis=1, keepdims=True) + EPS)
             gate = gate_ref[:, vcols].astype(F32)
             mixed = (out * norm)[0:tok] * gain_ref[...] * jax.nn.silu(gate)
-            mixed_ref[:, vcols] = mixed.astype(BF16)
+            if line:
+                span = group * repeat * vwidth
+                to = pl.multiple_of(step * span, span) + (repeat * i + j) * vwidth
+                mixed_ref[0:tok, pl.ds(to, vwidth)] = mixed
+            else:
+                mixed_ref[:, vcols] = mixed.astype(BF16)
             written.append(column(1 + drafts) * delta)
             keeps.append(jnp.broadcast_to(column(2 + drafts), (pad, vwidth)))
         written = jnp.concatenate(written, axis=1)
@@ -161,6 +199,25 @@
                 ).astype(BF16)
 
 
+    if not line:
+        return
+
+    @pl.when(step == pl.num_programs(0) - 1)
+    def _():
+        here = lax.axis_index("rows") // 4
+        full = mixed_ref.shape[1]
+        half, part = full // 2, full // line
+        extra = pack.shape[1] - half
+        pack[0:tok, 0:half] = mixed_ref[0:tok, 0:half]
+        pack[tok : 2 * tok, 0:half] = mixed_ref[0:tok, half:full]
+        for m in range(line):
+            to = pl.multiple_of((here ^ m) * part, part)
+            piece = residual_ref[:, pl.ds(to, part)].astype(F32)
+            pack[0:tok, half : half + extra] = piece[:, 0:extra]
+            pack[tok : 2 * tok, half : half + part - extra] = piece[:, extra:part]
+            packed_refs[m][...] = pack[...].astype(BF16)
+
+
 def delta_rule(
     query_in,
     key_in,
@@ -173,6 +230,10 @@
     norm_gain,
     prior_state,
     accepted,
+    line=0,
+    residual=None,
+    expert_ids=None,
+    expert_scores=None,
 ):
     tok = query_in.shape[0]
     reqs, heads, width, vwidth = prior_state.shape
@@ -185,51 +246,68 @@
     qblock = pl.BlockSpec((tok, group * width), lambda g: (0, g))
     vblock = pl.BlockSpec((tok, group * repeat * vwidth), lambda g: (0, g))
     sblock = pl.BlockSpec((reqs, group * repeat, width, vwidth), lambda g: (0, g, 0, 0))
-    return pl.pallas_call(
-        functools.partial(delta_kernel, drafts, group),
-        grid=(query_heads // group,),
-        in_specs=[
-            pl.BlockSpec(memory_space=pltpu.SMEM),
-            qblock,
-            qblock,
-            vblock,
-            vblock,
-            whole(tok, heads),
-            whole(tok, heads),
-            whole(1, heads),
-            whole(1, heads),
-            whole(1, vwidth),
-            sblock,
-        ],
-        out_specs=[vblock, sblock],
-        out_shape=[
-            jax.ShapeDtypeStruct((tok, heads * vwidth), BF16),
-            jax.ShapeDtypeStruct(prior_state.shape, BF16),
-        ],
-        scratch_shapes=[
-            pltpu.VMEM((3 + drafts, pad, heads), F32),
-            pltpu.VMEM((group, 2 * pad, width), F32),
-            pltpu.VMEM((repeat, pad, vwidth), F32),
-        ],
-        compiler_params=pltpu.CompilerParams(vmem_limit_bytes=32 * 1024 * 1024),
-        cost_estimate=pl.CostEstimate(
-            flops=4 * heads * reqs * width * vwidth * 96,
-            bytes_accessed=4 * heads * reqs * width * vwidth,
-            transcendentals=0,
-        ),
-    )(
+    in_specs = [
+        pl.BlockSpec(memory_space=pltpu.SMEM),
+        qblock,
+        qblock,
+        vblock,
+        vblock,
+        whole(heads, tok),
+        whole(heads, tok),
+        whole(1, heads),
+        whole(1, heads),
+        whole(1, vwidth),
+        sblock,
+    ]
+    args = [
         accepted,
         query_in,
         key_in,
         value_in,
         gate_in,
-        decay_in,
-        beta_in,
+        decay_in.T,
+        beta_in.T,
         decay_rate.reshape(1, heads),
         decay_bias.reshape(1, heads),
         norm_gain.reshape(1, vwidth),
         prior_state,
-    )
+    ]
+    scratch = [
+        pltpu.VMEM((128, 128), F32),
+        pltpu.VMEM((group, 2 * pad, width), F32),
+        pltpu.VMEM((repeat, pad, vwidth), F32),
+    ]
+    kept = jax.ShapeDtypeStruct(prior_state.shape, BF16)
+    full = heads * vwidth
+    if line:
+        packed = packed_shape(tok, full, line)
+        out_specs = [whole(*packed)] * line + [sblock]
+        out_shape = [jax.ShapeDtypeStruct(packed, BF16)] * line + [kept]
+        scratch += [pltpu.VMEM((pad, full), F32), pltpu.VMEM(packed, F32)]
+        top = expert_ids.shape[1]
+        in_specs += [whole(tok, full), whole(top, tok), whole(top, tok)]
+        args += [residual, expert_ids.T, expert_scores.T]
+    else:
+        out_specs = [vblock, sblock]
+        out_shape = [jax.ShapeDtypeStruct((tok, full), BF16), kept]
+    return pl.pallas_call(
+        functools.partial(delta_kernel, drafts, group, line),
+        grid=(query_heads // group,),
+        in_specs=in_specs,
+        out_specs=out_specs,
+        out_shape=out_shape,
+        scratch_shapes=scratch,
+        compiler_params=pltpu.CompilerParams(vmem_limit_bytes=56 * 1024 * 1024),
+        cost_estimate=pl.CostEstimate(
+            flops=1024 * heads * reqs * width * vwidth * 16,
+            bytes_accessed=64 * heads * reqs * width * vwidth,
+            transcendentals=0,
+        ),
+    )(*args)
+
+
+def packed_shape(tok, full, line):
+    return (2 * tok, full // 2 + round_up(full // line + 128, 256) // 2)
 
 
 def swap(values, mask):
@@ -237,22 +315,14 @@
     return lax.ppermute(values, "rows", [(i, i ^ mask) for i in range(count)])
 
 
-def routing(expert_ids, expert_scores, experts):
-    weights = expert_scores / jnp.sum(expert_scores, axis=1, keepdims=True)
-    named = expert_ids[:, :, None] == jnp.arange(experts, dtype=jnp.int32)
-    dense = jnp.sum(jnp.where(named, weights[:, :, None], 0.0), axis=1)
-    high = dense.astype(BF16)
-    low = (dense - high.astype(F32)).astype(BF16)
-    return jnp.concatenate([high, low], axis=1)
-
-
-def run_experts(tokens, routes, ups, downs, numbers, experts):
+def run_experts(tokens, routes, ups, downs, numbers):
     total = None
+    half = routes.shape[1] // 2
     for up, down, number in zip(ups, downs, numbers):
         inner = down.shape[0]
         full = jnp.dot(tokens, up, preferred_element_type=F32)
         here = lax.dynamic_slice(routes, (0, number), (routes.shape[0], 1)).astype(F32)
-        rest = lax.dynamic_slice(routes, (0, experts + number), (routes.shape[0], 1)).astype(F32)
+        rest = lax.dynamic_slice(routes, (0, half + number), (routes.shape[0], 1)).astype(F32)
         act = jax.nn.silu(full[:, :inner]) * full[:, inner:] * (here + rest)
         term = jnp.dot(act.astype(BF16), down, preferred_element_type=F32)
         total = term if total is None else total + term
@@ -260,70 +330,79 @@
 
 
 def plane_layer(
-    mixed,
+    line,
+    packed,
     out_weight,
     residual,
     post_gain,
-    expert_ids,
-    expert_scores,
     expert_up,
     expert_down,
 ):
-    count = lax.axis_size("rows")
-    line = count // 4
     me = lax.axis_index("rows")
     here = me // 4
-    others = range(1, line)
     tok, full = residual.shape
     exp_dev = expert_up.shape[0]
-    experts = exp_dev * count
-    part = full // line
+    part, half = full // line, full // 2
+    extra = packed[0].shape[1] - half
+    others = range(1, line)
 
     weight_x = swap(out_weight, 2)
+    weight_core = swap(out_weight, 1)
+    packed = list(packed)
+    packed[-1], weight_x = lax.optimization_barrier((packed[-1], weight_x))
+    weights = [out_weight, weight_core, weight_x, swap(weight_x, 1)]
+    expert_up, expert_down, weights[3] = lax.optimization_barrier(
+        (expert_up, expert_down, weights[3])
+    )
     up_mate = swap(expert_up, 1)
     down_mate = swap(expert_down, 1)
-    weights = [out_weight, swap(out_weight, 1), weight_x, swap(weight_x, 1)]
-    projection = jnp.zeros((out_weight.shape[0], part), BF16)
-    for mask, piece in enumerate(weights):
-        projection = lax.dynamic_update_slice(
-            projection, piece, (0, ((me % 4) ^ mask) * piece.shape[1])
+
+    got = [packed[0]] + [swap(packed[m], 4 * m) for m in others]
+    heads_in = [jnp.concatenate([g[:tok, :half], g[tok:, :half]], axis=1) for g in got]
+    heads_in = jnp.concatenate(heads_in, axis=0)
+    base = [
+        jnp.concatenate([g[:tok, half:], g[tok:, half : half + part - extra]], axis=1) for g in got
+    ]
+    at = half + part - extra
+    routes = jnp.concatenate([g[tok:, at : at + 128] for g in got], axis=0)
+    attention = jnp.zeros((line * tok, part), F32)
+    for mask, weight in enumerate(weights):
+        piece = jnp.dot(heads_in, weight, preferred_element_type=F32)
+        attention = lax.dynamic_update_slice(
+            attention, piece, (0, ((me % 4) ^ mask) * piece.shape[1])
         )
-
-    routes = routing(expert_ids, expert_scores, experts)
-    own_res = [
-        lax.dynamic_slice(residual, (0, (here ^ m) * part), (tok, part)) for m in range(line)
-    ]
-    packed = [jnp.concatenate([mixed, own_res[m], routes], axis=1) for m in range(line)]
-    got = [packed[0]] + [swap(packed[m], 4 * m) for m in others]
-    got = jnp.concatenate(got, axis=0)
-    width = mixed.shape[1]
-    hidden = got[:, width : width + part].astype(F32) + jnp.dot(
-        got[:, :width], projection, preferred_element_type=F32
-    )
-    hidden = hidden.astype(BF16)
-    routes = got[:, width + part :]
-
-    hid = jnp.zeros((line * tok, full), BF16)
+    owner = jnp.arange(line * tok)[:, None] // tok
+    base = jnp.concatenate(base, axis=0).astype(F32)
+    columns = [(attention + jnp.where(owner == m, 0.0, base)).astype(BF16) for m in range(line)]
+
+    hidden = jnp.zeros((line * tok, full), BF16)
     for m in range(line):
-        piece = hidden if m == 0 else swap(hidden, 4 * m)
-        piece = jnp.concatenate([piece[tok * (j ^ m) : tok * (j ^ m) + tok] for j in range(line)], axis=0)
-        hid = lax.dynamic_update_slice(hid, piece, (0, (here ^ m) * part))
-    hid = hid.astype(F32)
-    scale = lax.rsqrt(jnp.mean(hid * hid, axis=1, keepdims=True) + EPS)
-    normed = (hid * scale * post_gain).astype(BF16)
-
-    sent = jnp.concatenate([normed, routes], axis=1)
-    came = swap(sent, 2)
+        piece = columns[m] if m == 0 else swap(columns[m], 4 * m)
+        order = [piece[tok * (j ^ m) : tok * (j ^ m) + tok] for j in range(line)]
+        hidden = lax.dynamic_update_slice(
+            hidden, jnp.concatenate(order, axis=0), (0, (here ^ m) * part)
+        )
+    hidden = hidden.astype(F32)
+    mine = hidden[:tok] + residual.astype(F32)
+    hidden = jnp.concatenate([mine, hidden[tok:]], axis=0)
+    scale = lax.rsqrt(jnp.mean(hidden * hidden, axis=1, keepdims=True) + EPS)
+    normed = (hidden * scale * post_gain).astype(BF16)
+
+    came = swap(jnp.concatenate([normed, routes], axis=1), 2)
     ups = [expert_up[i] for i in range(exp_dev)] + [up_mate[i] for i in range(exp_dev)]
     downs = [expert_down[i] for i in range(exp_dev)] + [down_mate[i] for i in range(exp_dev)]
-    numbers = [me * exp_dev + i for i in range(exp_dev)] + [(me ^ 1) * exp_dev + i for i in range(exp_dev)]
-    own_sum = run_experts(normed, routes, ups, downs, numbers, experts)
-    far_sum = run_experts(came[:, :full], came[:, full:], ups, downs, numbers, experts)
-    back = swap(far_sum.astype(BF16), 2)
-    total = own_sum + back.astype(F32)
-    out = hid[:tok] + total[:tok]
+    numbers = [who * exp_dev + i for who in (me, me ^ 1) for i in range(exp_dev)]
+    own_sum = run_experts(normed, routes, ups, downs, numbers)
+    far_sum = run_experts(came[:, :full], came[:, full:], ups, downs, numbers)
+    total = own_sum + swap(far_sum.astype(BF16), 2).astype(F32)
+    folded = []
+    for m in range(line):
+        rows = total[m * tok : (m + 1) * tok]
+        folded.append(jnp.concatenate([rows[:, :half], rows[:, half:]], axis=0))
+    out = folded[0]
     for m in others:
-        out = out + swap(total[m * tok : (m + 1) * tok].astype(BF16), 4 * m).astype(F32)
+        out = out + swap(folded[m].astype(BF16), 4 * m).astype(F32)
+    out = mine + jnp.concatenate([out[:tok], out[tok:]], axis=1)
     return out.astype(BF16)
 
 
@@ -389,10 +468,16 @@
 
 def per_device(mesh_shape, *args):
     delta_args, layer_args = args[:11], args[11:]
-    mixed, kept_state = delta_rule(*delta_args)
-    short = mesh_shape["heads"] == 1 and mesh_shape["rows"] in (8, 16)
-    layer = plane_layer if short else general_layer
-    return (layer(mixed, *layer_args), kept_state)
+    rows = mesh_shape["rows"]
+    if mesh_shape["heads"] == 1 and rows in (8, 16):
+        line = rows // 4
+        out_weight, residual, post_gain, ids, scores, up, down = layer_args
+        *packed, kept_state = delta_rule(*delta_args, line, residual, ids, scores)
+        layer_out = plane_layer(line, packed, out_weight, residual, post_gain, up, down)
+    else:
+        mixed, kept_state = delta_rule(*delta_args)
+        layer_out = general_layer(mixed, *layer_args)
+    return (layer_out, kept_state)
 
 
 def solution(mesh):

time: 90.3 us -> 68.2 us (0.76)
  local copies, waits for them, and re-layouts: 15.1 us -> 2.65 us
  waiting for transfers between devices: 36.8 us -> 25.9 us
  other arithmetic: 4.04 us -> 2.13 us
  starting transfers between devices: 19.9 us -> 21.4 us
  Pallas kernels: 5.64 us -> 7.09 us
    ppermute x16, waiting for transfers between devices: 36.8 us -> 25.9 us  [swap(): return lax.ppermute(values, 'rows', [(i, i ^ mask) for i in range(count)])]
    unnamed x28 -> x10, local copies, waits for them, and re-layouts: 10.4 us -> 0.03 us
    dynamic_update_slice x4 -> x0, local copies, waits for them, and re-layouts: 2.6 us -> none  [plane_layer(): lax.dynamic_update_slice(projection, piece, (0, (me % 4 ^ mask) * piece.s...]
    slice x5 -> x20, local copies, waits for them, and re-layouts: 0.09 us -> 2.59 us  [the longest x4 0.93 us: plane_layer(): g[:tok, :half]]
    reduce_sum x3 -> x1, other arithmetic: 1.71 us -> 0.18 us  [plane_layer(): scale = lax.rsqrt(jnp.mean(hidden * hidden, axis=1, keepdims=True) + EPS)]
    pallas_call x1, Pallas kernels: 5.64 us -> 7.09 us  [delta_rule(): pl.pallas_call(functools.partial(delta_kernel, drafts, group, line), grid...]
    ppermute x16, starting transfers between devices: 19.9 us -> 21.4 us  [swap(): return lax.ppermute(values, 'rows', [(i, i ^ mask) for i in range(count)])]
    concatenate x4 -> x0, local copies, waits for them, and re-layouts: 1.02 us -> none  [plane_layer(): jnp.concatenate([mixed, own_res[m], routes], axis=1)]
  transfers between devices with their start and end apart: 16 -> 16, of which waited for: 10 -> 9; matrix products, arithmetic and copies ran while one was open for 17% -> 15% of each run, Pallas kernels for 6% -> 10%
where the time goes in v2:
time: 68.2 us; the launch traced here: 67.9 us
  waiting for transfers between devices  25.9 us (38%)
  starting transfers between devices  21.4 us (31%)
  matrix products  7.66 us (11%)
  Pallas kernels  7.09 us (10%)
  local copies, waits for them, and re-layouts  2.65 us (4%)
  other arithmetic  2.13 us (3%)
  between operations  1.05 us (2%)
    ppermute x16, waiting for transfers between devices, swap(): return lax.ppermute(values, 'rows', [(i, i ^ mask) for i in range(count)])  25.9 us
    ppermute x16, starting transfers between devices, swap(): return lax.ppermute(values, 'rows', [(i, i ^ mask) for i in range(count)])  21.4 us
    pallas_call x1, Pallas kernels, delta_rule(): pl.pallas_call(functools.partial(delta_kernel, drafts, group, line), grid...  7.09 us
    dot_general x8, matrix products, run_experts(): full = jnp.dot(tokens, up, preferred_element_type=F32)  3.83 us
    dot_general x8, matrix products, run_experts(): term = jnp.dot(act.astype(BF16), down, preferred_element_type=F32)  2.81 us
  transfers between devices with their start and end apart: 16, of which 9 were waited for; matrix products, arithmetic and copies ran while one was open for 15% of the time, Pallas kernels for 10%

profile of v2, /device:TPU:0, one launch (start us, length us, event | category | flops | bytes accessed | tf_op | source)
XLA Modules:
  0.0 67.9 jit_solution(255335974525401182)
XLA Ops:
  0.6 3.0 %collective-permute-start.2 = (bf16[2048,128]{1,0:T(8,128)(2,1)}, bf16[2048,128]{1,0:T(8,128)(2,1)S(1)}, u32[]{:S(2)}, u32[]{:S(2)}) collective-permute-start(bf16[2048,128]{1,0:T(8,128)(2,1)} %param.29), channel_id=1, source_target_pairs={{0,2},{1,3},{2,0},{3,1},{4,6},{5,7},{6,4},{7,5},{8,10},{9,11},{10,... | collective-permute-start | bytes 1572872 | tf_op jit(solution)/shard_map/ppermute | solution.py:315
  3.6 0.0 collective-permute-start.4
  3.6 7.1 %shard_map.185 = (bf16[40,1408]{1,0:T(8,128)(2,1)}, bf16[40,1408]{1,0:T(8,128)(2,1)}, bf16[40,1408]{1,0:T(8,128)(2,1)}, bf16[40,1408]{1,0:T(8,128)(2,1)}, bf16[5,16,128,128]{3,2,1,0:T(8,128)(2,1)}) custom-call(s32[5]{0:T(128)} %accepted_ref.1, bf16[20,1024]{1,0:T(8,128)(2,1)} %query_ref.1, bf16[20,1024]{1,0:T(8,128)(2,1)} %key_ref.1, ...), custom_call_target="tpu_custom_call" | custom-call | flops 21474836480 | bytes 83886080 | tf_op jit(solution)/shard_map/pallas_call | solution.py:293
  10.7 2.7 %collective-permute-start.1 = (bf16[40,1408]{1,0:T(8,128)(2,1)}, bf16[40,1408]{1,0:T(8,128)(2,1)S(1)}, u32[]{:S(2)}, u32[]{:S(2)}) collective-permute-start(bf16[40,1408]{1,0:T(8,128)(2,1)} %get-tuple-element.14), channel_id=1, source_target_pairs={{0,8},{1,9},{2,10},{3,11},{4,12},{5,13},{6,14},{7,15},{8,0},{9,1},... | collective-permute-start | bytes 337928 | tf_op jit(solution)/shard_map/ppermute | solution.py:315
  13.4 1.6 %collective-permute-start = (bf16[40,1408]{1,0:T(8,128)(2,1)}, bf16[40,1408]{1,0:T(8,128)(2,1)S(1)}, u32[]{:S(2)}, u32[]{:S(2)}) collective-permute-start(bf16[40,1408]{1,0:T(8,128)(2,1)} %get-tuple-element.13), channel_id=1, source_target_pairs={{0,4},{1,5},{2,6},{3,7},{4,0},{5,1},{6,2},{7,3},{8,12},{9,13},{10,... | collective-permute-start | bytes 337928 | tf_op jit(solution)/shard_map/ppermute | solution.py:315
  15.0 0.9 %fusion.103 = (bf16[20,1024]{1,0:T(8,128)(2,1)S(1)}, bf16[20,1024]{1,0:T(8,128)(2,1)S(1)}) fusion(bf16[40,1408]{1,0:T(8,128)(2,1)} %get-tuple-element.12), kind=kLoop, calls=%fused_computation.152 | loop fusion | bytes 163840 | tf_op jit(solution)/shard_map/slice | solution.py:361
  15.9 0.7 %fusion.99 = (bf16[20,128]{1,0:T(8,128)(2,1)S(1)}, bf16[20,128]{1,0:T(8,128)(2,1)S(1)}) fusion(bf16[40,1408]{1,0:T(8,128)(2,1)} %get-tuple-element.12), kind=kLoop, calls=%fused_computation.148 | loop fusion | bytes 20480 | tf_op jit(solution)/shard_map/slice | solution.py:367
  16.6 0.7 %slice.239 = bf16[20,384]{1,0:T(8,128)(2,1)S(1)} slice(bf16[40,1408]{1,0:T(8,128)(2,1)} %get-tuple-element.12), slice={[0:20], [1024:1408]} | slice | bytes 30720 | tf_op jit(solution)/shard_map/slice | solution.py:364
  17.4 2.5 %collective-permute-done.1 = bf16[40,1408]{1,0:T(8,128)(2,1)S(1)} collective-permute-done((bf16[40,1408]{1,0:T(8,128)(2,1)}, bf16[40,1408]{1,0:T(8,128)(2,1)S(1)}, u32[]{:S(2)}, u32[]{:S(2)}) %collective-permute-start.1) | collective-permute-done | bytes 112672 | tf_op jit(solution)/shard_map/ppermute | solution.py:315
  20.0 0.2 collective-permute-done
  20.2 0.0 collective-permute-done.2
  20.2 3.3 %collective-permute-start.3 = (bf16[40,1408]{1,0:T(8,128)(2,1)}, bf16[40,1408]{1,0:T(8,128)(2,1)S(1)}, u32[]{:S(2)}, u32[]{:S(2)}) collective-permute-start(bf16[40,1408]{1,0:T(8,128)(2,1)} %get-tuple-element.16), channel_id=1, source_target_pairs={{0,12},{1,13},{2,14},{3,15},{4,8},{5,9},{6,10},{7,11},{8,4},{9,5},... | collective-permute-start | bytes 337928 | tf_op jit(solution)/shard_map/ppermute | solution.py:315
  23.5 3.6 %collective-permute-done.3 = bf16[40,1408]{1,0:T(8,128)(2,1)S(1)} collective-permute-done((bf16[40,1408]{1,0:T(8,128)(2,1)}, bf16[40,1408]{1,0:T(8,128)(2,1)S(1)}, u32[]{:S(2)}, u32[]{:S(2)}) %collective-permute-start.3) | collective-permute-done | bytes 112672 | tf_op jit(solution)/shard_map/ppermute | solution.py:315
  27.2 0.3 convolution_dynamic-update-slice_fusion.3
  27.5 0.3 add_reduce_fusion.5
  27.8 0.3 convolution_dynamic-update-slice_fusion.2
  28.0 0.0 copy-start.3
  28.0 0.3 convolution_dynamic-update-slice_fusion.1
  28.3 0.0 copy-start
  28.3 0.3 convolution_dynamic-update-slice_fusion
  28.6 0.1 fusion.40
  28.7 2.0 %collective-permute-start.6 = (bf16[80,512]{1,0:T(8,128)(2,1)S(1)}, bf16[80,512]{1,0:T(8,128)(2,1)S(1)}, u32[]{:S(2)}, u32[]{:S(2)}) collective-permute-start(bf16[80,512]{1,0:T(8,128)(2,1)S(1)} %fusion.40), channel_id=1, source_target_pairs={{0,4},{1,5},{2,6},{3,7},{4,0},{5,1},{6,2},{7,3},{8,12},{9,13},{10,... | collective-permute-start | bytes 245768 | tf_op jit(solution)/shard_map/ppermute | solution.py:315
  30.6 0.1 fusion.44
  30.8 2.2 %collective-permute-start.7 = (bf16[80,512]{1,0:T(8,128)(2,1)S(1)}, bf16[80,512]{1,0:T(8,128)(2,1)S(1)}, u32[]{:S(2)}, u32[]{:S(2)}) collective-permute-start(bf16[80,512]{1,0:T(8,128)(2,1)S(1)} %get-tuple-element.39), channel_id=1, source_target_pairs={{0,8},{1,9},{2,10},{3,11},{4,12},{5,13},{6,14},{7,15},{8,0},{9,1},... | collective-permute-start | bytes 245768 | tf_op jit(solution)/shard_map/ppermute | solution.py:315
  32.9 0.4 collective-permute-start.8
  33.3 0.5 collective-permute-start.9
  33.9 0.1 fusion.47
  34.0 0.0 collective-permute-done.6
  34.0 0.0 copy-start.2
  34.0 4.3 %collective-permute-done.7 = bf16[80,512]{1,0:T(8,128)(2,1)S(1)} collective-permute-done((bf16[80,512]{1,0:T(8,128)(2,1)S(1)}, bf16[80,512]{1,0:T(8,128)(2,1)S(1)}, u32[]{:S(2)}, u32[]{:S(2)}) %collective-permute-start.7) | collective-permute-done | bytes 81952 | tf_op jit(solution)/shard_map/ppermute | solution.py:315
  38.3 0.9 %collective-permute-done.8 = bf16[80,512]{1,0:T(8,128)(2,1)S(1)} collective-permute-done((bf16[80,512]{1,0:T(8,128)(2,1)S(1)}, bf16[80,512]{1,0:T(8,128)(2,1)S(1)}, u32[]{:S(2)}, u32[]{:S(2)}) %collective-permute-start.8) | collective-permute-done | bytes 81952 | tf_op jit(solution)/shard_map/ppermute | solution.py:315
  39.4 0.1 slice.322
  39.5 0.2 multiply_reduce_fusion
  39.7 0.1 multiply_convert_fusion
  39.9 0.6 collective-permute-start.11
  40.5 0.5 fusion.10
  41.0 0.5 fusion.6
  41.4 0.4 fusion.24
  41.8 0.4 convolution_add_fusion.3
  42.2 5.3 %collective-permute-done.11 = bf16[80,2176]{1,0:T(8,128)(2,1)S(1)} collective-permute-done((bf16[80,2176]{1,0:T(8,128)(2,1)S(1)}, bf16[80,2176]{1,0:T(8,128)(2,1)S(1)}, u32[]{:S(2)}, u32[]{:S(2)}) %collective-permute-start.11) | collective-permute-done | bytes 348192 | tf_op jit(solution)/shard_map/ppermute | solution.py:315
  47.4 0.2 add_reduce_fusion.1
  47.7 0.5 fusion.8
  48.1 0.3 fusion.22
  48.5 0.5 fusion.4
  49.0 0.3 convolution_add_fusion.1
  49.3 0.0 collective-permute-done.9
  49.3 0.5 fusion.14
  49.8 0.5 fusion.12
  50.3 0.3 fusion.26
  50.7 0.4 fusion.3
  51.0 0.6 collective-permute-start.12
  51.6 0.5 fusion.15
  52.1 0.3 fusion.27
  52.4 0.5 fusion.13
  52.9 5.2 %collective-permute-done.12 = bf16[80,2048]{1,0:T(8,128)(2,1)S(1)} collective-permute-done((bf16[80,2048]{1,0:T(8,128)(2,1)S(1)}, bf16[80,2048]{1,0:T(8,128)(2,1)S(1)}, u32[]{:S(2)}, u32[]{:S(2)}) %collective-permute-start.12) | collective-permute-done | bytes 327712 | tf_op jit(solution)/shard_map/ppermute | solution.py:315
  58.1 0.4 fusion.110
  58.5 0.1 fusion.97
  58.6 2.2 %collective-permute-start.15 = (bf16[40,1024]{1,0:T(8,128)(2,1)S(1)}, bf16[40,1024]{1,0:T(8,128)(2,1)S(1)}, u32[]{:S(2)}, u32[]{:S(2)}) collective-permute-start(bf16[40,1024]{1,0:T(8,128)(2,1)S(1)} %pad_maximum_fusion.3), channel_id=1, source_target_pairs={{0,12},{1,13},{2,14},{3,15},{4,8},{5,9},{6,10},{7,11},{8,4},{9,5},... | collective-permute-start | bytes 245768 | tf_op jit(solution)/shard_map/ppermute | solution.py:315
  60.8 1.1 %collective-permute-start.14 = (bf16[40,1024]{1,0:T(8,128)(2,1)S(1)}, bf16[40,1024]{1,0:T(8,128)(2,1)S(1)}, u32[]{:S(2)}, u32[]{:S(2)}) collective-permute-start(bf16[40,1024]{1,0:T(8,128)(2,1)S(1)} %pad_maximum_fusion.2), channel_id=1, source_target_pairs={{0,8},{1,9},{2,10},{3,11},{4,12},{5,13},{6,14},{7,15},{8,0},{9,1},... | collective-permute-start | bytes 245768 | tf_op jit(solution)/shard_map/ppermute | solution.py:315
  62.0 1.3 %collective-permute-start.13 = (bf16[40,1024]{1,0:T(8,128)(2,1)S(1)}, bf16[40,1024]{1,0:T(8,128)(2,1)S(1)}, u32[]{:S(2)}, u32[]{:S(2)}) collective-permute-start(bf16[40,1024]{1,0:T(8,128)(2,1)S(1)} %pad_maximum_fusion.1), channel_id=1, source_target_pairs={{0,4},{1,5},{2,6},{3,7},{4,0},{5,1},{6,2},{7,3},{8,12},{9,13},{10,... | collective-permute-start | bytes 245768 | tf_op jit(solution)/shard_map/ppermute | solution.py:315
  63.2 1.8 %collective-permute-done.15 = bf16[40,1024]{1,0:T(8,128)(2,1)S(1)} collective-permute-done((bf16[40,1024]{1,0:T(8,128)(2,1)S(1)}, bf16[40,1024]{1,0:T(8,128)(2,1)S(1)}, u32[]{:S(2)}, u32[]{:S(2)}) %collective-permute-start.15) | collective-permute-done | bytes 81952 | tf_op jit(solution)/shard_map/ppermute | solution.py:315
  65.0 2.1 %collective-permute-done.14 = bf16[40,1024]{1,0:T(8,128)(2,1)S(1)} collective-permute-done((bf16[40,1024]{1,0:T(8,128)(2,1)S(1)}, bf16[40,1024]{1,0:T(8,128)(2,1)S(1)}, u32[]{:S(2)}, u32[]{:S(2)}) %collective-permute-start.14) | collective-permute-done | bytes 81952 | tf_op jit(solution)/shard_map/ppermute | solution.py:315
  67.1 0.1 fusion.46
  67.2 0.7 fusion.36
  (44 shorter events, 0.5 us)
Async XLA Ops:
  0.6 19.6 %collective-permute-start.2 = (bf16[2048,128]{1,0:T(8,128)(2,1)}, bf16[2048,128]{1,0:T(8,128)(2,1)S(1)}, u32[]{:S(2)}, u32[]{:S(2)}) collective-permute-start(bf16[2048,128]{1,0:T(8,128)(2,1)} %param.29), channel_id=1, source_target_pairs={{0,2},{1,3},{2,0},{3,1},{4,6},{5,7},{6,4},{7,5},{8,10},{9,11},{10,... | collective-permute-start | bytes 1572872 | tf_op jit(solution)/shard_map/ppermute | solution.py:315
  3.6 24.1 %collective-permute-start.4 = (bf16[2048,128]{1,0:T(8,128)(2,1)}, bf16[2048,128]{1,0:T(8,128)(2,1)S(1)}, u32[]{:S(2)}, u32[]{:S(2)}) collective-permute-start(bf16[2048,128]{1,0:T(8,128)(2,1)} %param.29), channel_id=1, source_target_pairs={{0,1},{1,0},{2,3},{3,2},{4,5},{5,4},{6,7},{7,6},{8,9},{9,8},{10,11... | collective-permute-start | bytes 1572872 | tf_op jit(solution)/shard_map/ppermute | solution.py:315
  3.6 23.6 %copy-start.4 = (bf16[2048,128]{1,0:T(8,128)(2,1)S(1)}, bf16[2048,128]{1,0:T(8,128)(2,1)}, u32[]{:S(2)}) copy-start(bf16[2048,128]{1,0:T(8,128)(2,1)} %param.29) | copy-start | bytes 1572868
  10.7 9.2 %collective-permute-start.1 = (bf16[40,1408]{1,0:T(8,128)(2,1)}, bf16[40,1408]{1,0:T(8,128)(2,1)S(1)}, u32[]{:S(2)}, u32[]{:S(2)}) collective-permute-start(bf16[40,1408]{1,0:T(8,128)(2,1)} %get-tuple-element.14), channel_id=1, source_target_pairs={{0,8},{1,9},{2,10},{3,11},{4,12},{5,13},{6,14},{7,15},{8,0},{9,1},... | collective-permute-start | bytes 337928 | tf_op jit(solution)/shard_map/ppermute | solution.py:315
  13.4 6.7 %collective-permute-start = (bf16[40,1408]{1,0:T(8,128)(2,1)}, bf16[40,1408]{1,0:T(8,128)(2,1)S(1)}, u32[]{:S(2)}, u32[]{:S(2)}) collective-permute-start(bf16[40,1408]{1,0:T(8,128)(2,1)} %get-tuple-element.13), channel_id=1, source_target_pairs={{0,4},{1,5},{2,6},{3,7},{4,0},{5,1},{6,2},{7,3},{8,12},{9,13},{10,... | collective-permute-start | bytes 337928 | tf_op jit(solution)/shard_map/ppermute | solution.py:315
  20.2 7.0 %collective-permute-start.3 = (bf16[40,1408]{1,0:T(8,128)(2,1)}, bf16[40,1408]{1,0:T(8,128)(2,1)S(1)}, u32[]{:S(2)}, u32[]{:S(2)}) collective-permute-start(bf16[40,1408]{1,0:T(8,128)(2,1)} %get-tuple-element.16), channel_id=1, source_target_pairs={{0,12},{1,13},{2,14},{3,15},{4,8},{5,9},{6,10},{7,11},{8,4},{9,5},... | collective-permute-start | bytes 337928 | tf_op jit(solution)/shard_map/ppermute | solution.py:315
  23.5 4.8 %collective-permute-start.5 = (bf16[2048,128]{1,0:T(8,128)(2,1)S(1)}, bf16[2048,128]{1,0:T(8,128)(2,1)S(1)}, u32[]{:S(2)}, u32[]{:S(2)}) collective-permute-start(bf16[2048,128]{1,0:T(8,128)(2,1)S(1)} %collective-permute-done.2), channel_id=1, source_target_pairs={{0,1},{1,0},{2,3},{3,2},{4,5},{5,4},{6,7},{7,6},{8,9},{9,8},{10,11... | collective-permute-start | bytes 1572872 | tf_op jit(solution)/shard_map/ppermute | solution.py:315
  28.0 5.3 %copy-start.3 = (bf16[2,2048,512]{2,1,0:T(8,128)(2,1)S(1)}, bf16[2,2048,512]{2,1,0:T(8,128)(2,1)}, u32[]{:S(2)}) copy-start(bf16[2,2048,512]{2,1,0:T(8,128)(2,1)} %param.34) | copy-start | bytes 12582916
  28.3 5.0 %copy-start = (bf16[2,256,2048]{2,1,0:T(8,128)(2,1)S(1)}, bf16[2,256,2048]{2,1,0:T(8,128)(2,1)}, u32[]{:S(2)}) copy-start(bf16[2,256,2048]{2,1,0:T(8,128)(2,1)} %param.35) | copy-start | bytes 6291460
  28.7 5.3 %collective-permute-start.6 = (bf16[80,512]{1,0:T(8,128)(2,1)S(1)}, bf16[80,512]{1,0:T(8,128)(2,1)S(1)}, u32[]{:S(2)}, u32[]{:S(2)}) collective-permute-start(bf16[80,512]{1,0:T(8,128)(2,1)S(1)} %fusion.40), channel_id=1, source_target_pairs={{0,4},{1,5},{2,6},{3,7},{4,0},{5,1},{6,2},{7,3},{8,12},{9,13},{10,... | collective-permute-start | bytes 245768 | tf_op jit(solution)/shard_map/ppermute | solution.py:315
  30.6 8.8 %copy-start.1 = (bf16[20,2048]{1,0:T(8,128)(2,1)S(1)}, bf16[20,2048]{1,0:T(8,128)(2,1)}, u32[]{:S(2)}) copy-start(bf16[20,2048]{1,0:T(8,128)(2,1)} %refs_0_.1) | copy-start | bytes 245764
  30.8 7.6 %collective-permute-start.7 = (bf16[80,512]{1,0:T(8,128)(2,1)S(1)}, bf16[80,512]{1,0:T(8,128)(2,1)S(1)}, u32[]{:S(2)}, u32[]{:S(2)}) collective-permute-start(bf16[80,512]{1,0:T(8,128)(2,1)S(1)} %get-tuple-element.39), channel_id=1, source_target_pairs={{0,8},{1,9},{2,10},{3,11},{4,12},{5,13},{6,14},{7,15},{8,0},{9,1},... | collective-permute-start | bytes 245768 | tf_op jit(solution)/shard_map/ppermute | solution.py:315
  32.9 6.3 %collective-permute-start.8 = (bf16[80,512]{1,0:T(8,128)(2,1)S(1)}, bf16[80,512]{1,0:T(8,128)(2,1)S(1)}, u32[]{:S(2)}, u32[]{:S(2)}) collective-permute-start(bf16[80,512]{1,0:T(8,128)(2,1)S(1)} %get-tuple-element.38), channel_id=1, source_target_pairs={{0,12},{1,13},{2,14},{3,15},{4,8},{5,9},{6,10},{7,11},{8,4},{9,5},... | collective-permute-start | bytes 245768 | tf_op jit(solution)/shard_map/ppermute | solution.py:315
  33.3 17.0 %collective-permute-start.10 = (bf16[2,256,2048]{2,1,0:T(8,128)(2,1)S(1)}, bf16[2,256,2048]{2,1,0:T(8,128)(2,1)S(1)}, u32[]{:S(2)}, u32[]{:S(2)}) collective-permute-start(bf16[2,256,2048]{2,1,0:T(8,128)(2,1)S(1)} %copy-done), channel_id=1, source_target_pairs={{0,1},{1,0},{2,3},{3,2},{4,5},{5,4},{6,7},{7,6},{8,9},{9,8},{10,11... | collective-permute-start | bytes 6291464 | tf_op jit(solution)/shard_map/ppermute | solution.py:315
  33.3 16.0 %collective-permute-start.9 = (bf16[2,2048,512]{2,1,0:T(8,128)(2,1)S(1)}, bf16[2,2048,512]{2,1,0:T(8,128)(2,1)S(1)}, u32[]{:S(2)}, u32[]{:S(2)}) collective-permute-start(bf16[2,2048,512]{2,1,0:T(8,128)(2,1)S(1)} %copy-done.3), channel_id=1, source_target_pairs={{0,1},{1,0},{2,3},{3,2},{4,5},{5,4},{6,7},{7,6},{8,9},{9,8},{10,11... | collective-permute-start | bytes 12582920 | tf_op jit(solution)/shard_map/ppermute | solution.py:315
  34.0 5.7 %copy-start.2 = (f32[2048]{0:T(1024)S(1)}, f32[2048]{0:T(1024)}, u32[]{:S(2)}) copy-start(f32[2048]{0:T(1024)} %param.31) | copy-start | bytes 24580
  39.9 7.5 %collective-permute-start.11 = (bf16[80,2176]{1,0:T(8,128)(2,1)S(1)}, bf16[80,2176]{1,0:T(8,128)(2,1)S(1)}, u32[]{:S(2)}, u32[]{:S(2)}) collective-permute-start(bf16[80,2176]{1,0:T(8,128)(2,1)S(1)} %maximum_maximum_fusion), channel_id=1, source_target_pairs={{0,2},{1,3},{2,0},{3,1},{4,6},{5,7},{6,4},{7,5},{8,10},{9,11},{10,... | collective-permute-start | bytes 1044488 | tf_op jit(solution)/shard_map/ppermute | solution.py:315
  51.0 7.1 %collective-permute-start.12 = (bf16[80,2048]{1,0:T(8,128)(2,1)S(1)}, bf16[80,2048]{1,0:T(8,128)(2,1)S(1)}, u32[]{:S(2)}, u32[]{:S(2)}) collective-permute-start(bf16[80,2048]{1,0:T(8,128)(2,1)S(1)} %fusion.3), channel_id=1, source_target_pairs={{0,2},{1,3},{2,0},{3,1},{4,6},{5,7},{6,4},{7,5},{8,10},{9,11},{10,... | collective-permute-start | bytes 983048 | tf_op jit(solution)/shard_map/ppermute | solution.py:315
  58.6 6.4 %collective-permute-start.15 = (bf16[40,1024]{1,0:T(8,128)(2,1)S(1)}, bf16[40,1024]{1,0:T(8,128)(2,1)S(1)}, u32[]{:S(2)}, u32[]{:S(2)}) collective-permute-start(bf16[40,1024]{1,0:T(8,128)(2,1)S(1)} %pad_maximum_fusion.3), channel_id=1, source_target_pairs={{0,12},{1,13},{2,14},{3,15},{4,8},{5,9},{6,10},{7,11},{8,4},{9,5},... | collective-permute-start | bytes 245768 | tf_op jit(solution)/shard_map/ppermute | solution.py:315
  60.8 6.3 %collective-permute-start.14 = (bf16[40,1024]{1,0:T(8,128)(2,1)S(1)}, bf16[40,1024]{1,0:T(8,128)(2,1)S(1)}, u32[]{:S(2)}, u32[]{:S(2)}) collective-permute-start(bf16[40,1024]{1,0:T(8,128)(2,1)S(1)} %pad_maximum_fusion.2), channel_id=1, source_target_pairs={{0,8},{1,9},{2,10},{3,11},{4,12},{5,13},{6,14},{7,15},{8,0},{9,1},... | collective-permute-start | bytes 245768 | tf_op jit(solution)/shard_map/ppermute | solution.py:315
  62.0 5.2 %collective-permute-start.13 = (bf16[40,1024]{1,0:T(8,128)(2,1)S(1)}, bf16[40,1024]{1,0:T(8,128)(2,1)S(1)}, u32[]{:S(2)}, u32[]{:S(2)}) collective-permute-start(bf16[40,1024]{1,0:T(8,128)(2,1)S(1)} %pad_maximum_fusion.1), channel_id=1, source_target_pairs={{0,4},{1,5},{2,6},{3,7},{4,0},{5,1},{6,2},{7,3},{8,12},{9,13},{10,... | collective-permute-start | bytes 245768 | tf_op jit(solution)/shard_map/ppermute | solution.py:315

commit v3 on v2

--- a/solution.py
+++ b/solution.py
@@ -36,9 +36,9 @@
     if line:
         residual_ref, ids_ref, scores_ref = refs[:3]
         packed_refs, refs = refs[3 : 3 + line], refs[3 + line :]
-        kept_ref, coef, unit, vals, mixed_ref, pack = refs
+        written_ref, coef, unit, vals, mixed_ref, pack = refs
     else:
-        mixed_ref, kept_ref, coef, unit, vals = refs
+        mixed_ref, written_ref, coef, unit, vals = refs
     step = pl.program_id(0)
     tok = query_ref.shape[0]
     pad = unit.shape[1] // 2
@@ -112,8 +112,6 @@
     lane = lax.broadcasted_iota(jnp.int32, (pad, coef.shape[1]), 1)
     row = lax.broadcasted_iota(jnp.int32, (2 * pad, width), 0)
     request = row % pad // drafts
-    row3 = lax.broadcasted_iota(jnp.int32, (3 * pad, width), 0)
-    request3 = row3 % pad // drafts
     for i in range(group):
         cols = slice(i * width, (i + 1) * width)
         for slot, ref, factor in ((0, query_ref, width ** (-0.5)), (1, key_ref, 1.0)):
@@ -146,8 +144,6 @@
         shifted = [shift(key, o) for o in range(drafts)]
         query_key = [jnp.sum(query * s, axis=1, keepdims=True) for s in shifted]
         key_key = [jnp.sum(key * s, axis=1, keepdims=True) for s in shifted]
-        written = []
-        keeps = []
         for j in range(repeat):
             head = (step * group + i) * repeat + j
             vcols = slice((repeat * i + j) * vwidth, (repeat * i + j + 1) * vwidth)
@@ -177,28 +173,7 @@
                 mixed_ref[0:tok, pl.ds(to, vwidth)] = mixed
             else:
                 mixed_ref[:, vcols] = mixed.astype(BF16)
-            written.append(column(1 + drafts) * delta)
-            keeps.append(jnp.broadcast_to(column(2 + drafts), (pad, vwidth)))
-        written = jnp.concatenate(written, axis=1)
-        whigh = written.astype(BF16).astype(F32)
-        wlow = written - whigh
-        wrote = jnp.concatenate([whigh, wlow, whigh], axis=0).astype(BF16)
-        kcat = jnp.concatenate([high[pad:], high[pad:], low[pad:]], axis=0)
-        kspread = jnp.concatenate(
-            [jnp.where(request3 == r, kcat, 0.0).astype(BF16) for r in range(reqs)], axis=1
-        )
-        update = lax.dot_general(
-            kspread, wrote, (((0,), (0,)), ((), ())), preferred_element_type=F32
-        )
-        for r in range(reqs):
-            for j in range(repeat):
-                keep = keeps[j][r * drafts : r * drafts + 1, :]
-                kept_ref[r, repeat * i + j] = (
-                    keep * state_ref[r, repeat * i + j].astype(F32)
-                    + update[r * width : (r + 1) * width, j * vwidth : (j + 1) * vwidth]
-                ).astype(BF16)
-
-
+            written_ref[:, vcols] = column(1 + drafts) * delta
     if not line:
         return
 
@@ -216,6 +191,48 @@
             pack[0:tok, half : half + extra] = piece[:, 0:extra]
             pack[tok : 2 * tok, half : half + part - extra] = piece[:, extra:part]
             packed_refs[m][...] = pack[...].astype(BF16)
+
+
+def kept_kernel(
+    drafts, group, key_ref, written_ref, coef_ref, state_ref, kept_ref, unit
+):
+    step = pl.program_id(0)
+    tok = key_ref.shape[0]
+    pad = written_ref.shape[0]
+    reqs, _, width, vwidth = state_ref.shape
+    repeat = state_ref.shape[1] // group
+    heads = pl.num_programs(0) * group * repeat
+
+    @pl.when(step == 0)
+    def _():
+        unit[...] = jnp.zeros_like(unit)
+
+    lane = lax.broadcasted_iota(jnp.int32, (pad, coef_ref.shape[1]), 1)
+    request = lax.broadcasted_iota(jnp.int32, (3 * pad, width), 0) % pad // drafts
+    for i in range(group):
+        raw = key_ref[:, i * width : (i + 1) * width].astype(F32)
+        unit[i, 0:tok, :] = raw * lax.rsqrt(jnp.sum(raw * raw, axis=1, keepdims=True) + EPS)
+        key = unit[i]
+        high = key.astype(BF16).astype(F32)
+        key = jnp.concatenate([high, high, key - high], axis=0)
+        spread = jnp.concatenate(
+            [jnp.where(request == r, key, 0.0).astype(BF16) for r in range(reqs)], axis=1
+        )
+        written = written_ref[:, i * repeat * vwidth : (i + 1) * repeat * vwidth]
+        high = written.astype(BF16).astype(F32)
+        wrote = jnp.concatenate([high, written - high, high], axis=0).astype(BF16)
+        update = lax.dot_general(
+            spread, wrote, (((0,), (0,)), ((), ())), preferred_element_type=F32
+        )
+        for j in range(repeat):
+            head = (step * group + i) * repeat + j
+            mine = jnp.where(lane == (2 + drafts) * heads + head, coef_ref[0:pad], 0.0)
+            keep = jnp.broadcast_to(jnp.sum(mine, axis=1, keepdims=True), (pad, vwidth))
+            for r in range(reqs):
+                kept_ref[r, repeat * i + j] = (
+                    keep[r * drafts : r * drafts + 1, :] * state_ref[r, repeat * i + j].astype(F32)
+                    + update[r * width : (r + 1) * width, j * vwidth : (j + 1) * vwidth]
+                ).astype(BF16)
 
 
 def delta_rule(
@@ -240,7 +257,7 @@
     drafts = tok // reqs
     query_heads = query_in.shape[1] // width
     repeat = heads // query_heads
-    group = 2 if query_heads % 2 == 0 else 1
+    group = 4 if query_heads % 4 == 0 else 1
     pad = round_up(tok, 8)
     whole = lambda *shape: pl.BlockSpec(shape, lambda g: (0,) * len(shape))
     qblock = pl.BlockSpec((tok, group * width), lambda g: (0, g))
@@ -273,37 +290,55 @@
         prior_state,
     ]
     scratch = [
-        pltpu.VMEM((128, 128), F32),
         pltpu.VMEM((group, 2 * pad, width), F32),
         pltpu.VMEM((repeat, pad, vwidth), F32),
     ]
-    kept = jax.ShapeDtypeStruct(prior_state.shape, BF16)
     full = heads * vwidth
+    out_specs = [pl.BlockSpec((pad, group * repeat * vwidth), lambda g: (0, g)), whole(128, 128)]
+    out_shape = [jax.ShapeDtypeStruct((pad, full), F32), jax.ShapeDtypeStruct((128, 128), F32)]
     if line:
         packed = packed_shape(tok, full, line)
-        out_specs = [whole(*packed)] * line + [sblock]
-        out_shape = [jax.ShapeDtypeStruct(packed, BF16)] * line + [kept]
+        out_specs = [whole(*packed)] * line + out_specs
+        out_shape = [jax.ShapeDtypeStruct(packed, BF16)] * line + out_shape
         scratch += [pltpu.VMEM((pad, full), F32), pltpu.VMEM(packed, F32)]
         top = expert_ids.shape[1]
         in_specs += [whole(tok, full), whole(top, tok), whole(top, tok)]
         args += [residual, expert_ids.T, expert_scores.T]
     else:
-        out_specs = [vblock, sblock]
-        out_shape = [jax.ShapeDtypeStruct((tok, full), BF16), kept]
-    return pl.pallas_call(
+        out_specs = [vblock] + out_specs
+        out_shape = [jax.ShapeDtypeStruct((tok, full), BF16)] + out_shape
+    cells = heads * reqs * width * vwidth
+    grid = (query_heads // group,)
+    *mixed, written, coef = pl.pallas_call(
         functools.partial(delta_kernel, drafts, group, line),
-        grid=(query_heads // group,),
+        grid=grid,
         in_specs=in_specs,
         out_specs=out_specs,
         out_shape=out_shape,
         scratch_shapes=scratch,
         compiler_params=pltpu.CompilerParams(vmem_limit_bytes=56 * 1024 * 1024),
         cost_estimate=pl.CostEstimate(
-            flops=1024 * heads * reqs * width * vwidth * 16,
-            bytes_accessed=64 * heads * reqs * width * vwidth,
-            transcendentals=0,
+            flops=8192 * cells, bytes_accessed=64 * cells, transcendentals=0
         ),
     )(*args)
+    kept = pl.pallas_call(
+        functools.partial(kept_kernel, drafts, group),
+        grid=grid,
+        in_specs=[
+            qblock,
+            pl.BlockSpec((pad, group * repeat * vwidth), lambda g: (0, g)),
+            whole(128, 128),
+            sblock,
+        ],
+        out_specs=sblock,
+        out_shape=jax.ShapeDtypeStruct(prior_state.shape, BF16),
+        scratch_shapes=[pltpu.VMEM((group, pad, width), F32)],
+        compiler_params=pltpu.CompilerParams(vmem_limit_bytes=56 * 1024 * 1024),
+        cost_estimate=pl.CostEstimate(
+            flops=8192 * cells, bytes_accessed=64 * cells, transcendentals=0
+        ),
+    )(key_in, written, coef, prior_state)
+    return (*mixed, kept)
 
 
 def packed_shape(tok, full, line):
@@ -348,16 +383,15 @@
 
     weight_x = swap(out_weight, 2)
     weight_core = swap(out_weight, 1)
-    packed = list(packed)
-    packed[-1], weight_x = lax.optimization_barrier((packed[-1], weight_x))
+
+    got = [packed[0]] + [swap(packed[m], 4 * m) for m in others]
+    got[1], weight_x = lax.optimization_barrier((got[1], weight_x))
     weights = [out_weight, weight_core, weight_x, swap(weight_x, 1)]
     expert_up, expert_down, weights[3] = lax.optimization_barrier(
         (expert_up, expert_down, weights[3])
     )
     up_mate = swap(expert_up, 1)
     down_mate = swap(expert_down, 1)
-
-    got = [packed[0]] + [swap(packed[m], 4 * m) for m in others]
     heads_in = [jnp.concatenate([g[:tok, :half], g[tok:, :half]], axis=1) for g in got]
     heads_in = jnp.concatenate(heads_in, axis=0)
     base = [

time: 68.2 us -> 65.4 us (0.959)
  waiting for transfers between devices: 25.9 us -> 23.6 us
  starting transfers between devices: 21.4 us -> 19.6 us
  Pallas kernels: 7.09 us -> 8.29 us
    pallas_call x0 -> x1, Pallas kernels: none -> 4.26 us  [delta_rule(): pl.pallas_call(functools.partial(kept_kernel, drafts, group), grid=grid,...]
    pallas_call x1, Pallas kernels: 7.09 us -> 4.03 us  [delta_rule(): pl.pallas_call(functools.partial(delta_kernel, drafts, group, line), grid...]
    ppermute x16, waiting for transfers between devices: 25.9 us -> 23.6 us  [swap(): return lax.ppermute(values, 'rows', [(i, i ^ mask) for i in range(count)])]
    ppermute x16, starting transfers between devices: 21.4 us -> 19.6 us  [swap(): return lax.ppermute(values, 'rows', [(i, i ^ mask) for i in range(count)])]
  transfers between devices with their start and end apart: 16 -> 16, of which waited for: 9 -> 9; matrix products, arithmetic and copies ran while one was open for 15% -> 16% of each run, Pallas kernels for 10% -> 13%
where the time goes in v3:
time: 65.4 us; the launch traced here: 65.1 us
  waiting for transfers between devices  23.6 us (36%)
  starting transfers between devices  19.6 us (30%)
  Pallas kernels  8.29 us (13%)
  matrix products  7.65 us (12%)
  local copies, waits for them, and re-layouts  2.66 us (4%)
  other arithmetic  2.13 us (3%)
  between operations  1.08 us (2%)
    ppermute x16, waiting for transfers between devices, swap(): return lax.ppermute(values, 'rows', [(i, i ^ mask) for i in range(count)])  23.6 us
    ppermute x16, starting transfers between devices, swap(): return lax.ppermute(values, 'rows', [(i, i ^ mask) for i in range(count)])  19.6 us
    pallas_call x1, Pallas kernels, delta_rule(): pl.pallas_call(functools.partial(kept_kernel, drafts, group), grid=grid,...  4.26 us
    pallas_call x1, Pallas kernels, delta_rule(): pl.pallas_call(functools.partial(delta_kernel, drafts, group, line), grid...  4.03 us
    dot_general x8, matrix products, run_experts(): full = jnp.dot(tokens, up, preferred_element_type=F32)  3.83 us
    dot_general x8, matrix products, run_experts(): term = jnp.dot(act.astype(BF16), down, preferred_element_type=F32)  2.8 us
  transfers between devices with their start and end apart: 16, of which 9 were waited for; matrix products, arithmetic and copies ran while one was open for 16% of the time, Pallas kernels for 13%

profile of v3, /device:TPU:0, one launch (start us, length us, event | category | flops | bytes accessed | tf_op | source)
XLA Modules:
  0.0 65.1 jit_solution(5786204649057190075)
XLA Ops:
  0.6 3.0 %collective-permute-start.1 = (bf16[2048,128]{1,0:T(8,128)(2,1)}, bf16[2048,128]{1,0:T(8,128)(2,1)S(1)}, u32[]{:S(2)}, u32[]{:S(2)}) collective-permute-start(bf16[2048,128]{1,0:T(8,128)(2,1)} %param.29), channel_id=1, source_target_pairs={{0,2},{1,3},{2,0},{3,1},{4,6},{5,7},{6,4},{7,5},{8,10},{9,11},{10,... | collective-permute-start | bytes 1572872 | tf_op jit(solution)/shard_map/ppermute | solution.py:350
  3.6 4.0 %shard_map.185 = (bf16[40,1408]{1,0:T(8,128)(2,1)}, bf16[40,1408]{1,0:T(8,128)(2,1)}, bf16[40,1408]{1,0:T(8,128)(2,1)}, bf16[40,1408]{1,0:T(8,128)(2,1)}, f32[24,2048]{1,0:T(8,128)}, /*index=5*/f32[128,128]{1,0:T(8,128)}) custom-call(s32[5]{0:T(128)} %accepted_ref.1, bf16[20,1024]{1,0:T(8,128)(2,1)} %query_ref.1, bf16[20,1024]{1,0:T(8,128)(2,1)} %key_ref.3, ...), custom_call_target="tpu_custom_call" | custom-call | flops 10737418240 | bytes 83886080 | tf_op jit(solution)/shard_map/pallas_call | solution.py:312
  7.7 3.7 %collective-permute-start.3 = (bf16[40,1408]{1,0:T(8,128)(2,1)}, bf16[40,1408]{1,0:T(8,128)(2,1)S(1)}, u32[]{:S(2)}, u32[]{:S(2)}) collective-permute-start(bf16[40,1408]{1,0:T(8,128)(2,1)} %get-tuple-element.17), channel_id=1, source_target_pairs={{0,12},{1,13},{2,14},{3,15},{4,8},{5,9},{6,10},{7,11},{8,4},{9,5},... | collective-permute-start | bytes 337928 | tf_op jit(solution)/shard_map/ppermute | solution.py:350
  11.3 0.8 %collective-permute-start = (bf16[40,1408]{1,0:T(8,128)(2,1)}, bf16[40,1408]{1,0:T(8,128)(2,1)S(1)}, u32[]{:S(2)}, u32[]{:S(2)}) collective-permute-start(bf16[40,1408]{1,0:T(8,128)(2,1)} %get-tuple-element.14), channel_id=1, source_target_pairs={{0,4},{1,5},{2,6},{3,7},{4,0},{5,1},{6,2},{7,3},{8,12},{9,13},{10,... | collective-permute-start | bytes 337928 | tf_op jit(solution)/shard_map/ppermute | solution.py:350
  12.2 0.9 %fusion.103 = (bf16[20,1024]{1,0:T(8,128)(2,1)S(1)}, bf16[20,1024]{1,0:T(8,128)(2,1)S(1)}) fusion(bf16[40,1408]{1,0:T(8,128)(2,1)} %get-tuple-element.13), kind=kLoop, calls=%fused_computation.152 | loop fusion | bytes 163840 | tf_op jit(solution)/shard_map/slice | solution.py:395
  13.0 0.7 %fusion.99 = (bf16[20,128]{1,0:T(8,128)(2,1)S(1)}, bf16[20,128]{1,0:T(8,128)(2,1)S(1)}) fusion(bf16[40,1408]{1,0:T(8,128)(2,1)} %get-tuple-element.13), kind=kLoop, calls=%fused_computation.148 | loop fusion | bytes 20480 | tf_op jit(solution)/shard_map/slice | solution.py:401
  13.8 0.7 %slice.239 = bf16[20,384]{1,0:T(8,128)(2,1)S(1)} slice(bf16[40,1408]{1,0:T(8,128)(2,1)} %get-tuple-element.13), slice={[0:20], [1024:1408]} | slice | bytes 30720 | tf_op jit(solution)/shard_map/slice | solution.py:398
  14.6 0.0 copy-start.4
  14.6 4.3 %shard_map.186 = bf16[5,16,128,128]{3,2,1,0:T(8,128)(2,1)} custom-call(bf16[20,1024]{1,0:T(8,128)(2,1)} %key_ref.3, f32[24,2048]{1,0:T(8,128)} %get-tuple-element.22.written_ref, f32[128,128]{1,0:T(8,128)} %get-tuple-element.23.coef_ref, bf16[5,16,128,128]{3,2,1,0:T(8,128)(2,1)} %state_ref.3), custom_call_target="tpu_custom_call" | custom-call | flops 10737418240 | bytes 83886080 | tf_op jit(solution)/shard_map/pallas_call | solution.py:324
  18.8 0.0 collective-permute-done.3
  18.9 2.8 %collective-permute-done.2 = bf16[40,1408]{1,0:T(8,128)(2,1)S(1)} collective-permute-done((bf16[40,1408]{1,0:T(8,128)(2,1)}, bf16[40,1408]{1,0:T(8,128)(2,1)S(1)}, u32[]{:S(2)}, u32[]{:S(2)}) %collective-permute-start.2) | collective-permute-done | bytes 112672 | tf_op jit(solution)/shard_map/ppermute | solution.py:350
  21.8 0.0 collective-permute-done
  21.8 0.1 collective-permute-start.5
  21.9 0.3 convolution_dynamic-update-slice_fusion.3
  22.2 0.3 add_reduce_fusion.5
  22.5 0.3 convolution_dynamic-update-slice_fusion.2
  22.7 0.0 copy-start.3
  22.8 0.3 convolution_dynamic-update-slice_fusion.1
  23.0 0.0 copy-start
  23.0 0.7 %collective-permute-done.5 = bf16[2048,128]{1,0:T(8,128)(2,1)S(1)} collective-permute-done((bf16[2048,128]{1,0:T(8,128)(2,1)S(1)}, bf16[2048,128]{1,0:T(8,128)(2,1)S(1)}, u32[]{:S(2)}, u32[]{:S(2)}) %collective-permute-start.5) | collective-permute-done | bytes 524320 | tf_op jit(solution)/shard_map/ppermute | solution.py:350
  23.8 0.2 convolution_dynamic-update-slice_fusion
  24.0 0.1 fusion.40
  24.1 0.3 collective-permute-start.6
  24.4 0.1 fusion.44
  24.5 2.9 %collective-permute-start.7 = (bf16[80,512]{1,0:T(8,128)(2,1)S(1)}, bf16[80,512]{1,0:T(8,128)(2,1)S(1)}, u32[]{:S(2)}, u32[]{:S(2)}) collective-permute-start(bf16[80,512]{1,0:T(8,128)(2,1)S(1)} %get-tuple-element.41), channel_id=1, source_target_pairs={{0,8},{1,9},{2,10},{3,11},{4,12},{5,13},{6,14},{7,15},{8,0},{9,1},... | collective-permute-start | bytes 245768 | tf_op jit(solution)/shard_map/ppermute | solution.py:350
  27.4 1.3 %collective-permute-start.8 = (bf16[80,512]{1,0:T(8,128)(2,1)S(1)}, bf16[80,512]{1,0:T(8,128)(2,1)S(1)}, u32[]{:S(2)}, u32[]{:S(2)}) collective-permute-start(bf16[80,512]{1,0:T(8,128)(2,1)S(1)} %get-tuple-element.40), channel_id=1, source_target_pairs={{0,12},{1,13},{2,14},{3,15},{4,8},{5,9},{6,10},{7,11},{8,4},{9,5},... | collective-permute-start | bytes 245768 | tf_op jit(solution)/shard_map/ppermute | solution.py:350
  28.8 0.5 collective-permute-start.9
  29.3 0.1 fusion.47
  29.4 0.5 collective-permute-done.6
  29.9 0.0 copy-start.2
  29.9 4.2 %collective-permute-done.7 = bf16[80,512]{1,0:T(8,128)(2,1)S(1)} collective-permute-done((bf16[80,512]{1,0:T(8,128)(2,1)S(1)}, bf16[80,512]{1,0:T(8,128)(2,1)S(1)}, u32[]{:S(2)}, u32[]{:S(2)}) %collective-permute-start.7) | collective-permute-done | bytes 81952 | tf_op jit(solution)/shard_map/ppermute | solution.py:350
  34.2 0.1 slice.318
  34.3 0.2 multiply_reduce_fusion
  34.5 0.1 multiply_convert_fusion
  34.7 0.6 collective-permute-start.11
  35.3 0.5 fusion.10
  35.8 0.5 fusion.6
  36.3 0.4 fusion.24
  36.6 0.4 convolution_add_fusion.3
  37.0 5.8 %collective-permute-done.11 = bf16[80,2176]{1,0:T(8,128)(2,1)S(1)} collective-permute-done((bf16[80,2176]{1,0:T(8,128)(2,1)S(1)}, bf16[80,2176]{1,0:T(8,128)(2,1)S(1)}, u32[]{:S(2)}, u32[]{:S(2)}) %collective-permute-start.11) | collective-permute-done | bytes 348192 | tf_op jit(solution)/shard_map/ppermute | solution.py:350
  42.8 0.2 add_reduce_fusion.1
  43.1 0.5 fusion.8
  43.5 0.3 fusion.22
  43.9 0.5 fusion.4
  44.4 0.3 convolution_add_fusion.1
  44.7 0.5 fusion.14
  45.2 0.5 fusion.12
  45.7 0.3 fusion.26
  46.1 0.4 fusion.3
  46.4 0.6 collective-permute-start.12
  47.0 0.5 fusion.15
  47.5 0.3 fusion.27
  47.8 0.5 fusion.13
  48.3 5.2 %collective-permute-done.12 = bf16[80,2048]{1,0:T(8,128)(2,1)S(1)} collective-permute-done((bf16[80,2048]{1,0:T(8,128)(2,1)S(1)}, bf16[80,2048]{1,0:T(8,128)(2,1)S(1)}, u32[]{:S(2)}, u32[]{:S(2)}) %collective-permute-start.12) | collective-permute-done | bytes 327712 | tf_op jit(solution)/shard_map/ppermute | solution.py:350
  53.5 0.4 fusion.110
  53.9 0.1 fusion.97
  54.0 2.2 %collective-permute-start.15 = (bf16[40,1024]{1,0:T(8,128)(2,1)S(1)}, bf16[40,1024]{1,0:T(8,128)(2,1)S(1)}, u32[]{:S(2)}, u32[]{:S(2)}) collective-permute-start(bf16[40,1024]{1,0:T(8,128)(2,1)S(1)} %pad_maximum_fusion.3), channel_id=1, source_target_pairs={{0,12},{1,13},{2,14},{3,15},{4,8},{5,9},{6,10},{7,11},{8,4},{9,5},... | collective-permute-start | bytes 245768 | tf_op jit(solution)/shard_map/ppermute | solution.py:350
  56.2 3.6 %collective-permute-start.14 = (bf16[40,1024]{1,0:T(8,128)(2,1)S(1)}, bf16[40,1024]{1,0:T(8,128)(2,1)S(1)}, u32[]{:S(2)}, u32[]{:S(2)}) collective-permute-start(bf16[40,1024]{1,0:T(8,128)(2,1)S(1)} %pad_maximum_fusion.2), channel_id=1, source_target_pairs={{0,8},{1,9},{2,10},{3,11},{4,12},{5,13},{6,14},{7,15},{8,0},{9,1},... | collective-permute-start | bytes 245768 | tf_op jit(solution)/shard_map/ppermute | solution.py:350
  59.8 0.1 collective-permute-start.13
  59.9 1.1 %collective-permute-done.15 = bf16[40,1024]{1,0:T(8,128)(2,1)S(1)} collective-permute-done((bf16[40,1024]{1,0:T(8,128)(2,1)S(1)}, bf16[40,1024]{1,0:T(8,128)(2,1)S(1)}, u32[]{:S(2)}, u32[]{:S(2)}) %collective-permute-start.15) | collective-permute-done | bytes 81952 | tf_op jit(solution)/shard_map/ppermute | solution.py:350
  61.0 2.1 %collective-permute-done.14 = bf16[40,1024]{1,0:T(8,128)(2,1)S(1)} collective-permute-done((bf16[40,1024]{1,0:T(8,128)(2,1)S(1)}, bf16[40,1024]{1,0:T(8,128)(2,1)S(1)}, u32[]{:S(2)}, u32[]{:S(2)}) %collective-permute-start.14) | collective-permute-done | bytes 81952 | tf_op jit(solution)/shard_map/ppermute | solution.py:350
  63.2 1.2 %collective-permute-done.13 = bf16[40,1024]{1,0:T(8,128)(2,1)S(1)} collective-permute-done((bf16[40,1024]{1,0:T(8,128)(2,1)S(1)}, bf16[40,1024]{1,0:T(8,128)(2,1)S(1)}, u32[]{:S(2)}, u32[]{:S(2)}) %collective-permute-start.13) | collective-permute-done | bytes 81952 | tf_op jit(solution)/shard_map/ppermute | solution.py:350
  64.3 0.1 fusion.46
  64.4 0.7 %fusion.36 = bf16[20,2048]{1,0:T(8,128)(2,1)} fusion(f32[20,2048]{1,0:T(8,128)S(1)} %slice_add_fusion, f32[20,1024]{1,0:T(8,128)S(1)} %get-tuple-element.43, f32[20,1024]{1,0:T(8,128)S(1)} %get-tuple-element.42), kind=kLoop, calls=%fused_computation.59 | loop fusion | flops 122880 | bytes 409600 | tf_op jit(solution)/shard_map/convert_element_type | solution.py:440
  (45 shorter events, 0.5 us)
Async XLA Ops:
  0.6 21.1 %collective-permute-start.1 = (bf16[2048,128]{1,0:T(8,128)(2,1)}, bf16[2048,128]{1,0:T(8,128)(2,1)S(1)}, u32[]{:S(2)}, u32[]{:S(2)}) collective-permute-start(bf16[2048,128]{1,0:T(8,128)(2,1)} %param.29), channel_id=1, source_target_pairs={{0,2},{1,3},{2,0},{3,1},{4,6},{5,7},{6,4},{7,5},{8,10},{9,11},{10,... | collective-permute-start | bytes 1572872 | tf_op jit(solution)/shard_map/ppermute | solution.py:350
  3.6 18.8 %collective-permute-start.4 = (bf16[2048,128]{1,0:T(8,128)(2,1)}, bf16[2048,128]{1,0:T(8,128)(2,1)S(1)}, u32[]{:S(2)}, u32[]{:S(2)}) collective-permute-start(bf16[2048,128]{1,0:T(8,128)(2,1)} %param.29), channel_id=1, source_target_pairs={{0,1},{1,0},{2,3},{3,2},{4,5},{5,4},{6,7},{7,6},{8,9},{9,8},{10,11... | collective-permute-start | bytes 1572872 | tf_op jit(solution)/shard_map/ppermute | solution.py:350
  7.7 11.2 %collective-permute-start.3 = (bf16[40,1408]{1,0:T(8,128)(2,1)}, bf16[40,1408]{1,0:T(8,128)(2,1)S(1)}, u32[]{:S(2)}, u32[]{:S(2)}) collective-permute-start(bf16[40,1408]{1,0:T(8,128)(2,1)} %get-tuple-element.17), channel_id=1, source_target_pairs={{0,12},{1,13},{2,14},{3,15},{4,8},{5,9},{6,10},{7,11},{8,4},{9,5},... | collective-permute-start | bytes 337928 | tf_op jit(solution)/shard_map/ppermute | solution.py:350
  11.3 10.4 %collective-permute-start.2 = (bf16[40,1408]{1,0:T(8,128)(2,1)}, bf16[40,1408]{1,0:T(8,128)(2,1)S(1)}, u32[]{:S(2)}, u32[]{:S(2)}) collective-permute-start(bf16[40,1408]{1,0:T(8,128)(2,1)} %get-tuple-element.16), channel_id=1, source_target_pairs={{0,8},{1,9},{2,10},{3,11},{4,12},{5,13},{6,14},{7,15},{8,0},{9,1},... | collective-permute-start | bytes 337928 | tf_op jit(solution)/shard_map/ppermute | solution.py:350
  11.3 10.4 %collective-permute-start = (bf16[40,1408]{1,0:T(8,128)(2,1)}, bf16[40,1408]{1,0:T(8,128)(2,1)S(1)}, u32[]{:S(2)}, u32[]{:S(2)}) collective-permute-start(bf16[40,1408]{1,0:T(8,128)(2,1)} %get-tuple-element.14), channel_id=1, source_target_pairs={{0,4},{1,5},{2,6},{3,7},{4,0},{5,1},{6,2},{7,3},{8,12},{9,13},{10,... | collective-permute-start | bytes 337928 | tf_op jit(solution)/shard_map/ppermute | solution.py:350
  14.6 7.4 %copy-start.4 = (bf16[2048,128]{1,0:T(8,128)(2,1)S(1)}, bf16[2048,128]{1,0:T(8,128)(2,1)}, u32[]{:S(2)}) copy-start(bf16[2048,128]{1,0:T(8,128)(2,1)} %param.29) | copy-start | bytes 1572868
  21.8 2.0 %collective-permute-start.5 = (bf16[2048,128]{1,0:T(8,128)(2,1)S(1)}, bf16[2048,128]{1,0:T(8,128)(2,1)S(1)}, u32[]{:S(2)}, u32[]{:S(2)}) collective-permute-start(bf16[2048,128]{1,0:T(8,128)(2,1)S(1)} %collective-permute-done.1), channel_id=1, source_target_pairs={{0,1},{1,0},{2,3},{3,2},{4,5},{5,4},{6,7},{7,6},{8,9},{9,8},{10,11... | collective-permute-start | bytes 1572872 | tf_op jit(solution)/shard_map/ppermute | solution.py:350
  22.7 6.0 %copy-start.3 = (bf16[2,2048,512]{2,1,0:T(8,128)(2,1)S(1)}, bf16[2,2048,512]{2,1,0:T(8,128)(2,1)}, u32[]{:S(2)}) copy-start(bf16[2,2048,512]{2,1,0:T(8,128)(2,1)} %param.34) | copy-start | bytes 12582916
  23.0 5.7 %copy-start = (bf16[2,256,2048]{2,1,0:T(8,128)(2,1)S(1)}, bf16[2,256,2048]{2,1,0:T(8,128)(2,1)}, u32[]{:S(2)}) copy-start(bf16[2,256,2048]{2,1,0:T(8,128)(2,1)} %param.35) | copy-start | bytes 6291460
  24.1 5.7 %collective-permute-start.6 = (bf16[80,512]{1,0:T(8,128)(2,1)S(1)}, bf16[80,512]{1,0:T(8,128)(2,1)S(1)}, u32[]{:S(2)}, u32[]{:S(2)}) collective-permute-start(bf16[80,512]{1,0:T(8,128)(2,1)S(1)} %fusion.40), channel_id=1, source_target_pairs={{0,4},{1,5},{2,6},{3,7},{4,0},{5,1},{6,2},{7,3},{8,12},{9,13},{10,... | collective-permute-start | bytes 245768 | tf_op jit(solution)/shard_map/ppermute | solution.py:350
  24.4 9.9 %copy-start.1 = (bf16[20,2048]{1,0:T(8,128)(2,1)S(1)}, bf16[20,2048]{1,0:T(8,128)(2,1)}, u32[]{:S(2)}) copy-start(bf16[20,2048]{1,0:T(8,128)(2,1)} %refs_0_.1) | copy-start | bytes 245764
  24.5 9.6 %collective-permute-start.7 = (bf16[80,512]{1,0:T(8,128)(2,1)S(1)}, bf16[80,512]{1,0:T(8,128)(2,1)S(1)}, u32[]{:S(2)}, u32[]{:S(2)}) collective-permute-start(bf16[80,512]{1,0:T(8,128)(2,1)S(1)} %get-tuple-element.41), channel_id=1, source_target_pairs={{0,8},{1,9},{2,10},{3,11},{4,12},{5,13},{6,14},{7,15},{8,0},{9,1},... | collective-permute-start | bytes 245768 | tf_op jit(solution)/shard_map/ppermute | solution.py:350
  27.4 6.7 %collective-permute-start.8 = (bf16[80,512]{1,0:T(8,128)(2,1)S(1)}, bf16[80,512]{1,0:T(8,128)(2,1)S(1)}, u32[]{:S(2)}, u32[]{:S(2)}) collective-permute-start(bf16[80,512]{1,0:T(8,128)(2,1)S(1)} %get-tuple-element.40), channel_id=1, source_target_pairs={{0,12},{1,13},{2,14},{3,15},{4,8},{5,9},{6,10},{7,11},{8,4},{9,5},... | collective-permute-start | bytes 245768 | tf_op jit(solution)/shard_map/ppermute | solution.py:350
  28.8 16.9 %collective-permute-start.10 = (bf16[2,256,2048]{2,1,0:T(8,128)(2,1)S(1)}, bf16[2,256,2048]{2,1,0:T(8,128)(2,1)S(1)}, u32[]{:S(2)}, u32[]{:S(2)}) collective-permute-start(bf16[2,256,2048]{2,1,0:T(8,128)(2,1)S(1)} %copy-done), channel_id=1, source_target_pairs={{0,1},{1,0},{2,3},{3,2},{4,5},{5,4},{6,7},{7,6},{8,9},{9,8},{10,11... | collective-permute-start | bytes 6291464 | tf_op jit(solution)/shard_map/ppermute | solution.py:350
  28.8 16.0 %collective-permute-start.9 = (bf16[2,2048,512]{2,1,0:T(8,128)(2,1)S(1)}, bf16[2,2048,512]{2,1,0:T(8,128)(2,1)S(1)}, u32[]{:S(2)}, u32[]{:S(2)}) collective-permute-start(bf16[2,2048,512]{2,1,0:T(8,128)(2,1)S(1)} %copy-done.3), channel_id=1, source_target_pairs={{0,1},{1,0},{2,3},{3,2},{4,5},{5,4},{6,7},{7,6},{8,9},{9,8},{10,11... | collective-permute-start | bytes 12582920 | tf_op jit(solution)/shard_map/ppermute | solution.py:350
  29.9 4.7 %copy-start.2 = (f32[2048]{0:T(1024)S(1)}, f32[2048]{0:T(1024)}, u32[]{:S(2)}) copy-start(f32[2048]{0:T(1024)} %param.31) | copy-start | bytes 24580
  34.7 8.1 %collective-permute-start.11 = (bf16[80,2176]{1,0:T(8,128)(2,1)S(1)}, bf16[80,2176]{1,0:T(8,128)(2,1)S(1)}, u32[]{:S(2)}, u32[]{:S(2)}) collective-permute-start(bf16[80,2176]{1,0:T(8,128)(2,1)S(1)} %maximum_maximum_fusion), channel_id=1, source_target_pairs={{0,2},{1,3},{2,0},{3,1},{4,6},{5,7},{6,4},{7,5},{8,10},{9,11},{10,... | collective-permute-start | bytes 1044488 | tf_op jit(solution)/shard_map/ppermute | solution.py:350
  46.4 7.1 %collective-permute-start.12 = (bf16[80,2048]{1,0:T(8,128)(2,1)S(1)}, bf16[80,2048]{1,0:T(8,128)(2,1)S(1)}, u32[]{:S(2)}, u32[]{:S(2)}) collective-permute-start(bf16[80,2048]{1,0:T(8,128)(2,1)S(1)} %fusion.3), channel_id=1, source_target_pairs={{0,2},{1,3},{2,0},{3,1},{4,6},{5,7},{6,4},{7,5},{8,10},{9,11},{10,... | collective-permute-start | bytes 983048 | tf_op jit(solution)/shard_map/ppermute | solution.py:350
  54.0 7.1 %collective-permute-start.15 = (bf16[40,1024]{1,0:T(8,128)(2,1)S(1)}, bf16[40,1024]{1,0:T(8,128)(2,1)S(1)}, u32[]{:S(2)}, u32[]{:S(2)}) collective-permute-start(bf16[40,1024]{1,0:T(8,128)(2,1)S(1)} %pad_maximum_fusion.3), channel_id=1, source_target_pairs={{0,12},{1,13},{2,14},{3,15},{4,8},{5,9},{6,10},{7,11},{8,4},{9,5},... | collective-permute-start | bytes 245768 | tf_op jit(solution)/shard_map/ppermute | solution.py:350
  56.2 6.9 %collective-permute-start.14 = (bf16[40,1024]{1,0:T(8,128)(2,1)S(1)}, bf16[40,1024]{1,0:T(8,128)(2,1)S(1)}, u32[]{:S(2)}, u32[]{:S(2)}) collective-permute-start(bf16[40,1024]{1,0:T(8,128)(2,1)S(1)} %pad_maximum_fusion.2), channel_id=1, source_target_pairs={{0,8},{1,9},{2,10},{3,11},{4,12},{5,13},{6,14},{7,15},{8,0},{9,1},... | collective-permute-start | bytes 245768 | tf_op jit(solution)/shard_map/ppermute | solution.py:350
  59.8 4.5 %collective-permute-start.13 = (bf16[40,1024]{1,0:T(8,128)(2,1)S(1)}, bf16[40,1024]{1,0:T(8,128)(2,1)S(1)}, u32[]{:S(2)}, u32[]{:S(2)}) collective-permute-start(bf16[40,1024]{1,0:T(8,128)(2,1)S(1)} %pad_maximum_fusion.1), channel_id=1, source_target_pairs={{0,4},{1,5},{2,6},{3,7},{4,0},{5,1},{6,2},{7,3},{8,12},{9,13},{10,... | collective-permute-start | bytes 245768 | tf_op jit(solution)/shard_map/ppermute | solution.py:350

commit v4 on v3

--- a/solution.py
+++ b/solution.py
@@ -318,7 +318,7 @@
         scratch_shapes=scratch,
         compiler_params=pltpu.CompilerParams(vmem_limit_bytes=56 * 1024 * 1024),
         cost_estimate=pl.CostEstimate(
-            flops=8192 * cells, bytes_accessed=64 * cells, transcendentals=0
+            flops=512 * cells, bytes_accessed=4 * cells, transcendentals=0
         ),
     )(*args)
     kept = pl.pallas_call(
@@ -335,7 +335,7 @@
         scratch_shapes=[pltpu.VMEM((group, pad, width), F32)],
         compiler_params=pltpu.CompilerParams(vmem_limit_bytes=56 * 1024 * 1024),
         cost_estimate=pl.CostEstimate(
-            flops=8192 * cells, bytes_accessed=64 * cells, transcendentals=0
+            flops=512 * cells, bytes_accessed=4 * cells, transcendentals=0
         ),
     )(key_in, written, coef, prior_state)
     return (*mixed, kept)
@@ -422,12 +422,13 @@
     scale = lax.rsqrt(jnp.mean(hidden * hidden, axis=1, keepdims=True) + EPS)
     normed = (hidden * scale * post_gain).astype(BF16)
 
-    came = swap(jnp.concatenate([normed, routes], axis=1), 2)
+    came = swap(normed, 2)
+    far_routes = swap(routes, 2)
     ups = [expert_up[i] for i in range(exp_dev)] + [up_mate[i] for i in range(exp_dev)]
     downs = [expert_down[i] for i in range(exp_dev)] + [down_mate[i] for i in range(exp_dev)]
     numbers = [who * exp_dev + i for who in (me, me ^ 1) for i in range(exp_dev)]
     own_sum = run_experts(normed, routes, ups, downs, numbers)
-    far_sum = run_experts(came[:, :full], came[:, full:], ups, downs, numbers)
+    far_sum = run_experts(came, far_routes, ups, downs, numbers)
     total = own_sum + swap(far_sum.astype(BF16), 2).astype(F32)
     folded = []
     for m in range(line):

time: 65.4 us -> 64.4 us (0.985)
  starting transfers between devices: 19.6 us -> 18.9 us
    ppermute x16 -> x17, starting transfers between devices: 19.6 us -> 18.9 us  [swap(): return lax.ppermute(values, 'rows', [(i, i ^ mask) for i in range(count)])]
    ppermute x16 -> x17, waiting for transfers between devices: 23.6 us -> 23.4 us  [swap(): return lax.ppermute(values, 'rows', [(i, i ^ mask) for i in range(count)])]
  transfers between devices with their start and end apart: 16 -> 17, of which waited for: 9 -> 9; matrix products, arithmetic and copies ran while one was open for 16% -> 16% of each run, Pallas kernels for 13% -> 13%
where the time goes in v4:
time: 64.4 us; the launch traced here: 64.1 us
  waiting for transfers between devices  23.4 us (36%)
  starting transfers between devices  18.9 us (29%)
  Pallas kernels  8.29 us (13%)
  matrix products  7.64 us (12%)
  local copies, waits for them, and re-layouts  2.66 us (4%)
  other arithmetic  2.1 us (3%)
  between operations  1.05 us (2%)
    ppermute x17, waiting for transfers between devices, swap(): return lax.ppermute(values, 'rows', [(i, i ^ mask) for i in range(count)])  23.4 us
    ppermute x17, starting transfers between devices, swap(): return lax.ppermute(values, 'rows', [(i, i ^ mask) for i in range(count)])  18.9 us
    pallas_call x1, Pallas kernels, delta_rule(): pl.pallas_call(functools.partial(kept_kernel, drafts, group), grid=grid,...  4.26 us
    pallas_call x1, Pallas kernels, delta_rule(): pl.pallas_call(functools.partial(delta_kernel, drafts, group, line), grid...  4.03 us
    dot_general x8, matrix products, run_experts(): full = jnp.dot(tokens, up, preferred_element_type=F32)  3.84 us
    dot_general x8, matrix products, run_experts(): term = jnp.dot(act.astype(BF16), down, preferred_element_type=F32)  2.81 us
  transfers between devices with their start and end apart: 17, of which 9 were waited for; matrix products, arithmetic and copies ran while one was open for 16% of the time, Pallas kernels for 13%

profile of v4, /device:TPU:0, one launch (start us, length us, event | category | flops | bytes accessed | tf_op | source)
XLA Modules:
  0.0 64.1 jit_solution(493445510491815835)
XLA Ops:
  0.6 3.0 %collective-permute-start.1 = (bf16[2048,128]{1,0:T(8,128)(2,1)}, bf16[2048,128]{1,0:T(8,128)(2,1)S(1)}, u32[]{:S(2)}, u32[]{:S(2)}) collective-permute-start(bf16[2048,128]{1,0:T(8,128)(2,1)} %param.29), channel_id=1, source_target_pairs={{0,2},{1,3},{2,0},{3,1},{4,6},{5,7},{6,4},{7,5},{8,10},{9,11},{10,... | collective-permute-start | bytes 1572872 | tf_op jit(solution)/shard_map/ppermute | solution.py:350
  3.6 0.0 collective-permute-start.4
  3.6 4.0 %shard_map.185 = (bf16[40,1408]{1,0:T(8,128)(2,1)}, bf16[40,1408]{1,0:T(8,128)(2,1)}, bf16[40,1408]{1,0:T(8,128)(2,1)}, bf16[40,1408]{1,0:T(8,128)(2,1)}, f32[24,2048]{1,0:T(8,128)}, /*index=5*/f32[128,128]{1,0:T(8,128)}) custom-call(s32[5]{0:T(128)} %accepted_ref.1, bf16[20,1024]{1,0:T(8,128)(2,1)} %query_ref.1, bf16[20,1024]{1,0:T(8,128)(2,1)} %key_ref.3, ...), custom_call_target="tpu_custom_call" | custom-call | flops 671088640 | bytes 5242880 | tf_op jit(solution)/shard_map/pallas_call | solution.py:312
  7.7 3.7 %collective-permute-start.3 = (bf16[40,1408]{1,0:T(8,128)(2,1)}, bf16[40,1408]{1,0:T(8,128)(2,1)S(1)}, u32[]{:S(2)}, u32[]{:S(2)}) collective-permute-start(bf16[40,1408]{1,0:T(8,128)(2,1)} %get-tuple-element.17), channel_id=1, source_target_pairs={{0,12},{1,13},{2,14},{3,15},{4,8},{5,9},{6,10},{7,11},{8,4},{9,5},... | collective-permute-start | bytes 337928 | tf_op jit(solution)/shard_map/ppermute | solution.py:350
  11.3 0.8 %collective-permute-start = (bf16[40,1408]{1,0:T(8,128)(2,1)}, bf16[40,1408]{1,0:T(8,128)(2,1)S(1)}, u32[]{:S(2)}, u32[]{:S(2)}) collective-permute-start(bf16[40,1408]{1,0:T(8,128)(2,1)} %get-tuple-element.14), channel_id=1, source_target_pairs={{0,4},{1,5},{2,6},{3,7},{4,0},{5,1},{6,2},{7,3},{8,12},{9,13},{10,... | collective-permute-start | bytes 337928 | tf_op jit(solution)/shard_map/ppermute | solution.py:350
  12.2 0.9 %fusion.99 = (bf16[20,1024]{1,0:T(8,128)(2,1)S(1)}, bf16[20,1024]{1,0:T(8,128)(2,1)S(1)}) fusion(bf16[40,1408]{1,0:T(8,128)(2,1)} %get-tuple-element.13), kind=kLoop, calls=%fused_computation.147 | loop fusion | bytes 163840 | tf_op jit(solution)/shard_map/slice | solution.py:395
  13.0 0.7 %fusion.95 = (bf16[20,128]{1,0:T(8,128)(2,1)S(1)}, bf16[20,128]{1,0:T(8,128)(2,1)S(1)}) fusion(bf16[40,1408]{1,0:T(8,128)(2,1)} %get-tuple-element.13), kind=kLoop, calls=%fused_computation.143 | loop fusion | bytes 20480 | tf_op jit(solution)/shard_map/slice | solution.py:401
  13.8 0.7 %slice.233 = bf16[20,384]{1,0:T(8,128)(2,1)S(1)} slice(bf16[40,1408]{1,0:T(8,128)(2,1)} %get-tuple-element.13), slice={[0:20], [1024:1408]} | slice | bytes 30720 | tf_op jit(solution)/shard_map/slice | solution.py:398
  14.6 0.0 copy-start.4
  14.6 4.3 %shard_map.186 = bf16[5,16,128,128]{3,2,1,0:T(8,128)(2,1)} custom-call(bf16[20,1024]{1,0:T(8,128)(2,1)} %key_ref.3, f32[24,2048]{1,0:T(8,128)} %get-tuple-element.22.written_ref, f32[128,128]{1,0:T(8,128)} %get-tuple-element.23.coef_ref, bf16[5,16,128,128]{3,2,1,0:T(8,128)(2,1)} %state_ref.3), custom_call_target="tpu_custom_call" | custom-call | flops 671088640 | bytes 5242880 | tf_op jit(solution)/shard_map/pallas_call | solution.py:324
  18.9 2.8 %collective-permute-done.2 = bf16[40,1408]{1,0:T(8,128)(2,1)S(1)} collective-permute-done((bf16[40,1408]{1,0:T(8,128)(2,1)}, bf16[40,1408]{1,0:T(8,128)(2,1)S(1)}, u32[]{:S(2)}, u32[]{:S(2)}) %collective-permute-start.2) | collective-permute-done | bytes 112672 | tf_op jit(solution)/shard_map/ppermute | solution.py:350
  21.8 0.1 collective-permute-start.5
  21.9 0.6 collective-permute-start.12
  22.5 0.3 convolution_dynamic-update-slice_fusion.3
  22.8 0.2 convolution_dynamic-update-slice_fusion.2
  23.1 0.0 copy-start.3
  23.1 0.3 convolution_dynamic-update-slice_fusion.1
  23.3 0.0 copy-start
  23.3 0.3 add_reduce_fusion.5
  23.6 2.1 %collective-permute-done.12 = bf16[80,128]{1,0:T(8,128)(2,1)S(1)} collective-permute-done((bf16[80,128]{1,0:T(8,128)(2,1)S(1)}, bf16[80,128]{1,0:T(8,128)(2,1)S(1)}, u32[]{:S(2)}, u32[]{:S(2)}) %collective-permute-start.12) | collective-permute-done | bytes 20512 | tf_op jit(solution)/shard_map/ppermute | solution.py:350
  25.7 0.2 add_reduce_fusion.1
  26.0 0.3 convolution_dynamic-update-slice_fusion
  26.3 0.1 fusion.36
  26.3 0.2 collective-permute-start.6
  26.5 0.1 fusion.40
  26.6 3.0 %collective-permute-start.7 = (bf16[80,512]{1,0:T(8,128)(2,1)S(1)}, bf16[80,512]{1,0:T(8,128)(2,1)S(1)}, u32[]{:S(2)}, u32[]{:S(2)}) collective-permute-start(bf16[80,512]{1,0:T(8,128)(2,1)S(1)} %get-tuple-element.41), channel_id=1, source_target_pairs={{0,8},{1,9},{2,10},{3,11},{4,12},{5,13},{6,14},{7,15},{8,0},{9,1},... | collective-permute-start | bytes 245768 | tf_op jit(solution)/shard_map/ppermute | solution.py:350
  29.7 1.3 %collective-permute-start.8 = (bf16[80,512]{1,0:T(8,128)(2,1)S(1)}, bf16[80,512]{1,0:T(8,128)(2,1)S(1)}, u32[]{:S(2)}, u32[]{:S(2)}) collective-permute-start(bf16[80,512]{1,0:T(8,128)(2,1)S(1)} %get-tuple-element.40), channel_id=1, source_target_pairs={{0,12},{1,13},{2,14},{3,15},{4,8},{5,9},{6,10},{7,11},{8,4},{9,5},... | collective-permute-start | bytes 245768 | tf_op jit(solution)/shard_map/ppermute | solution.py:350
  31.0 0.5 collective-permute-start.9
  31.5 0.1 fusion.43
  31.7 0.0 copy-start.2
  31.7 3.4 %collective-permute-done.7 = bf16[80,512]{1,0:T(8,128)(2,1)S(1)} collective-permute-done((bf16[80,512]{1,0:T(8,128)(2,1)S(1)}, bf16[80,512]{1,0:T(8,128)(2,1)S(1)}, u32[]{:S(2)}, u32[]{:S(2)}) %collective-permute-start.7) | collective-permute-done | bytes 81952 | tf_op jit(solution)/shard_map/ppermute | solution.py:350
  35.1 0.9 %collective-permute-done.8 = bf16[80,512]{1,0:T(8,128)(2,1)S(1)} collective-permute-done((bf16[80,512]{1,0:T(8,128)(2,1)S(1)}, bf16[80,512]{1,0:T(8,128)(2,1)S(1)}, u32[]{:S(2)}, u32[]{:S(2)}) %collective-permute-start.8) | collective-permute-done | bytes 81952 | tf_op jit(solution)/shard_map/ppermute | solution.py:350
  36.1 0.1 slice.310
  36.2 0.2 multiply_reduce_fusion
  36.4 0.1 multiply_convert_fusion
  36.6 0.6 collective-permute-start.11
  37.2 0.5 fusion.10
  37.6 0.5 fusion.6
  38.1 0.4 fusion.24
  38.5 0.4 convolution_add_fusion.3
  38.8 5.5 %collective-permute-done.11 = bf16[80,2048]{1,0:T(8,128)(2,1)S(1)} collective-permute-done((bf16[80,2048]{1,0:T(8,128)(2,1)S(1)}, bf16[80,2048]{1,0:T(8,128)(2,1)S(1)}, u32[]{:S(2)}, u32[]{:S(2)}) %collective-permute-start.11) | collective-permute-done | bytes 327712 | tf_op jit(solution)/shard_map/ppermute | solution.py:350
  44.3 0.5 fusion.8
  44.8 0.3 fusion.22
  45.2 0.5 fusion.4
  45.6 0.4 convolution_add_fusion.1
  46.0 0.5 fusion.14
  46.5 0.5 fusion.12
  47.0 0.3 fusion.26
  47.3 0.4 fusion.3
  47.7 0.6 collective-permute-start.13
  48.3 0.5 fusion.15
  48.8 0.3 fusion.27
  49.1 0.5 fusion.13
  49.6 5.2 %collective-permute-done.13 = bf16[80,2048]{1,0:T(8,128)(2,1)S(1)} collective-permute-done((bf16[80,2048]{1,0:T(8,128)(2,1)S(1)}, bf16[80,2048]{1,0:T(8,128)(2,1)S(1)}, u32[]{:S(2)}, u32[]{:S(2)}) %collective-permute-start.13) | collective-permute-done | bytes 327712 | tf_op jit(solution)/shard_map/ppermute | solution.py:350
  54.8 0.4 fusion.106
  55.2 0.1 fusion.93
  55.3 1.5 %collective-permute-start.16 = (bf16[40,1024]{1,0:T(8,128)(2,1)S(1)}, bf16[40,1024]{1,0:T(8,128)(2,1)S(1)}, u32[]{:S(2)}, u32[]{:S(2)}) collective-permute-start(bf16[40,1024]{1,0:T(8,128)(2,1)S(1)} %pad_maximum_fusion.3), channel_id=1, source_target_pairs={{0,12},{1,13},{2,14},{3,15},{4,8},{5,9},{6,10},{7,11},{8,4},{9,5},... | collective-permute-start | bytes 245768 | tf_op jit(solution)/shard_map/ppermute | solution.py:350
  56.8 1.2 %collective-permute-start.15 = (bf16[40,1024]{1,0:T(8,128)(2,1)S(1)}, bf16[40,1024]{1,0:T(8,128)(2,1)S(1)}, u32[]{:S(2)}, u32[]{:S(2)}) collective-permute-start(bf16[40,1024]{1,0:T(8,128)(2,1)S(1)} %pad_maximum_fusion.2), channel_id=1, source_target_pairs={{0,8},{1,9},{2,10},{3,11},{4,12},{5,13},{6,14},{7,15},{8,0},{9,1},... | collective-permute-start | bytes 245768 | tf_op jit(solution)/shard_map/ppermute | solution.py:350
  58.1 1.8 %collective-permute-start.14 = (bf16[40,1024]{1,0:T(8,128)(2,1)S(1)}, bf16[40,1024]{1,0:T(8,128)(2,1)S(1)}, u32[]{:S(2)}, u32[]{:S(2)}) collective-permute-start(bf16[40,1024]{1,0:T(8,128)(2,1)S(1)} %pad_maximum_fusion.1), channel_id=1, source_target_pairs={{0,4},{1,5},{2,6},{3,7},{4,0},{5,1},{6,2},{7,3},{8,12},{9,13},{10,... | collective-permute-start | bytes 245768 | tf_op jit(solution)/shard_map/ppermute | solution.py:350
  59.9 1.7 %collective-permute-done.16 = bf16[40,1024]{1,0:T(8,128)(2,1)S(1)} collective-permute-done((bf16[40,1024]{1,0:T(8,128)(2,1)S(1)}, bf16[40,1024]{1,0:T(8,128)(2,1)S(1)}, u32[]{:S(2)}, u32[]{:S(2)}) %collective-permute-start.16) | collective-permute-done | bytes 81952 | tf_op jit(solution)/shard_map/ppermute | solution.py:350
  61.6 0.9 %collective-permute-done.15 = bf16[40,1024]{1,0:T(8,128)(2,1)S(1)} collective-permute-done((bf16[40,1024]{1,0:T(8,128)(2,1)S(1)}, bf16[40,1024]{1,0:T(8,128)(2,1)S(1)}, u32[]{:S(2)}, u32[]{:S(2)}) %collective-permute-start.15) | collective-permute-done | bytes 81952 | tf_op jit(solution)/shard_map/ppermute | solution.py:350
  62.5 0.8 %collective-permute-done.14 = bf16[40,1024]{1,0:T(8,128)(2,1)S(1)} collective-permute-done((bf16[40,1024]{1,0:T(8,128)(2,1)S(1)}, bf16[40,1024]{1,0:T(8,128)(2,1)S(1)}, u32[]{:S(2)}, u32[]{:S(2)}) %collective-permute-start.14) | collective-permute-done | bytes 81952 | tf_op jit(solution)/shard_map/ppermute | solution.py:350
  63.3 0.1 fusion.42
  63.4 0.7 %fusion.32 = bf16[20,2048]{1,0:T(8,128)(2,1)} fusion(f32[20,2048]{1,0:T(8,128)S(1)} %slice_add_fusion, f32[20,1024]{1,0:T(8,128)S(1)} %get-tuple-element.43, f32[20,1024]{1,0:T(8,128)S(1)} %get-tuple-element.42), kind=kLoop, calls=%fused_computation.54 | loop fusion | flops 122880 | bytes 409600 | tf_op jit(solution)/shard_map/convert_element_type | solution.py:441
  (45 shorter events, 0.5 us)
Async XLA Ops:
  0.6 21.1 %collective-permute-start.1 = (bf16[2048,128]{1,0:T(8,128)(2,1)}, bf16[2048,128]{1,0:T(8,128)(2,1)S(1)}, u32[]{:S(2)}, u32[]{:S(2)}) collective-permute-start(bf16[2048,128]{1,0:T(8,128)(2,1)} %param.29), channel_id=1, source_target_pairs={{0,2},{1,3},{2,0},{3,1},{4,6},{5,7},{6,4},{7,5},{8,10},{9,11},{10,... | collective-permute-start | bytes 1572872 | tf_op jit(solution)/shard_map/ppermute | solution.py:350
  3.6 19.2 %collective-permute-start.4 = (bf16[2048,128]{1,0:T(8,128)(2,1)}, bf16[2048,128]{1,0:T(8,128)(2,1)S(1)}, u32[]{:S(2)}, u32[]{:S(2)}) collective-permute-start(bf16[2048,128]{1,0:T(8,128)(2,1)} %param.29), channel_id=1, source_target_pairs={{0,1},{1,0},{2,3},{3,2},{4,5},{5,4},{6,7},{7,6},{8,9},{9,8},{10,11... | collective-permute-start | bytes 1572872 | tf_op jit(solution)/shard_map/ppermute | solution.py:350
  7.7 11.2 %collective-permute-start.3 = (bf16[40,1408]{1,0:T(8,128)(2,1)}, bf16[40,1408]{1,0:T(8,128)(2,1)S(1)}, u32[]{:S(2)}, u32[]{:S(2)}) collective-permute-start(bf16[40,1408]{1,0:T(8,128)(2,1)} %get-tuple-element.17), channel_id=1, source_target_pairs={{0,12},{1,13},{2,14},{3,15},{4,8},{5,9},{6,10},{7,11},{8,4},{9,5},... | collective-permute-start | bytes 337928 | tf_op jit(solution)/shard_map/ppermute | solution.py:350
  11.3 10.4 %collective-permute-start.2 = (bf16[40,1408]{1,0:T(8,128)(2,1)}, bf16[40,1408]{1,0:T(8,128)(2,1)S(1)}, u32[]{:S(2)}, u32[]{:S(2)}) collective-permute-start(bf16[40,1408]{1,0:T(8,128)(2,1)} %get-tuple-element.16), channel_id=1, source_target_pairs={{0,8},{1,9},{2,10},{3,11},{4,12},{5,13},{6,14},{7,15},{8,0},{9,1},... | collective-permute-start | bytes 337928 | tf_op jit(solution)/shard_map/ppermute | solution.py:350
  11.3 10.4 %collective-permute-start = (bf16[40,1408]{1,0:T(8,128)(2,1)}, bf16[40,1408]{1,0:T(8,128)(2,1)S(1)}, u32[]{:S(2)}, u32[]{:S(2)}) collective-permute-start(bf16[40,1408]{1,0:T(8,128)(2,1)} %get-tuple-element.14), channel_id=1, source_target_pairs={{0,4},{1,5},{2,6},{3,7},{4,0},{5,1},{6,2},{7,3},{8,12},{9,13},{10,... | collective-permute-start | bytes 337928 | tf_op jit(solution)/shard_map/ppermute | solution.py:350
  14.6 8.0 %copy-start.4 = (bf16[2048,128]{1,0:T(8,128)(2,1)S(1)}, bf16[2048,128]{1,0:T(8,128)(2,1)}, u32[]{:S(2)}) copy-start(bf16[2048,128]{1,0:T(8,128)(2,1)} %param.29) | copy-start | bytes 1572868
  21.8 4.2 %collective-permute-start.5 = (bf16[2048,128]{1,0:T(8,128)(2,1)S(1)}, bf16[2048,128]{1,0:T(8,128)(2,1)S(1)}, u32[]{:S(2)}, u32[]{:S(2)}) collective-permute-start(bf16[2048,128]{1,0:T(8,128)(2,1)S(1)} %collective-permute-done.1), channel_id=1, source_target_pairs={{0,1},{1,0},{2,3},{3,2},{4,5},{5,4},{6,7},{7,6},{8,9},{9,8},{10,11... | collective-permute-start | bytes 1572872 | tf_op jit(solution)/shard_map/ppermute | solution.py:350
  21.9 3.8 %collective-permute-start.12 = (bf16[80,128]{1,0:T(8,128)(2,1)S(1)}, bf16[80,128]{1,0:T(8,128)(2,1)S(1)}, u32[]{:S(2)}, u32[]{:S(2)}) collective-permute-start(bf16[80,128]{1,0:T(8,128)(2,1)S(1)} %pad_maximum_fusion.4), channel_id=1, source_target_pairs={{0,2},{1,3},{2,0},{3,1},{4,6},{5,7},{6,4},{7,5},{8,10},{9,11},{10,... | collective-permute-start | bytes 61448 | tf_op jit(solution)/shard_map/ppermute | solution.py:350
  23.1 7.9 %copy-start.3 = (bf16[2,2048,512]{2,1,0:T(8,128)(2,1)S(1)}, bf16[2,2048,512]{2,1,0:T(8,128)(2,1)}, u32[]{:S(2)}) copy-start(bf16[2,2048,512]{2,1,0:T(8,128)(2,1)} %param.34) | copy-start | bytes 12582916
  23.3 7.7 %copy-start = (bf16[2,256,2048]{2,1,0:T(8,128)(2,1)S(1)}, bf16[2,256,2048]{2,1,0:T(8,128)(2,1)}, u32[]{:S(2)}) copy-start(bf16[2,256,2048]{2,1,0:T(8,128)(2,1)} %param.35) | copy-start | bytes 6291460
  26.3 5.3 %collective-permute-start.6 = (bf16[80,512]{1,0:T(8,128)(2,1)S(1)}, bf16[80,512]{1,0:T(8,128)(2,1)S(1)}, u32[]{:S(2)}, u32[]{:S(2)}) collective-permute-start(bf16[80,512]{1,0:T(8,128)(2,1)S(1)} %fusion.36), channel_id=1, source_target_pairs={{0,4},{1,5},{2,6},{3,7},{4,0},{5,1},{6,2},{7,3},{8,12},{9,13},{10,... | collective-permute-start | bytes 245768 | tf_op jit(solution)/shard_map/ppermute | solution.py:350
  26.5 9.6 %copy-start.1 = (bf16[20,2048]{1,0:T(8,128)(2,1)S(1)}, bf16[20,2048]{1,0:T(8,128)(2,1)}, u32[]{:S(2)}) copy-start(bf16[20,2048]{1,0:T(8,128)(2,1)} %refs_0_.1) | copy-start | bytes 245764
  26.6 8.4 %collective-permute-start.7 = (bf16[80,512]{1,0:T(8,128)(2,1)S(1)}, bf16[80,512]{1,0:T(8,128)(2,1)S(1)}, u32[]{:S(2)}, u32[]{:S(2)}) collective-permute-start(bf16[80,512]{1,0:T(8,128)(2,1)S(1)} %get-tuple-element.41), channel_id=1, source_target_pairs={{0,8},{1,9},{2,10},{3,11},{4,12},{5,13},{6,14},{7,15},{8,0},{9,1},... | collective-permute-start | bytes 245768 | tf_op jit(solution)/shard_map/ppermute | solution.py:350
  29.7 6.3 %collective-permute-start.8 = (bf16[80,512]{1,0:T(8,128)(2,1)S(1)}, bf16[80,512]{1,0:T(8,128)(2,1)S(1)}, u32[]{:S(2)}, u32[]{:S(2)}) collective-permute-start(bf16[80,512]{1,0:T(8,128)(2,1)S(1)} %get-tuple-element.40), channel_id=1, source_target_pairs={{0,12},{1,13},{2,14},{3,15},{4,8},{5,9},{6,10},{7,11},{8,4},{9,5},... | collective-permute-start | bytes 245768 | tf_op jit(solution)/shard_map/ppermute | solution.py:350
  31.0 16.0 %collective-permute-start.10 = (bf16[2,256,2048]{2,1,0:T(8,128)(2,1)S(1)}, bf16[2,256,2048]{2,1,0:T(8,128)(2,1)S(1)}, u32[]{:S(2)}, u32[]{:S(2)}) collective-permute-start(bf16[2,256,2048]{2,1,0:T(8,128)(2,1)S(1)} %copy-done), channel_id=1, source_target_pairs={{0,1},{1,0},{2,3},{3,2},{4,5},{5,4},{6,7},{7,6},{8,9},{9,8},{10,11... | collective-permute-start | bytes 6291464 | tf_op jit(solution)/shard_map/ppermute | solution.py:350
  31.0 15.0 %collective-permute-start.9 = (bf16[2,2048,512]{2,1,0:T(8,128)(2,1)S(1)}, bf16[2,2048,512]{2,1,0:T(8,128)(2,1)S(1)}, u32[]{:S(2)}, u32[]{:S(2)}) collective-permute-start(bf16[2,2048,512]{2,1,0:T(8,128)(2,1)S(1)} %copy-done.3), channel_id=1, source_target_pairs={{0,1},{1,0},{2,3},{3,2},{4,5},{5,4},{6,7},{7,6},{8,9},{9,8},{10,11... | collective-permute-start | bytes 12582920 | tf_op jit(solution)/shard_map/ppermute | solution.py:350
  31.7 4.7 %copy-start.2 = (f32[2048]{0:T(1024)S(1)}, f32[2048]{0:T(1024)}, u32[]{:S(2)}) copy-start(f32[2048]{0:T(1024)} %param.31) | copy-start | bytes 24580
  36.6 7.8 %collective-permute-start.11 = (bf16[80,2048]{1,0:T(8,128)(2,1)S(1)}, bf16[80,2048]{1,0:T(8,128)(2,1)S(1)}, u32[]{:S(2)}, u32[]{:S(2)}) collective-permute-start(bf16[80,2048]{1,0:T(8,128)(2,1)S(1)} %multiply_convert_fusion), channel_id=1, source_target_pairs={{0,2},{1,3},{2,0},{3,1},{4,6},{5,7},{6,4},{7,5},{8,10},{9,11},{10,... | collective-permute-start | bytes 983048 | tf_op jit(solution)/shard_map/ppermute | solution.py:350
  47.7 7.1 %collective-permute-start.13 = (bf16[80,2048]{1,0:T(8,128)(2,1)S(1)}, bf16[80,2048]{1,0:T(8,128)(2,1)S(1)}, u32[]{:S(2)}, u32[]{:S(2)}) collective-permute-start(bf16[80,2048]{1,0:T(8,128)(2,1)S(1)} %fusion.3), channel_id=1, source_target_pairs={{0,2},{1,3},{2,0},{3,1},{4,6},{5,7},{6,4},{7,5},{8,10},{9,11},{10,... | collective-permute-start | bytes 983048 | tf_op jit(solution)/shard_map/ppermute | solution.py:350
  55.3 6.3 %collective-permute-start.16 = (bf16[40,1024]{1,0:T(8,128)(2,1)S(1)}, bf16[40,1024]{1,0:T(8,128)(2,1)S(1)}, u32[]{:S(2)}, u32[]{:S(2)}) collective-permute-start(bf16[40,1024]{1,0:T(8,128)(2,1)S(1)} %pad_maximum_fusion.3), channel_id=1, source_target_pairs={{0,12},{1,13},{2,14},{3,15},{4,8},{5,9},{6,10},{7,11},{8,4},{9,5},... | collective-permute-start | bytes 245768 | tf_op jit(solution)/shard_map/ppermute | solution.py:350
  56.8 5.7 %collective-permute-start.15 = (bf16[40,1024]{1,0:T(8,128)(2,1)S(1)}, bf16[40,1024]{1,0:T(8,128)(2,1)S(1)}, u32[]{:S(2)}, u32[]{:S(2)}) collective-permute-start(bf16[40,1024]{1,0:T(8,128)(2,1)S(1)} %pad_maximum_fusion.2), channel_id=1, source_target_pairs={{0,8},{1,9},{2,10},{3,11},{4,12},{5,13},{6,14},{7,15},{8,0},{9,1},... | collective-permute-start | bytes 245768 | tf_op jit(solution)/shard_map/ppermute | solution.py:350
  58.1 5.3 %collective-permute-start.14 = (bf16[40,1024]{1,0:T(8,128)(2,1)S(1)}, bf16[40,1024]{1,0:T(8,128)(2,1)S(1)}, u32[]{:S(2)}, u32[]{:S(2)}) collective-permute-start(bf16[40,1024]{1,0:T(8,128)(2,1)S(1)} %pad_maximum_fusion.1), channel_id=1, source_target_pairs={{0,4},{1,5},{2,6},{3,7},{4,0},{5,1},{6,2},{7,3},{8,12},{9,13},{10,... | collective-permute-start | bytes 245768 | tf_op jit(solution)/shard_map/ppermute | solution.py:350

commit v5 on v4

--- a/solution.py
+++ b/solution.py
@@ -350,16 +350,24 @@
     return lax.ppermute(values, "rows", [(i, i ^ mask) for i in range(count)])
 
 
-def run_experts(tokens, routes, ups, downs, numbers):
+def run_experts(tokens, routes, pairs):
     total = None
     half = routes.shape[1] // 2
-    for up, down, number in zip(ups, downs, numbers):
-        inner = down.shape[0]
-        full = jnp.dot(tokens, up, preferred_element_type=F32)
-        here = lax.dynamic_slice(routes, (0, number), (routes.shape[0], 1)).astype(F32)
-        rest = lax.dynamic_slice(routes, (0, half + number), (routes.shape[0], 1)).astype(F32)
-        act = jax.nn.silu(full[:, :inner]) * full[:, inner:] * (here + rest)
-        term = jnp.dot(act.astype(BF16), down, preferred_element_type=F32)
+    for up, down, first in pairs:
+        inner = down.shape[1]
+        wide = jnp.broadcast_to(tokens, (up.shape[0], *tokens.shape))
+        full = jnp.einsum("lnd,ldf->lnf", wide, up, preferred_element_type=F32)
+        acts = []
+        for i in range(up.shape[0]):
+            here = lax.dynamic_slice(routes, (0, first + i), (routes.shape[0], 1)).astype(F32)
+            rest = lax.dynamic_slice(routes, (0, half + first + i), (routes.shape[0], 1))
+            act = jax.nn.silu(full[i][:, :inner]) * full[i][:, inner:]
+            acts.append((act * (here + rest.astype(F32))).astype(BF16))
+        term = jnp.dot(
+            jnp.concatenate(acts, axis=1),
+            down.reshape(-1, down.shape[2]),
+            preferred_element_type=F32,
+        )
         total = term if total is None else total + term
     return total
 
@@ -385,7 +393,7 @@
     weight_core = swap(out_weight, 1)
 
     got = [packed[0]] + [swap(packed[m], 4 * m) for m in others]
-    got[1], weight_x = lax.optimization_barrier((got[1], weight_x))
+    got[line // 2], weight_x = lax.optimization_barrier((got[line // 2], weight_x))
     weights = [out_weight, weight_core, weight_x, swap(weight_x, 1)]
     expert_up, expert_down, weights[3] = lax.optimization_barrier(
         (expert_up, expert_down, weights[3])
@@ -424,11 +432,9 @@
 
     came = swap(normed, 2)
     far_routes = swap(routes, 2)
-    ups = [expert_up[i] for i in range(exp_dev)] + [up_mate[i] for i in range(exp_dev)]
-    downs = [expert_down[i] for i in range(exp_dev)] + [down_mate[i] for i in range(exp_dev)]
-    numbers = [who * exp_dev + i for who in (me, me ^ 1) for i in range(exp_dev)]
-    own_sum = run_experts(normed, routes, ups, downs, numbers)
-    far_sum = run_experts(came, far_routes, ups, downs, numbers)
+    pairs = [(expert_up, expert_down, me * exp_dev), (up_mate, down_mate, (me ^ 1) * exp_dev)]
+    own_sum = run_experts(normed, routes, pairs)
+    far_sum = run_experts(came, far_routes, pairs)
     total = own_sum + swap(far_sum.astype(BF16), 2).astype(F32)
     folded = []
     for m in range(line):

time: 64.4 us -> 64.2 us (level)
  matrix products: 7.64 us -> 6.33 us
  other arithmetic: 2.1 us -> 2.77 us
    dot_general x16 -> x8, matrix products: 6.64 us -> 5.3 us  [the longest x4 3.29 us: run_experts(): full = jnp.einsum('lnd,ldf->lnf', wide, up, preferred_element_type=F32)]
    convert_element_type x0 -> x8, other arithmetic: none -> 0.65 us  [run_experts(): acts.append((act * (here + rest.astype(F32))).astype(BF16))]
  transfers between devices with their start and end apart: 17 -> 17, of which waited for: 9 -> 10; matrix products, arithmetic and copies ran while one was open for 16% -> 14% of each run, Pallas kernels for 13% -> 13%
where the time goes in v5:
time: 64.2 us; the launch traced here: 63.9 us
  waiting for transfers between devices  23.8 us (37%)
  starting transfers between devices  18.9 us (29%)
  Pallas kernels  8.29 us (13%)
  matrix products  6.33 us (10%)
  other arithmetic  2.77 us (4%)
  local copies, waits for them, and re-layouts  2.76 us (4%)
  between operations  1.06 us (2%)
    ppermute x17, waiting for transfers between devices, swap(): return lax.ppermute(values, 'rows', [(i, i ^ mask) for i in range(count)])  23.8 us
    ppermute x17, starting transfers between devices, swap(): return lax.ppermute(values, 'rows', [(i, i ^ mask) for i in range(count)])  18.9 us
    pallas_call x1, Pallas kernels, delta_rule(): pl.pallas_call(functools.partial(kept_kernel, drafts, group), grid=grid,...  4.27 us
    pallas_call x1, Pallas kernels, delta_rule(): pl.pallas_call(functools.partial(delta_kernel, drafts, group, line), grid...  4.03 us
    dot_general x4, matrix products, run_experts(): full = jnp.einsum('lnd,ldf->lnf', wide, up, preferred_element_type=F32)  3.29 us
    dot_general x4, matrix products, run_experts(): jnp.dot(jnp.concatenate(acts, axis=1), down.reshape(-1, down.shape[2]), p...  2.01 us
  transfers between devices with their start and end apart: 17, of which 10 were waited for; matrix products, arithmetic and copies ran while one was open for 14% of the time, Pallas kernels for 13%

profile of v5, /device:TPU:0, one launch (start us, length us, event | category | flops | bytes accessed | tf_op | source)
XLA Modules:
  0.0 63.9 jit_solution(1690459633426490803)
XLA Ops:
  0.6 3.0 %collective-permute-start.2 = (bf16[2048,128]{1,0:T(8,128)(2,1)}, bf16[2048,128]{1,0:T(8,128)(2,1)S(1)}, u32[]{:S(2)}, u32[]{:S(2)}) collective-permute-start(bf16[2048,128]{1,0:T(8,128)(2,1)} %param.29), channel_id=1, source_target_pairs={{0,2},{1,3},{2,0},{3,1},{4,6},{5,7},{6,4},{7,5},{8,10},{9,11},{10,... | collective-permute-start | bytes 1572872 | tf_op jit(solution)/shard_map/ppermute | solution.py:350
  3.6 0.0 collective-permute-start.4
  3.6 4.0 %shard_map.185 = (bf16[40,1408]{1,0:T(8,128)(2,1)}, bf16[40,1408]{1,0:T(8,128)(2,1)}, bf16[40,1408]{1,0:T(8,128)(2,1)}, bf16[40,1408]{1,0:T(8,128)(2,1)}, f32[24,2048]{1,0:T(8,128)}, /*index=5*/f32[128,128]{1,0:T(8,128)}) custom-call(s32[5]{0:T(128)} %accepted_ref.1, bf16[20,1024]{1,0:T(8,128)(2,1)} %query_ref.1, bf16[20,1024]{1,0:T(8,128)(2,1)} %key_ref.3, ...), custom_call_target="tpu_custom_call" | custom-call | flops 671088640 | bytes 5242880 | tf_op jit(solution)/shard_map/pallas_call | solution.py:312
  7.7 3.7 %collective-permute-start.3 = (bf16[40,1408]{1,0:T(8,128)(2,1)}, bf16[40,1408]{1,0:T(8,128)(2,1)S(1)}, u32[]{:S(2)}, u32[]{:S(2)}) collective-permute-start(bf16[40,1408]{1,0:T(8,128)(2,1)} %get-tuple-element.17), channel_id=1, source_target_pairs={{0,12},{1,13},{2,14},{3,15},{4,8},{5,9},{6,10},{7,11},{8,4},{9,5},... | collective-permute-start | bytes 337928 | tf_op jit(solution)/shard_map/ppermute | solution.py:350
  11.3 0.0 collective-permute-start.1
  11.3 0.8 %collective-permute-start = (bf16[40,1408]{1,0:T(8,128)(2,1)}, bf16[40,1408]{1,0:T(8,128)(2,1)S(1)}, u32[]{:S(2)}, u32[]{:S(2)}) collective-permute-start(bf16[40,1408]{1,0:T(8,128)(2,1)} %get-tuple-element.14), channel_id=1, source_target_pairs={{0,4},{1,5},{2,6},{3,7},{4,0},{5,1},{6,2},{7,3},{8,12},{9,13},{10,... | collective-permute-start | bytes 337928 | tf_op jit(solution)/shard_map/ppermute | solution.py:350
  12.2 0.9 %fusion.63 = (bf16[20,1024]{1,0:T(8,128)(2,1)S(1)}, bf16[20,1024]{1,0:T(8,128)(2,1)S(1)}) fusion(bf16[40,1408]{1,0:T(8,128)(2,1)} %get-tuple-element.13), kind=kLoop, calls=%fused_computation.121 | loop fusion | bytes 163840 | tf_op jit(solution)/shard_map/slice | solution.py:403
  13.0 0.7 %fusion.59 = (bf16[20,128]{1,0:T(8,128)(2,1)S(1)}, bf16[20,128]{1,0:T(8,128)(2,1)S(1)}) fusion(bf16[40,1408]{1,0:T(8,128)(2,1)} %get-tuple-element.13), kind=kLoop, calls=%fused_computation.117 | loop fusion | bytes 20480 | tf_op jit(solution)/shard_map/slice | solution.py:409
  13.8 0.7 %slice.241 = bf16[20,384]{1,0:T(8,128)(2,1)S(1)} slice(bf16[40,1408]{1,0:T(8,128)(2,1)} %get-tuple-element.13), slice={[0:20], [1024:1408]} | slice | bytes 30720 | tf_op jit(solution)/shard_map/slice | solution.py:406
  14.6 0.0 copy-start.4
  14.6 4.3 %shard_map.186 = bf16[5,16,128,128]{3,2,1,0:T(8,128)(2,1)} custom-call(bf16[20,1024]{1,0:T(8,128)(2,1)} %key_ref.3, f32[24,2048]{1,0:T(8,128)} %get-tuple-element.22.written_ref, f32[128,128]{1,0:T(8,128)} %get-tuple-element.23.coef_ref, bf16[5,16,128,128]{3,2,1,0:T(8,128)(2,1)} %state_ref.3), custom_call_target="tpu_custom_call" | custom-call | flops 671088640 | bytes 5242880 | tf_op jit(solution)/shard_map/pallas_call | solution.py:324
  18.9 0.7 %collective-permute-done = bf16[40,1408]{1,0:T(8,128)(2,1)S(1)} collective-permute-done((bf16[40,1408]{1,0:T(8,128)(2,1)}, bf16[40,1408]{1,0:T(8,128)(2,1)S(1)}, u32[]{:S(2)}, u32[]{:S(2)}) %collective-permute-start) | collective-permute-done | bytes 112672 | tf_op jit(solution)/shard_map/ppermute | solution.py:350
  19.6 2.1 %collective-permute-done.1 = bf16[40,1408]{1,0:T(8,128)(2,1)S(1)} collective-permute-done((bf16[40,1408]{1,0:T(8,128)(2,1)}, bf16[40,1408]{1,0:T(8,128)(2,1)S(1)}, u32[]{:S(2)}, u32[]{:S(2)}) %collective-permute-start.1) | collective-permute-done | bytes 112672 | tf_op jit(solution)/shard_map/ppermute | solution.py:350
  21.8 0.6 collective-permute-start.12
  22.4 0.3 convolution_dynamic-update-slice_fusion.3
  22.7 0.3 convolution_dynamic-update-slice_fusion.2
  22.9 0.0 copy-start
  22.9 0.3 convolution_dynamic-update-slice_fusion.1
  23.2 0.0 copy-start.1
  23.2 0.3 add_reduce_fusion.7
  23.5 2.1 %collective-permute-done.12 = bf16[80,128]{1,0:T(8,128)(2,1)S(1)} collective-permute-done((bf16[80,128]{1,0:T(8,128)(2,1)S(1)}, bf16[80,128]{1,0:T(8,128)(2,1)S(1)}, u32[]{:S(2)}, u32[]{:S(2)}) %collective-permute-start.12) | collective-permute-done | bytes 20512 | tf_op jit(solution)/shard_map/ppermute | solution.py:350
  25.6 0.2 add_reduce_fusion.3
  25.9 0.3 convolution_dynamic-update-slice_fusion
  26.1 0.0 copy-start.2
  26.1 0.1 fusion.14
  26.2 0.5 collective-permute-start.6
  26.7 0.1 fusion.18
  26.8 2.7 %collective-permute-start.7 = (bf16[80,512]{1,0:T(8,128)(2,1)S(1)}, bf16[80,512]{1,0:T(8,128)(2,1)S(1)}, u32[]{:S(2)}, u32[]{:S(2)}) collective-permute-start(bf16[80,512]{1,0:T(8,128)(2,1)S(1)} %get-tuple-element.49), channel_id=1, source_target_pairs={{0,8},{1,9},{2,10},{3,11},{4,12},{5,13},{6,14},{7,15},{8,0},{9,1},... | collective-permute-start | bytes 245768 | tf_op jit(solution)/shard_map/ppermute | solution.py:350
  29.5 1.3 %collective-permute-start.8 = (bf16[80,512]{1,0:T(8,128)(2,1)S(1)}, bf16[80,512]{1,0:T(8,128)(2,1)S(1)}, u32[]{:S(2)}, u32[]{:S(2)}) collective-permute-start(bf16[80,512]{1,0:T(8,128)(2,1)S(1)} %get-tuple-element.48), channel_id=1, source_target_pairs={{0,12},{1,13},{2,14},{3,15},{4,8},{5,9},{6,10},{7,11},{8,4},{9,5},... | collective-permute-start | bytes 245768 | tf_op jit(solution)/shard_map/ppermute | solution.py:350
  30.9 0.5 collective-permute-start.9
  31.4 0.1 fusion.21
  31.6 3.4 %collective-permute-done.7 = bf16[80,512]{1,0:T(8,128)(2,1)S(1)} collective-permute-done((bf16[80,512]{1,0:T(8,128)(2,1)S(1)}, bf16[80,512]{1,0:T(8,128)(2,1)S(1)}, u32[]{:S(2)}, u32[]{:S(2)}) %collective-permute-start.7) | collective-permute-done | bytes 81952 | tf_op jit(solution)/shard_map/ppermute | solution.py:350
  35.0 0.9 %collective-permute-done.8 = bf16[80,512]{1,0:T(8,128)(2,1)S(1)} collective-permute-done((bf16[80,512]{1,0:T(8,128)(2,1)S(1)}, bf16[80,512]{1,0:T(8,128)(2,1)S(1)}, u32[]{:S(2)}, u32[]{:S(2)}) %collective-permute-start.8) | collective-permute-done | bytes 81952 | tf_op jit(solution)/shard_map/ppermute | solution.py:350
  36.0 0.1 slice.318
  36.1 0.2 multiply_reduce_fusion
  36.3 0.2 multiply_convert_fusion
  36.5 0.6 collective-permute-start.11
  37.0 0.8 %fusion.8 = f32[2,80,512]{2,1,0:T(8,128)S(1)} fusion(bf16[2,2048,512]{2,1,0:T(8,128)(2,1)S(1)} %copy-done, bf16[80,2048]{1,0:T(8,128)(2,1)S(1)} %multiply_convert_fusion), kind=kOutput, calls=%fused_computation.18 | convolution fusion | flops 335544320 | bytes 4849664 | tf_op jit(solution)/shard_map/lnd,ldf->lnf/dot_general | solution.py:359
  37.9 0.1 fusion.35
  38.0 0.1 fusion.37
  38.1 6.2 %collective-permute-done.11 = bf16[80,2048]{1,0:T(8,128)(2,1)S(1)} collective-permute-done((bf16[80,2048]{1,0:T(8,128)(2,1)S(1)}, bf16[80,2048]{1,0:T(8,128)(2,1)S(1)}, u32[]{:S(2)}, u32[]{:S(2)}) %collective-permute-start.11) | collective-permute-done | bytes 327712 | tf_op jit(solution)/shard_map/ppermute | solution.py:350
  44.2 0.8 %fusion.4 = f32[2,80,512]{2,1,0:T(8,128)S(1)} fusion(bf16[2,2048,512]{2,1,0:T(8,128)(2,1)S(1)} %copy-done, bf16[80,2048]{1,0:T(8,128)(2,1)S(1)} %collective-permute-done.11), kind=kOutput, calls=%fused_computation.14 | convolution fusion | flops 335544320 | bytes 4849664 | tf_op jit(solution)/shard_map/lnd,ldf->lnf/dot_general | solution.py:359
  45.1 0.1 fusion.27
  45.2 0.1 fusion.29
  45.3 0.8 %fusion.2 = f32[2,80,512]{2,1,0:T(8,128)S(1)} fusion(bf16[2,2048,512]{2,1,0:T(8,128)(2,1)S(1)} %collective-permute-done.9, bf16[80,2048]{1,0:T(8,128)(2,1)S(1)} %collective-permute-done.11), kind=kOutput, calls=%fused_computation.12 | convolution fusion | flops 335544320 | bytes 4849664 | tf_op jit(solution)/shard_map/lnd,ldf->lnf/dot_general | solution.py:359
  46.1 0.1 fusion.23
  46.2 0.1 fusion.25
  46.3 0.5 fusion.48
  46.8 0.5 fusion.1
  47.3 0.6 collective-permute-start.13
  47.9 0.8 %fusion.6 = f32[2,80,512]{2,1,0:T(8,128)S(1)} fusion(bf16[2,2048,512]{2,1,0:T(8,128)(2,1)S(1)} %collective-permute-done.9, bf16[80,2048]{1,0:T(8,128)(2,1)S(1)} %multiply_convert_fusion), kind=kOutput, calls=%fused_computation.16 | convolution fusion | flops 335544320 | bytes 4849664 | tf_op jit(solution)/shard_map/lnd,ldf->lnf/dot_general | solution.py:359
  48.8 0.1 fusion.31
  48.8 0.1 fusion.33
  48.9 0.5 fusion.41
  49.4 5.0 %collective-permute-done.13 = bf16[80,2048]{1,0:T(8,128)(2,1)S(1)} collective-permute-done((bf16[80,2048]{1,0:T(8,128)(2,1)S(1)}, bf16[80,2048]{1,0:T(8,128)(2,1)S(1)}, u32[]{:S(2)}, u32[]{:S(2)}) %collective-permute-start.13) | collective-permute-done | bytes 327712 | tf_op jit(solution)/shard_map/ppermute | solution.py:350
  54.5 0.5 fusion.70
  55.0 0.1 fusion.57
  55.1 1.6 %collective-permute-start.16 = (bf16[40,1024]{1,0:T(8,128)(2,1)S(1)}, bf16[40,1024]{1,0:T(8,128)(2,1)S(1)}, u32[]{:S(2)}, u32[]{:S(2)}) collective-permute-start(bf16[40,1024]{1,0:T(8,128)(2,1)S(1)} %pad_maximum_fusion.3), channel_id=1, source_target_pairs={{0,12},{1,13},{2,14},{3,15},{4,8},{5,9},{6,10},{7,11},{8,4},{9,5},... | collective-permute-start | bytes 245768 | tf_op jit(solution)/shard_map/ppermute | solution.py:350
  56.6 1.2 %collective-permute-start.15 = (bf16[40,1024]{1,0:T(8,128)(2,1)S(1)}, bf16[40,1024]{1,0:T(8,128)(2,1)S(1)}, u32[]{:S(2)}, u32[]{:S(2)}) collective-permute-start(bf16[40,1024]{1,0:T(8,128)(2,1)S(1)} %pad_maximum_fusion.2), channel_id=1, source_target_pairs={{0,8},{1,9},{2,10},{3,11},{4,12},{5,13},{6,14},{7,15},{8,0},{9,1},... | collective-permute-start | bytes 245768 | tf_op jit(solution)/shard_map/ppermute | solution.py:350
  57.8 1.8 %collective-permute-start.14 = (bf16[40,1024]{1,0:T(8,128)(2,1)S(1)}, bf16[40,1024]{1,0:T(8,128)(2,1)S(1)}, u32[]{:S(2)}, u32[]{:S(2)}) collective-permute-start(bf16[40,1024]{1,0:T(8,128)(2,1)S(1)} %pad_maximum_fusion.1), channel_id=1, source_target_pairs={{0,4},{1,5},{2,6},{3,7},{4,0},{5,1},{6,2},{7,3},{8,12},{9,13},{10,... | collective-permute-start | bytes 245768 | tf_op jit(solution)/shard_map/ppermute | solution.py:350
  59.7 1.7 %collective-permute-done.16 = bf16[40,1024]{1,0:T(8,128)(2,1)S(1)} collective-permute-done((bf16[40,1024]{1,0:T(8,128)(2,1)S(1)}, bf16[40,1024]{1,0:T(8,128)(2,1)S(1)}, u32[]{:S(2)}, u32[]{:S(2)}) %collective-permute-start.16) | collective-permute-done | bytes 81952 | tf_op jit(solution)/shard_map/ppermute | solution.py:350
  61.4 0.9 %collective-permute-done.15 = bf16[40,1024]{1,0:T(8,128)(2,1)S(1)} collective-permute-done((bf16[40,1024]{1,0:T(8,128)(2,1)S(1)}, bf16[40,1024]{1,0:T(8,128)(2,1)S(1)}, u32[]{:S(2)}, u32[]{:S(2)}) %collective-permute-start.15) | collective-permute-done | bytes 81952 | tf_op jit(solution)/shard_map/ppermute | solution.py:350
  62.3 0.8 %collective-permute-done.14 = bf16[40,1024]{1,0:T(8,128)(2,1)S(1)} collective-permute-done((bf16[40,1024]{1,0:T(8,128)(2,1)S(1)}, bf16[40,1024]{1,0:T(8,128)(2,1)S(1)}, u32[]{:S(2)}, u32[]{:S(2)}) %collective-permute-start.14) | collective-permute-done | bytes 81952 | tf_op jit(solution)/shard_map/ppermute | solution.py:350
  63.2 0.7 %fusion.10 = bf16[20,2048]{1,0:T(8,128)(2,1)} fusion(f32[20,2048]{1,0:T(8,128)S(1)} %slice_add_fusion, f32[20,1024]{1,0:T(8,128)S(1)} %get-tuple-element.51, f32[20,1024]{1,0:T(8,128)S(1)} %get-tuple-element.50), kind=kLoop, calls=%fused_computation.26 | loop fusion | flops 122880 | bytes 409600 | tf_op jit(solution)/shard_map/convert_element_type | solution.py:447
  (49 shorter events, 0.6 us)
Async XLA Ops:
  0.6 21.1 %collective-permute-start.2 = (bf16[2048,128]{1,0:T(8,128)(2,1)}, bf16[2048,128]{1,0:T(8,128)(2,1)S(1)}, u32[]{:S(2)}, u32[]{:S(2)}) collective-permute-start(bf16[2048,128]{1,0:T(8,128)(2,1)} %param.29), channel_id=1, source_target_pairs={{0,2},{1,3},{2,0},{3,1},{4,6},{5,7},{6,4},{7,5},{8,10},{9,11},{10,... | collective-permute-start | bytes 1572872 | tf_op jit(solution)/shard_map/ppermute | solution.py:350
  3.6 19.0 %collective-permute-start.4 = (bf16[2048,128]{1,0:T(8,128)(2,1)}, bf16[2048,128]{1,0:T(8,128)(2,1)S(1)}, u32[]{:S(2)}, u32[]{:S(2)}) collective-permute-start(bf16[2048,128]{1,0:T(8,128)(2,1)} %param.29), channel_id=1, source_target_pairs={{0,1},{1,0},{2,3},{3,2},{4,5},{5,4},{6,7},{7,6},{8,9},{9,8},{10,11... | collective-permute-start | bytes 1572872 | tf_op jit(solution)/shard_map/ppermute | solution.py:350
  7.7 11.2 %collective-permute-start.3 = (bf16[40,1408]{1,0:T(8,128)(2,1)}, bf16[40,1408]{1,0:T(8,128)(2,1)S(1)}, u32[]{:S(2)}, u32[]{:S(2)}) collective-permute-start(bf16[40,1408]{1,0:T(8,128)(2,1)} %get-tuple-element.17), channel_id=1, source_target_pairs={{0,12},{1,13},{2,14},{3,15},{4,8},{5,9},{6,10},{7,11},{8,4},{9,5},... | collective-permute-start | bytes 337928 | tf_op jit(solution)/shard_map/ppermute | solution.py:350
  11.3 10.4 %collective-permute-start.1 = (bf16[40,1408]{1,0:T(8,128)(2,1)}, bf16[40,1408]{1,0:T(8,128)(2,1)S(1)}, u32[]{:S(2)}, u32[]{:S(2)}) collective-permute-start(bf16[40,1408]{1,0:T(8,128)(2,1)} %get-tuple-element.15), channel_id=1, source_target_pairs={{0,8},{1,9},{2,10},{3,11},{4,12},{5,13},{6,14},{7,15},{8,0},{9,1},... | collective-permute-start | bytes 337928 | tf_op jit(solution)/shard_map/ppermute | solution.py:350
  11.3 8.3 %collective-permute-start = (bf16[40,1408]{1,0:T(8,128)(2,1)}, bf16[40,1408]{1,0:T(8,128)(2,1)S(1)}, u32[]{:S(2)}, u32[]{:S(2)}) collective-permute-start(bf16[40,1408]{1,0:T(8,128)(2,1)} %get-tuple-element.14), channel_id=1, source_target_pairs={{0,4},{1,5},{2,6},{3,7},{4,0},{5,1},{6,2},{7,3},{8,12},{9,13},{10,... | collective-permute-start | bytes 337928 | tf_op jit(solution)/shard_map/ppermute | solution.py:350
  14.6 7.8 %copy-start.4 = (bf16[2048,128]{1,0:T(8,128)(2,1)S(1)}, bf16[2048,128]{1,0:T(8,128)(2,1)}, u32[]{:S(2)}) copy-start(bf16[2048,128]{1,0:T(8,128)(2,1)} %param.29) | copy-start | bytes 1572868
  21.7 4.1 %collective-permute-start.5 = (bf16[2048,128]{1,0:T(8,128)(2,1)S(1)}, bf16[2048,128]{1,0:T(8,128)(2,1)S(1)}, u32[]{:S(2)}, u32[]{:S(2)}) collective-permute-start(bf16[2048,128]{1,0:T(8,128)(2,1)S(1)} %collective-permute-done.2), channel_id=1, source_target_pairs={{0,1},{1,0},{2,3},{3,2},{4,5},{5,4},{6,7},{7,6},{8,9},{9,8},{10,11... | collective-permute-start | bytes 1572872 | tf_op jit(solution)/shard_map/ppermute | solution.py:350
  21.8 3.8 %collective-permute-start.12 = (bf16[80,128]{1,0:T(8,128)(2,1)S(1)}, bf16[80,128]{1,0:T(8,128)(2,1)S(1)}, u32[]{:S(2)}, u32[]{:S(2)}) collective-permute-start(bf16[80,128]{1,0:T(8,128)(2,1)S(1)} %pad_maximum_fusion.4), channel_id=1, source_target_pairs={{0,2},{1,3},{2,0},{3,1},{4,6},{5,7},{6,4},{7,5},{8,10},{9,11},{10,... | collective-permute-start | bytes 61448 | tf_op jit(solution)/shard_map/ppermute | solution.py:350
  22.9 7.9 %copy-start = (bf16[2,2048,512]{2,1,0:T(8,128)(2,1)S(1)}, bf16[2,2048,512]{2,1,0:T(8,128)(2,1)}, u32[]{:S(2)}) copy-start(bf16[2,2048,512]{2,1,0:T(8,128)(2,1)} %param.34) | copy-start | bytes 12582916
  23.2 7.7 %copy-start.1 = (bf16[2,256,2048]{2,1,0:T(8,128)(2,1)S(1)}, bf16[2,256,2048]{2,1,0:T(8,128)(2,1)}, u32[]{:S(2)}) copy-start(bf16[2,256,2048]{2,1,0:T(8,128)(2,1)} %param.35) | copy-start | bytes 6291460
  26.1 9.9 %copy-start.2 = (bf16[20,2048]{1,0:T(8,128)(2,1)S(1)}, bf16[20,2048]{1,0:T(8,128)(2,1)}, u32[]{:S(2)}) copy-start(bf16[20,2048]{1,0:T(8,128)(2,1)} %refs_0_.1) | copy-start | bytes 245764
  26.2 5.3 %collective-permute-start.6 = (bf16[80,512]{1,0:T(8,128)(2,1)S(1)}, bf16[80,512]{1,0:T(8,128)(2,1)S(1)}, u32[]{:S(2)}, u32[]{:S(2)}) collective-permute-start(bf16[80,512]{1,0:T(8,128)(2,1)S(1)} %fusion.14), channel_id=1, source_target_pairs={{0,4},{1,5},{2,6},{3,7},{4,0},{5,1},{6,2},{7,3},{8,12},{9,13},{10,... | collective-permute-start | bytes 245768 | tf_op jit(solution)/shard_map/ppermute | solution.py:350
  26.7 9.6 %copy-start.3 = (f32[2048]{0:T(1024)S(1)}, f32[2048]{0:T(1024)}, u32[]{:S(2)}) copy-start(f32[2048]{0:T(1024)} %param.31) | copy-start | bytes 24580
  26.8 8.2 %collective-permute-start.7 = (bf16[80,512]{1,0:T(8,128)(2,1)S(1)}, bf16[80,512]{1,0:T(8,128)(2,1)S(1)}, u32[]{:S(2)}, u32[]{:S(2)}) collective-permute-start(bf16[80,512]{1,0:T(8,128)(2,1)S(1)} %get-tuple-element.49), channel_id=1, source_target_pairs={{0,8},{1,9},{2,10},{3,11},{4,12},{5,13},{6,14},{7,15},{8,0},{9,1},... | collective-permute-start | bytes 245768 | tf_op jit(solution)/shard_map/ppermute | solution.py:350
  29.5 6.3 %collective-permute-start.8 = (bf16[80,512]{1,0:T(8,128)(2,1)S(1)}, bf16[80,512]{1,0:T(8,128)(2,1)S(1)}, u32[]{:S(2)}, u32[]{:S(2)}) collective-permute-start(bf16[80,512]{1,0:T(8,128)(2,1)S(1)} %get-tuple-element.48), channel_id=1, source_target_pairs={{0,12},{1,13},{2,14},{3,15},{4,8},{5,9},{6,10},{7,11},{8,4},{9,5},... | collective-permute-start | bytes 245768 | tf_op jit(solution)/shard_map/ppermute | solution.py:350
  30.9 15.4 %collective-permute-start.10 = (bf16[2,256,2048]{2,1,0:T(8,128)(2,1)S(1)}, bf16[2,256,2048]{2,1,0:T(8,128)(2,1)S(1)}, u32[]{:S(2)}, u32[]{:S(2)}) collective-permute-start(bf16[2,256,2048]{2,1,0:T(8,128)(2,1)S(1)} %copy-done.1), channel_id=1, source_target_pairs={{0,1},{1,0},{2,3},{3,2},{4,5},{5,4},{6,7},{7,6},{8,9},{9,8},{10,11... | collective-permute-start | bytes 6291464 | tf_op jit(solution)/shard_map/ppermute | solution.py:350
  30.9 14.4 %collective-permute-start.9 = (bf16[2,2048,512]{2,1,0:T(8,128)(2,1)S(1)}, bf16[2,2048,512]{2,1,0:T(8,128)(2,1)S(1)}, u32[]{:S(2)}, u32[]{:S(2)}) collective-permute-start(bf16[2,2048,512]{2,1,0:T(8,128)(2,1)S(1)} %copy-done), channel_id=1, source_target_pairs={{0,1},{1,0},{2,3},{3,2},{4,5},{5,4},{6,7},{7,6},{8,9},{9,8},{10,11... | collective-permute-start | bytes 12582920 | tf_op jit(solution)/shard_map/ppermute | solution.py:350
  36.5 7.8 %collective-permute-start.11 = (bf16[80,2048]{1,0:T(8,128)(2,1)S(1)}, bf16[80,2048]{1,0:T(8,128)(2,1)S(1)}, u32[]{:S(2)}, u32[]{:S(2)}) collective-permute-start(bf16[80,2048]{1,0:T(8,128)(2,1)S(1)} %multiply_convert_fusion), channel_id=1, source_target_pairs={{0,2},{1,3},{2,0},{3,1},{4,6},{5,7},{6,4},{7,5},{8,10},{9,11},{10,... | collective-permute-start | bytes 983048 | tf_op jit(solution)/shard_map/ppermute | solution.py:350
  47.3 7.1 %collective-permute-start.13 = (bf16[80,2048]{1,0:T(8,128)(2,1)S(1)}, bf16[80,2048]{1,0:T(8,128)(2,1)S(1)}, u32[]{:S(2)}, u32[]{:S(2)}) collective-permute-start(bf16[80,2048]{1,0:T(8,128)(2,1)S(1)} %fusion.1), channel_id=1, source_target_pairs={{0,2},{1,3},{2,0},{3,1},{4,6},{5,7},{6,4},{7,5},{8,10},{9,11},{10,... | collective-permute-start | bytes 983048 | tf_op jit(solution)/shard_map/ppermute | solution.py:350
  55.1 6.3 %collective-permute-start.16 = (bf16[40,1024]{1,0:T(8,128)(2,1)S(1)}, bf16[40,1024]{1,0:T(8,128)(2,1)S(1)}, u32[]{:S(2)}, u32[]{:S(2)}) collective-permute-start(bf16[40,1024]{1,0:T(8,128)(2,1)S(1)} %pad_maximum_fusion.3), channel_id=1, source_target_pairs={{0,12},{1,13},{2,14},{3,15},{4,8},{5,9},{6,10},{7,11},{8,4},{9,5},... | collective-permute-start | bytes 245768 | tf_op jit(solution)/shard_map/ppermute | solution.py:350
  56.6 5.7 %collective-permute-start.15 = (bf16[40,1024]{1,0:T(8,128)(2,1)S(1)}, bf16[40,1024]{1,0:T(8,128)(2,1)S(1)}, u32[]{:S(2)}, u32[]{:S(2)}) collective-permute-start(bf16[40,1024]{1,0:T(8,128)(2,1)S(1)} %pad_maximum_fusion.2), channel_id=1, source_target_pairs={{0,8},{1,9},{2,10},{3,11},{4,12},{5,13},{6,14},{7,15},{8,0},{9,1},... | collective-permute-start | bytes 245768 | tf_op jit(solution)/shard_map/ppermute | solution.py:350
  57.8 5.3 %collective-permute-start.14 = (bf16[40,1024]{1,0:T(8,128)(2,1)S(1)}, bf16[40,1024]{1,0:T(8,128)(2,1)S(1)}, u32[]{:S(2)}, u32[]{:S(2)}) collective-permute-start(bf16[40,1024]{1,0:T(8,128)(2,1)S(1)} %pad_maximum_fusion.1), channel_id=1, source_target_pairs={{0,4},{1,5},{2,6},{3,7},{4,0},{5,1},{6,2},{7,3},{8,12},{9,13},{10,... | collective-permute-start | bytes 245768 | tf_op jit(solution)/shard_map/ppermute | solution.py:350
